TPU v7x, 128 devices: a whole 4x4x4 slice. The times are simulated.
128 devices in a mesh: gx: 16 (over z, x), gy: 8 (over y, core).
Axes of the slice: x: 4, y: 4, z: 4, core: 2. Of those that a mesh axis runs over, the one named last changes fastest.
Arguments:
- part_feat: bfloat16 [64, 1048576], P(None, ('gx', 'gy')), may hold values from -6 to 6
- target: bfloat16 [64, 1048576], P(None, ('gx', 'gy')), may hold values from -6 to 6
- block_tile: int32 [8192, 1], P(('gx', 'gy')), may hold values from 0 to 127; in each aligned block of 64 rows (0 to 63, 64 to 127, ...) at most 2 rows name the same one
- block_patch: int32 [8192], P(('gx', 'gy')), may hold values from 0 to 31
- cell_idx: int32 [8192, 128], P(('gx', 'gy')), may hold values from 0 to 127
- block_fill: int32 [8192], P(('gx', 'gy')), may hold values from 64 to 128
- conv_in: bfloat16 [9, 64, 64], replicated, may hold values from -0.25 to 0.25
- conv_mid: bfloat16 [9, 64, 64], replicated, may hold values from -0.25 to 0.25
- conv_out: bfloat16 [9, 64, 64], replicated, may hold values from -0.25 to 0.25
- mlp_grid: bfloat16 [64, 128], replicated, may hold values from -0.5 to 0.5
- mlp_part: bfloat16 [64, 128], replicated, may hold values from -0.5 to 0.5
- mlp_out: bfloat16 [128, 64], replicated, may hold values from -0.5 to 0.5
Outputs:
- pred: bfloat16 [64, 1048576], P(None, ('gx', 'gy'))
- grad_conv_in: float32 [9, 64, 64], replicated
- grad_conv_mid: float32 [9, 64, 64], replicated
- grad_conv_out: float32 [9, 64, 64], replicated
- grad_mlp_grid: float32 [64, 128], replicated
- grad_mlp_part: float32 [64, 128], replicated
- grad_mlp_out: float32 [128, 64], replicated
Inputs may be any that keep to these rules, and one draw needn't show every extreme that they name: `block_tile`: among the 64 blocks of one device no tile is named by more than 2 blocks, a bound that some block reaches.
All inputs are finite; a program needn't handle non-finite values.
Results may differ from a plain program's by a relative error of at most 0.009.
Values may be sent and summed in bfloat16 or wider, within the bound.
No kernel may reach another device: no remote copies, remote signals or barrier semaphores. Data moves between devices by JAX's collectives and lax.ppermute only.
A program may use at most 128 MiB of HBM per device.

v0:
```python
import math

import jax
import jax.numpy as jnp
from jax import lax
from jax.sharding import PartitionSpec as P

PR = 8
PC = 16
CR = 16
CC = 256


root_two_pi = 0.7978845608028654
cubic_coef = 0.044715


def with_halo(cells, sides, width):
    for axis, dim in sides:
        count = lax.axis_size(axis)
        ends = count - 1
        head = lax.slice_in_dim(cells, 0, width, axis=dim)
        tail = lax.slice_in_dim(cells, cells.shape[dim] - width, cells.shape[dim], axis=dim)
        cells = jnp.concatenate(
            [
                lax.ppermute(tail, axis, [(i, (i + 1) % count) for i in range(ends)]),
                cells,
                lax.ppermute(head, axis, [((i + 1) % count, i) for i in range(ends)]),
            ],
            axis=dim,
        )
    return cells


def gelu_value(value):
    return (
        0.5 * value * (1.0 + jnp.tanh(root_two_pi * (value + cubic_coef * value * value * value)))
    )


def gelu_slope(value):
    inner = jnp.tanh(root_two_pi * (value + cubic_coef * value * value * value))
    return 0.5 * (1.0 + inner) + 0.5 * value * (1.0 - inner * inner) * root_two_pi * (
        1.0 + 3.0 * cubic_coef * value * value
    )


def product(form, left, right):
    return jnp.einsum(form, left, right, preferred_element_type=jnp.float32)


def conv_valid(padded, weight):
    kernel = weight.reshape(3, 3, weight.shape[1], weight.shape[2])
    result = lax.conv_general_dilated(
        padded[None],
        kernel,
        (1, 1),
        "VALID",
        dimension_numbers=("NCHW", "HWIO", "NCHW"),
        preferred_element_type=jnp.float32,
    )
    return result[0]


def weight_term(padded, cotangent):
    result = lax.conv_general_dilated(
        padded[None],
        cotangent[None],
        (1, 1),
        "VALID",
        dimension_numbers=("CNHW", "IOHW", "NCHW"),
        preferred_element_type=jnp.float32,
    )
    return jnp.transpose(result, (2, 3, 0, 1)).reshape(9, result.shape[0], result.shape[1])


def flipped(weight):
    return jnp.transpose(weight[::-1], (0, 2, 1))


def with_rim(field):
    return with_halo(field, (("gy", 1), ("gx", 2)), 1)


def pool_mean(field):
    return field.reshape(field.shape[0], field.shape[1] // 2, 2, field.shape[2] // 2, 2).mean(
        axis=(2, 4)
    )


def pool_total(field):
    return field.reshape(field.shape[0], field.shape[1] // 2, 2, field.shape[2] // 2, 2).sum(
        axis=(2, 4)
    )


def spread(field):
    return jnp.repeat(jnp.repeat(field, 2, axis=1), 2, axis=2)


def to_patches(field):
    channels = field.shape[0]
    shaped = field.reshape(channels, CR // PR, PR, CC // PC, PC)
    return jnp.transpose(shaped, (0, 2, 4, 1, 3)).reshape(channels, PR * PC, CR // PR * (CC // PC))


def from_patches(field):
    channels = field.shape[0]
    shaped = field.reshape(channels, PR, PC, CR // PR, CC // PC)
    return jnp.transpose(shaped, (0, 3, 1, 4, 2)).reshape(channels, CR, CC)


def deposit_cells(values, cell_hot, patch_hot):
    per_slot = jnp.einsum("ksj,sjc->ksc", values, cell_hot, preferred_element_type=jnp.float32)
    return jnp.einsum("ksc,sn->kcn", per_slot, patch_hot, precision=lax.Precision.HIGHEST)


def unet_forward(grid_input, conv_in, conv_mid, conv_out):
    input_pad = with_rim(grid_input)
    first_pre = conv_valid(input_pad, conv_in)
    fine_act = gelu_value(first_pre).astype(jnp.bfloat16)
    coarse = pool_mean(fine_act.astype(jnp.float32)).astype(jnp.bfloat16)
    coarse_pad = with_rim(coarse)
    mid_pre = conv_valid(coarse_pad, conv_mid)
    coarse_new = (coarse.astype(jnp.float32) + gelu_value(mid_pre)).astype(jnp.bfloat16)
    rebuilt = (
        fine_act.astype(jnp.float32)
        + spread(coarse_new.astype(jnp.float32) - coarse.astype(jnp.float32))
    ).astype(jnp.bfloat16)
    rebuilt_pad = with_rim(rebuilt)
    grid_output = conv_valid(rebuilt_pad, conv_out).astype(jnp.bfloat16)
    return (grid_output, (input_pad, first_pre, coarse_pad, mid_pre, rebuilt_pad))


def unet_backward(output_grad, saved, conv_mid, conv_out):
    input_pad, first_pre, coarse_pad, mid_pre, rebuilt_pad = saved
    grad_out = weight_term(rebuilt_pad, output_grad)
    rebuilt_grad = conv_valid(with_rim(output_grad), flipped(conv_out)).astype(jnp.bfloat16)
    mid_grad = (pool_total(rebuilt_grad.astype(jnp.float32)) * gelu_slope(mid_pre)).astype(
        jnp.bfloat16
    )
    grad_mid = weight_term(coarse_pad, mid_grad)
    coarse_grad = conv_valid(with_rim(mid_grad), flipped(conv_mid))
    first_grad = (
        (rebuilt_grad.astype(jnp.float32) + 0.25 * spread(coarse_grad)) * gelu_slope(first_pre)
    ).astype(jnp.bfloat16)
    grad_in = weight_term(input_pad, first_grad)
    return (grad_in, grad_mid, grad_out)


def particle_head(gathered, part_feat, target, living, mlp_grid, mlp_part, mlp_out, scale):
    hidden_pre = product("ch,cp->hp", mlp_grid, gathered) + product(
        "ch,cp->hp", mlp_part, part_feat
    )
    hidden = gelu_value(hidden_pre).astype(jnp.bfloat16)
    pred_full = product("hc,hp->cp", mlp_out, hidden)
    pred_grad = (living * (pred_full - target.astype(jnp.float32)) * scale).astype(jnp.bfloat16)
    grad_out = product("hp,cp->hc", hidden, pred_grad)
    hidden_grad = (product("hc,cp->hp", mlp_out, pred_grad) * gelu_slope(hidden_pre)).astype(
        jnp.bfloat16
    )
    grad_grid = product("cp,hp->ch", gathered, hidden_grad)
    grad_part = product("cp,hp->ch", part_feat, hidden_grad)
    gathered_grad = product("ch,hp->cp", mlp_grid, hidden_grad).astype(jnp.bfloat16)
    return (pred_full.astype(jnp.bfloat16), grad_grid, grad_part, grad_out, gathered_grad)


def send_out(features, places):
    return (
        lax.all_to_all(features, ("gx", "gy"), split_axis=1, concat_axis=1, tiled=True),
        lax.all_to_all(places, ("gx", "gy"), split_axis=1, concat_axis=1, tiled=True),
    )


def send_back(values):
    return lax.all_to_all(values, ("gx", "gy"), split_axis=1, concat_axis=1, tiled=True)


def shards(
    part_feat,
    target,
    block_tile,
    block_patch,
    cell_idx,
    block_fill,
    conv_in,
    conv_mid,
    conv_out,
    mlp_grid,
    mlp_part,
    mlp_out,
):
    channels = part_feat.shape[0]
    nblocks = block_tile.shape[0]
    devices = lax.axis_size("gx") * lax.axis_size("gy")
    capacity = max(2, 2 * nblocks // devices)
    slot_total = devices * capacity
    patch_cells = PR * PC
    patch_count = CR // PR * (CC // PC)
    owners = block_tile[:, 0]
    ordinal = jnp.arange(nblocks, dtype=jnp.int32)
    same_owner = owners[:, None] == owners[None, :]
    earlier = ordinal[None, :] < ordinal[:, None]
    rank_in = jnp.sum(jnp.logical_and(same_owner, earlier), axis=1)
    slot_of = owners * capacity + rank_in
    slot_match = slot_of[:, None] == jnp.arange(slot_total, dtype=jnp.int32)[None, :]
    slot_hot = slot_match.astype(jnp.bfloat16)
    within = jnp.arange(128, dtype=jnp.int32)
    alive = within[None, :] < block_fill[:, None]
    feat_blocks = part_feat.reshape(channels, nblocks, 128)
    feat_buffer = jnp.einsum(
        "kbj,bs->ksj", feat_blocks, slot_hot, preferred_element_type=jnp.float32
    ).astype(jnp.bfloat16)
    coded = jnp.where(alive, block_patch[:, None] * patch_cells + cell_idx, -1) + 1
    place_buffer = (jnp.sum(jnp.where(slot_match[:, :, None], coded[:, None, :], 0), axis=0) - 1)[
        None
    ]
    got_feat, got_place = send_out(feat_buffer, place_buffer)
    raw_places = got_place[0]
    slot_patch = jnp.max(raw_places, axis=1) // patch_cells
    patch_match = slot_patch[:, None] == jnp.arange(patch_count, dtype=jnp.int32)[None, :]
    patch_hot = patch_match.astype(jnp.float32)
    patch_pick = patch_match.astype(jnp.bfloat16)
    in_patch = raw_places - slot_patch[:, None] * patch_cells
    cell_match = jnp.logical_and(
        raw_places[:, :, None] >= 0,
        in_patch[:, :, None] == jnp.arange(patch_cells, dtype=jnp.int32)[None, None, :],
    )
    cell_hot = cell_match.astype(jnp.bfloat16)
    deposit = deposit_cells(got_feat, cell_hot, patch_hot)
    slot_counts = jnp.sum(cell_hot, axis=1, dtype=jnp.float32)
    counts = jnp.einsum("sc,sn->cn", slot_counts, patch_hot, precision=lax.Precision.HIGHEST)
    grid_input = from_patches((deposit / (1.0 + counts[None])).astype(jnp.bfloat16))
    grid_output, saved = unet_forward(grid_input, conv_in, conv_mid, conv_out)
    patch_values = to_patches(grid_output)
    slot_cells = jnp.einsum(
        "kcn,sn->ksc", patch_values, patch_pick, preferred_element_type=jnp.float32
    ).astype(jnp.bfloat16)
    slot_values = jnp.einsum(
        "ksc,sjc->ksj", slot_cells, cell_hot, preferred_element_type=jnp.float32
    ).astype(jnp.bfloat16)
    got_values = send_back(slot_values)
    gathered = (
        jnp.einsum("ksj,bs->kbj", got_values, slot_hot, preferred_element_type=jnp.float32)
        .astype(jnp.bfloat16)
        .reshape(channels, nblocks * 128)
    )
    living = alive.reshape(1, -1).astype(jnp.float32)
    scale = 1.0 / math.sqrt(nblocks * 128 * devices)
    pred, grad_grid, grad_part, grad_out, gathered_grad = particle_head(
        gathered, part_feat, target, living, mlp_grid, mlp_part, mlp_out, scale
    )
    grad_buffer = jnp.einsum(
        "kbj,bs->ksj",
        gathered_grad.reshape(channels, nblocks, 128),
        slot_hot,
        preferred_element_type=jnp.float32,
    ).astype(jnp.bfloat16)
    got_grads = send_back(grad_buffer)
    output_grad = from_patches(deposit_cells(got_grads, cell_hot, patch_hot).astype(jnp.bfloat16))
    grad_in, grad_mid, grad_conv = unet_backward(output_grad, saved, conv_mid, conv_out)
    sums = lax.psum((grad_in, grad_mid, grad_conv, grad_grid, grad_part, grad_out), ("gx", "gy"))
    return (pred, sums[0], sums[1], sums[2], sums[3], sums[4], sums[5])


def solution(mesh):
    return jax.shard_map(
        shards,
        mesh=mesh,
        in_specs=(
            P(None, ("gx", "gy")),
            P(None, ("gx", "gy")),
            P(("gx", "gy"), None),
            P(("gx", "gy")),
            P(("gx", "gy"), None),
            P(("gx", "gy")),
            P(),
            P(),
            P(),
            P(),
            P(),
            P(),
        ),
        out_specs=(P(None, ("gx", "gy")), P(), P(), P(), P(), P(), P()),
        check_vma=False,
    )
```

profile of v0, /device:TPU:1, one launch (start us, length us, event | category | flops | bytes accessed | tf_op | source)
XLA Modules:
  0.0 710.4 jit_solution(9748671624651863107)
XLA Ops:
  13.8 11.5 %all-to-all-start = ((s32[1,256,128]{2,0,1:T(1,128)}), s32[1,256,128]{2,0,1:T(1,128)S(1)}, u32[]{:S(2)}, u32[]{:S(2)}) async-start(s32[1,256,128]{2,0,1:T(1,128)} %bitcast.5), calls=%async_computation | async-start | bytes 262144 | tf_op jit(solution)/shard_map/all_to_all | solution.py:171
  28.2 4.7 copy.323
  35.3 7.8 %all-to-all-start.1 = ((bf16[64,256,128]{2,0,1:T(8,128)(2,1)}), bf16[64,256,128]{2,0,1:T(8,128)(2,1)}, u32[]{:S(2)}, u32[]{:S(2)}) async-start(bf16[64,256,128]{2,0,1:T(8,128)(2,1)} %copy.323), calls=%async_computation.1 | async-start | bytes 8388608 | tf_op jit(solution)/shard_map/all_to_all | solution.py:170
  43.1 4.7 reduce_max.9
  48.0 11.2 %convert_reduce_fusion = f32[256,128]{1,0:T(8,128)S(1)} fusion(s32[256,128]{1,0:T(8,128)S(1)} %broadcast_subtract_fusion, pred[256,128]{1,0:T(8,128)(4,1)S(1)} %broadcast_compare_fusion), kind=kLoop, calls=%fused_computation | loop fusion | flops 20938752 | bytes 294912 | tf_op jit(solution)/shard_map/reduce_sum | solution.py:231
  59.4 36.6 %all-to-all-done.1 = bf16[64,256,128]{2,0,1:T(8,128)(2,1)} async-done(((bf16[64,256,128]{2,0,1:T(8,128)(2,1)}), bf16[64,256,128]{2,0,1:T(8,128)(2,1)}, u32[]{:S(2)}, u32[]{:S(2)}) %all-to-all-start.1) | async-done | bytes 4194336 | tf_op jit(solution)/shard_map/all_to_all | solution.py:170
  95.9 16.5 %fusion.28 = f32[64,256,128]{2,0,1:T(8,128)S(1)} fusion(bf16[64,256,128]{2,0,1:T(8,128)(2,1)} %all-to-all-done.1, s32[256,128]{1,0:T(8,128)S(1)} %broadcast_subtract_fusion, pred[256,128]{1,0:T(8,128)(4,1)S(1)} %broadcast_compare_fusion), kind=kOutput, calls=%fused_computation.42 | convolution fusion | flops 545259520 | bytes 12746752 | tf_op jit(solution)/shard_map/ksj,sjc->ksc/dot_general | solution.py:114
  112.4 7.8 %fusion.67 = bf16[64,128,32]{1,2,0:T(8,128)(2,1)S(1)} fusion(f32[64,256,128]{2,0,1:T(8,128)S(1)} %fusion.28, f32[128,32]{0,1:T(8,128)S(1)} %convolution_add_fusion.1, s32[256]{0:T(256)S(1)} %get-tuple-element.14), kind=kOutput, calls=%fused_computation.81 | convolution fusion | flops 805838848 | bytes 8930304 | tf_op jit(solution)/shard_map/ksc,sn->kcn/dot_general | solution.py:115
  173.0 4.7 collective-permute-start.8
  184.3 4.6 collective-permute-start.10
  211.7 17.3 %convert_bitcast_fusion.1 = bf16[64,256,128]{2,0,1:T(8,128)(2,1)} fusion(bf16[64,256,128]{2,1,0:T(8,128)(2,1)S(1)} %convert_bitcast_fusion.2, s32[256,128]{1,0:T(8,128)S(1)} %broadcast_subtract_fusion, pred[256,128]{1,0:T(8,128)(4,1)S(1)} %broadcast_compare_fusion), kind=kOutput, calls=%fused_computation.37 | convolution fusion | flops 547356672 | bytes 8552448 | tf_op jit(solution)/shard_map/ksc,sjc->ksj/dot_general | solution.py:239
  229.0 11.5 %all-to-all-start.2 = ((bf16[64,256,128]{2,0,1:T(8,128)(2,1)}), bf16[64,256,128]{2,0,1:T(8,128)(2,1)}, u32[]{:S(2)}, u32[]{:S(2)}) async-start(bf16[64,256,128]{2,0,1:T(8,128)(2,1)} %convert_bitcast_fusion.1), calls=%async_computation.2 | async-start | bytes 8388608 | tf_op jit(solution)/shard_map/all_to_all | solution.py:176
  240.6 52.6 %all-to-all-done.2 = bf16[64,256,128]{2,0,1:T(8,128)(2,1)} async-done(((bf16[64,256,128]{2,0,1:T(8,128)(2,1)}), bf16[64,256,128]{2,0,1:T(8,128)(2,1)}, u32[]{:S(2)}, u32[]{:S(2)}) %all-to-all-start.2) | async-done | bytes 4194336 | tf_op jit(solution)/shard_map/all_to_all | solution.py:176
  293.2 4.8 fusion.60
  308.9 4.6 copy.358
  313.5 5.4 all-to-all-start.3
  328.2 6.8 copy.381
  339.5 32.3 %all-to-all-done.3 = bf16[64,256,128]{2,0,1:T(8,128)(2,1)} async-done(((bf16[64,256,128]{2,0,1:T(8,128)(2,1)}), bf16[64,256,128]{2,0,1:T(8,128)(2,1)}, u32[]{:S(2)}, u32[]{:S(2)}) %all-to-all-start.3) | async-done | bytes 4194336 | tf_op jit(solution)/shard_map/all_to_all | solution.py:176
  371.8 16.3 %fusion.31 = f32[64,256,128]{2,0,1:T(8,128)S(1)} fusion(bf16[64,256,128]{2,0,1:T(8,128)(2,1)} %all-to-all-done.3, s32[256,128]{1,0:T(8,128)S(1)} %broadcast_subtract_fusion, pred[256,128]{1,0:T(8,128)(4,1)S(1)} %broadcast_compare_fusion), kind=kOutput, calls=%fused_computation.43 | convolution fusion | flops 545259520 | bytes 12746752 | tf_op jit(solution)/shard_map/ksj,sjc->ksc/dot_general | solution.py:114
  388.1 7.8 %fusion.70 = bf16[64,128,32]{1,2,0:T(8,128)(2,1)S(1)} fusion(f32[64,256,128]{2,0,1:T(8,128)S(1)} %fusion.31, s32[256]{0:T(256)S(1)} %copy-done.25), kind=kOutput, calls=%fused_computation.82 | convolution fusion | flops 805576704 | bytes 8913920 | tf_op jit(solution)/shard_map/ksc,sn->kcn/dot_general | solution.py:115
  412.4 14.4 %fusion.57 = f32[3,3,64,64]{3,2,1,0:T(8,128)} fusion(bf16[1,64,18,258]{1,0,3,2:T(2,128)(2,1)} %copy.381, bf16[1,64,16,256]{1,3,2,0:T(8,128)(2,1)S(1)} %bitcast.254), kind=kOutput, calls=%fused_computation.72 | convolution fusion | flops 301989888 | bytes 1266176 | tf_op jit(solution)/shard_map/transpose | solution.py:74
  459.3 13.2 %fusion.41 = f32[3,3,64,64]{3,2,1,0:T(8,128)} fusion(bf16[1,64,18,258]{1,3,2,0:T(8,128)(2,1)S(1)} %copy-done.13, bf16[1,64,16,256]{1,2,3,0:T(8,128)(2,1)S(1)} %fusion.54), kind=kOutput, calls=%fused_computation.49 | convolution fusion | flops 301989888 | bytes 1266176 | tf_op jit(solution)/shard_map/transpose | solution.py:74
  472.6 69.9 %all-reduce.5.cloned.1.call-done = (f32[64,128]{1,0:T(8,128)}, f32[64,128]{1,0:T(8,128)}, f32[128,64]{0,1:T(8,128)}) async-done(((f32[64,128]{1,0:T(8,128)}, f32[64,128]{1,0:T(8,128)}, f32[128,64]{0,1:T(8,128)}), (f32[64,128]{1,0:T(8,128)}, f32[64,128]{1,0:T(8,128)}, f32[128,64]{0,1:T(8,128)})) %all-reduce.5.cloned.1.call-update) | async-done | bytes 98320 | tf_op jit(solution)/shard_map/psum | solution.py:262
  542.5 151.4 %all-reduce.7.cloned.1.call-done = (f32[9,64,64]{2,1,0:T(8,128)}, f32[9,64,64]{2,1,0:T(8,128)}, f32[9,64,64]{2,1,0:T(8,128)}) async-done(((f32[9,64,64]{2,1,0:T(8,128)}, f32[9,64,64]{2,1,0:T(8,128)}, f32[9,64,64]{2,1,0:T(8,128)}), (f32[9,64,64]{2,1,0:T(8,128)}, f32[9,64,64]{2,1,0:T(8,128)}, f32[9,64,64]{2,1,0:T(8,128)})) %all-reduce.7.cloned.1.call-update) | async-done | bytes 442384 | tf_op jit(solution)/shard_map/psum | solution.py:262
  (236 shorter events, 176.5 us)
Async XLA Ops:
  13.8 21.5 %all-to-all-start = ((s32[1,256,128]{2,0,1:T(1,128)}), s32[1,256,128]{2,0,1:T(1,128)S(1)}, u32[]{:S(2)}, u32[]{:S(2)}) async-start(s32[1,256,128]{2,0,1:T(1,128)} %bitcast.5), calls=%async_computation | async-start | bytes 262144 | tf_op jit(solution)/shard_map/all_to_all | solution.py:171
  35.3 60.6 %all-to-all-start.1 = ((bf16[64,256,128]{2,0,1:T(8,128)(2,1)}), bf16[64,256,128]{2,0,1:T(8,128)(2,1)}, u32[]{:S(2)}, u32[]{:S(2)}) async-start(bf16[64,256,128]{2,0,1:T(8,128)(2,1)} %copy.323), calls=%async_computation.1 | async-start | bytes 8388608 | tf_op jit(solution)/shard_map/all_to_all | solution.py:170
  122.3 4.8 collective-permute-start
  125.2 5.6 collective-permute-start.1
  149.5 5.0 collective-permute-start.4
  152.6 5.2 collective-permute-start.5
  158.0 5.1 collective-permute-start.6
  160.7 6.4 collective-permute-start.7
  173.0 7.5 %collective-permute-start.8 = (bf16[64,1,256]{0,1,2:T(2,128)(2,1)S(1)}, bf16[64,1,256]{0,1,2:T(2,128)(2,1)S(1)}, u32[]{:S(2)}, u32[]{:S(2)}) collective-permute-start(bf16[64,1,256]{0,1,2:T(2,128)(2,1)S(1)} %get-tuple-element.27), channel_id=1, source_target_pairs={{0,1},{1,2},{2,3},{3,4},{4,5},{5,6},{6,7},{8,9},{9,10},{10,11},{11... | collective-permute-start | bytes 98312 | tf_op jit(solution)/shard_map/ppermute | solution.py:26
  177.7 6.3 collective-permute-start.9
  184.3 8.8 %collective-permute-start.10 = (bf16[64,18,1]{2,0,1:T(8,128)(2,1)S(1)}, bf16[64,18,1]{2,0,1:T(8,128)(2,1)S(1)}, u32[]{:S(2)}, u32[]{:S(2)}) collective-permute-start(bf16[64,18,1]{2,0,1:T(8,128)(2,1)S(1)} %get-tuple-element.31), channel_id=1, source_target_pairs={{0,8},{8,16},{16,24},{24,32},{32,40},{40,48},{48,56},{56,64},{64,7... | collective-permute-start | bytes 6920 | tf_op jit(solution)/shard_map/ppermute | solution.py:26
  188.9 8.5 %collective-permute-start.11 = (bf16[64,18,1]{2,0,1:T(8,128)(2,1)S(1)}, bf16[64,18,1]{2,0,1:T(8,128)(2,1)S(1)}, u32[]{:S(2)}, u32[]{:S(2)}) collective-permute-start(bf16[64,18,1]{2,0,1:T(8,128)(2,1)S(1)} %get-tuple-element.32), channel_id=1, source_target_pairs={{8,0},{16,8},{24,16},{32,24},{40,32},{48,40},{56,48},{64,56},{72,6... | collective-permute-start | bytes 6920 | tf_op jit(solution)/shard_map/ppermute | solution.py:28
  229.0 64.2 %all-to-all-start.2 = ((bf16[64,256,128]{2,0,1:T(8,128)(2,1)}), bf16[64,256,128]{2,0,1:T(8,128)(2,1)}, u32[]{:S(2)}, u32[]{:S(2)}) async-start(bf16[64,256,128]{2,0,1:T(8,128)(2,1)} %convert_bitcast_fusion.1), calls=%async_computation.2 | async-start | bytes 8388608 | tf_op jit(solution)/shard_map/all_to_all | solution.py:176
  313.5 58.3 %all-to-all-start.3 = ((bf16[64,256,128]{2,0,1:T(8,128)(2,1)}), bf16[64,256,128]{2,0,1:T(8,128)(2,1)}, u32[]{:S(2)}, u32[]{:S(2)}) async-start(bf16[64,256,128]{2,0,1:T(8,128)(2,1)} %copy.358), calls=%async_computation.3 | async-start | bytes 8388608 | tf_op jit(solution)/shard_map/all_to_all | solution.py:176
  318.8 223.7 %all-reduce.5.cloned.1.call-start = ((), (), s32[]{:S(2)}) async-start(), calls=%async_computation.4 | async-start | bytes 196608 | tf_op jit(solution)/shard_map/psum | solution.py:262
  400.1 6.2 collective-permute-start.12
  403.0 5.6 collective-permute-start.13
  406.3 287.6 %all-reduce.7.cloned.1.call-start = ((), (), s32[]{:S(2)}) async-start(), calls=%async_computation.5 | async-start | bytes 1769472 | tf_op jit(solution)/shard_map/psum | solution.py:262
  409.2 17.5 %collective-permute-start.14 = (bf16[64,18,1]{0,2,1:T(2,128)(2,1)}, bf16[64,18,1]{0,2,1:T(2,128)(2,1)}, u32[]{:S(2)}, u32[]{:S(2)}) collective-permute-start(bf16[64,18,1]{0,2,1:T(2,128)(2,1)} %get-tuple-element.21), channel_id=1, source_target_pairs={{0,8},{8,16},{16,24},{24,32},{32,40},{40,48},{48,56},{56,64},{64,7... | collective-permute-start | bytes 6920 | tf_op jit(solution)/shard_map/ppermute | solution.py:26
  411.1 15.7 %collective-permute-start.15 = (bf16[64,18,1]{0,2,1:T(2,128)(2,1)}, bf16[64,18,1]{0,2,1:T(2,128)(2,1)}, u32[]{:S(2)}, u32[]{:S(2)}) collective-permute-start(bf16[64,18,1]{0,2,1:T(2,128)(2,1)} %get-tuple-element.22), channel_id=1, source_target_pairs={{8,0},{16,8},{24,16},{32,24},{40,32},{48,40},{56,48},{64,56},{72,6... | collective-permute-start | bytes 6920 | tf_op jit(solution)/shard_map/ppermute | solution.py:28
  435.4 5.4 collective-permute-start.16
  438.4 5.2 collective-permute-start.17
  443.8 10.4 %collective-permute-start.18 = (bf16[64,10,1]{2,0,1:T(8,128)(2,1)S(1)}, bf16[64,10,1]{2,0,1:T(8,128)(2,1)S(1)}, u32[]{:S(2)}, u32[]{:S(2)}) collective-permute-start(bf16[64,10,1]{2,0,1:T(8,128)(2,1)S(1)} %get-tuple-element.35), channel_id=1, source_target_pairs={{0,8},{8,16},{16,24},{24,32},{32,40},{40,48},{48,56},{56,64},{64,7... | collective-permute-start | bytes 3848 | tf_op jit(solution)/shard_map/ppermute | solution.py:26
  448.3 6.5 collective-permute-start.19
  (38 other events, 726.1 us)
Sparse Core Ops, SparseCore 0:
  406.4 136.0 all-reduce.4
  549.2 144.6 all-reduce.6
where the time goes:
time: 721 us; the launch traced here: 710 us
  waiting for transfers between devices  377 us (52%)
  matrix products  133 us (18%)
  starting transfers between devices  83.7 us (12%)
  local copies, waits for them, and re-layouts  67.4 us (9%)
  other arithmetic  33.8 us (5%)
  between operations  15.7 us (2%)
    psum x2, waiting for transfers between devices, shards(): lax.psum((grad_in, grad_mid, grad_conv, grad_grid, grad_part, grad_out),...  221 us
    all_to_all x2, waiting for transfers between devices, send_back(): lax.all_to_all(values, ('gx', 'gy'), split_axis=1, concat_axis=1, tiled=T...  84.9 us
    all_to_all x1, waiting for transfers between devices, send_out(): lax.all_to_all(features, ('gx', 'gy'), split_axis=1, concat_axis=1, tiled...  36.6 us
    dot_general x2, matrix products, deposit_cells(): jnp.einsum('ksj,sjc->ksc', values, cell_hot, preferred_element_type=jnp.f...  32.7 us
    transpose x3, matrix products, weight_term(): jnp.transpose(result, (2, 3, 0, 1))  31.6 us
    ppermute x10, starting transfers between devices, with_halo(): lax.ppermute(tail, axis, [(i, (i + 1) % count) for i in range(ends)])  30.4 us
    ppermute x10, waiting for transfers between devices, with_halo(): lax.ppermute(head, axis, [((i + 1) % count, i) for i in range(ends)])  27.5 us
    dot_general x1, matrix products, shards(): jnp.einsum('ksc,sjc->ksj', slot_cells, cell_hot, preferred_element_type=j...  17.3 us
  transfers between devices with their start and end apart: 26, of which 17 were waited for; matrix products, arithmetic and copies ran while one was open for 13% of the time, Pallas kernels for 0%

commit v1 on v0

v1 whole, which is shorter than its diff:
```python
import functools
import math

import jax
import jax.numpy as jnp
from jax import lax
from jax.experimental import pallas as pl
from jax.experimental.pallas import tpu as pltpu
from jax.sharding import PartitionSpec as P

CH = 64
HID = 128
CR = 16
CC = 256
LANES = 128
WIDE = 384
NPATCH = 32
META = 16
SLOT_ROWS = 2 * CH + META
HALO_IN = 5
HALO_OUT = 3
REDUCE_ROWS = 2048

root_two_pi = 0.7978845608028654
cubic_coef = 0.044715

VMEM_LIMIT = 56 * 1024 * 1024
BF = jnp.bfloat16
F32 = jnp.float32


def params():
    return pltpu.CompilerParams(vmem_limit_bytes=VMEM_LIMIT)


def cost(flops, moved, tanhs=0):
    return pl.CostEstimate(flops=flops, bytes_accessed=moved, transcendentals=tanhs)


def smem():
    return pl.BlockSpec(memory_space=pltpu.SMEM)


def vmem():
    return pl.BlockSpec(memory_space=pltpu.VMEM)


def whole(shape):
    return pl.BlockSpec(shape, lambda i: (0,) * len(shape))


def nt_dot(left, right):
    return lax.dot_general(left, right, (((1,), (1,)), ((), ())), preferred_element_type=F32)


def dot(left, right):
    return jnp.dot(left, right, preferred_element_type=F32)


def gelu_both(value):
    square = value * value
    inner = jnp.tanh(value * (root_two_pi + (root_two_pi * cubic_coef) * square))
    half = 0.5 + 0.5 * inner
    result = value * half
    bend = 2.0 * root_two_pi + (6.0 * cubic_coef * root_two_pi) * square
    return result, half + (result - result * half) * bend


def gelu_value(value):
    inner = jnp.tanh(value * (root_two_pi + (root_two_pi * cubic_coef) * (value * value)))
    return value * (0.5 + 0.5 * inner)


def lane_index(shape):
    return lax.broadcasted_iota(jnp.int32, shape, len(shape) - 1)


def place_blocks(tile_s, slot_s, count_s, blocks, devices):
    def clear(i, carry):
        count_s[i] = 0
        slot_s[2 * i] = -1
        slot_s[2 * i + 1] = -1
        return carry

    def place(b, carry):
        owner = tile_s[b]
        rank = count_s[owner]
        slot_s[2 * owner + rank] = b
        count_s[owner] = rank + 1
        return carry

    lax.fori_loop(0, devices, clear, 0, unroll=16)
    lax.fori_loop(0, blocks, place, 0, unroll=8)


def block_lanes(b):
    return pl.ds(pl.multiple_of(b * LANES, LANES), LANES)


def dispatch_kernel(blocks, devices, per, tile_s, patch_s, fill_s, cell_ref, feat_ref, out_ref, slot_s, count_s):
    step = pl.program_id(0)

    @pl.when(step == 0)
    def _():
        place_blocks(tile_s, slot_s, count_s, blocks, devices)

    def one(i, carry):
        owner = step * per + i
        row = lax.broadcasted_iota(jnp.int32, (META, LANES), 0)
        lane = lane_index((1, LANES))
        meta = jnp.zeros((META, LANES), F32)
        for r in range(2):
            b = slot_s[2 * owner + r]
            at = jnp.maximum(b, 0)
            out_ref[i, r * CH : (r + 1) * CH, :] = feat_ref[:, block_lanes(at)]
            fill = jnp.where(b >= 0, fill_s[at], 0)
            code = jnp.where(lane < fill, cell_ref[pl.ds(at, 1), :], -1).astype(F32)
            meta = jnp.where(row == r, code, meta)
            meta = jnp.where(row == 2 + r, patch_s[at].astype(F32), meta)
        out_ref[i, 2 * CH :, :] = meta.astype(BF)
        return carry

    lax.fori_loop(0, per, one, 0, unroll=16)


def route_scratch(devices):
    return [pltpu.SMEM((2 * devices,), jnp.int32), pltpu.SMEM((devices,), jnp.int32)]


def dispatch(tile, patch, fill, cells, features, devices):
    blocks = tile.shape[0]
    steps = 4
    per = devices // steps
    return pl.pallas_call(
        functools.partial(dispatch_kernel, blocks, devices, per),
        grid=(steps,),
        in_specs=[smem(), smem(), smem(), whole(cells.shape), whole(features.shape)],
        out_specs=pl.BlockSpec((per, SLOT_ROWS, LANES), lambda i: (i, 0, 0)),
        out_shape=jax.ShapeDtypeStruct((devices, SLOT_ROWS, LANES), BF),
        scratch_shapes=route_scratch(devices),
        compiler_params=params(),
        cost_estimate=cost(0, 6 << 20),
        name="dispatch",
    )(tile, patch, fill, cells, features)


def dispatch_target_kernel(blocks, devices, per, tile_s, feat_ref, first_ref, second_ref, slot_s, count_s):
    step = pl.program_id(0)

    @pl.when(step == 0)
    def _():
        place_blocks(tile_s, slot_s, count_s, blocks, devices)

    def one(i, carry):
        owner = step * per + i
        for r, out_ref in enumerate((first_ref, second_ref)):
            at = jnp.maximum(slot_s[2 * owner + r], 0)
            out_ref[i] = feat_ref[:, block_lanes(at)]
        return carry

    lax.fori_loop(0, per, one, 0, unroll=16)


def dispatch_target(tile, features, devices):
    blocks = tile.shape[0]
    steps = 4
    per = devices // steps
    shape = jax.ShapeDtypeStruct((devices, CH, LANES), BF)
    spec = pl.BlockSpec((per, CH, LANES), lambda i: (i, 0, 0))
    return pl.pallas_call(
        functools.partial(dispatch_target_kernel, blocks, devices, per),
        grid=(steps,),
        in_specs=[smem(), whole(features.shape)],
        out_specs=[spec, spec],
        out_shape=[shape, shape],
        scratch_shapes=route_scratch(devices),
        compiler_params=params(),
        cost_estimate=cost(0, 6 << 20),
        name="dispatch_target",
    )(tile, features)


def home_kernel(blocks, devices, tile_s, got_ref, feat_ref, w_hidden, w_pred, out_ref, pair, count_s):
    def clear(i, carry):
        count_s[i] = 0
        return carry

    lax.fori_loop(0, devices, clear, 0, unroll=16)

    def one(b, carry):
        owner = tile_s[b]
        rank = count_s[owner]
        count_s[owner] = rank + 1
        rows = pl.ds(pl.multiple_of(rank * CH, CH), CH)
        pair[:CH, block_lanes(b)] = got_ref[owner, rows, :]
        return carry

    lax.fori_loop(0, blocks, one, 0, unroll=8)
    pair[CH:, :] = feat_ref[...]
    span = 2048
    for start in range(0, blocks * LANES, span):
        lanes = slice(start, start + span)
        value = gelu_value(dot(w_hidden[...], pair[:, lanes])).astype(BF)
        out_ref[:, lanes] = dot(w_pred[...], value).astype(BF)


def home_predictions(tile, got, features, w_hidden, w_pred, devices):
    blocks = tile.shape[0]
    return pl.pallas_call(
        functools.partial(home_kernel, blocks, devices),
        in_specs=[smem()] + [vmem()] * 4,
        out_specs=vmem(),
        out_shape=jax.ShapeDtypeStruct((CH, blocks * LANES), BF),
        scratch_shapes=[
            pltpu.VMEM((2 * CH, blocks * LANES), BF),
            pltpu.SMEM((devices,), jnp.int32),
        ],
        compiler_params=params(),
        cost_estimate=cost(2 * 8192 * 128 * 192, 8 << 20, 8192 * 128),
        name="home_predictions",
    )(tile, got, features, w_hidden, w_pred)


def prepare_kernel(conv_in, conv_mid, conv_out, mlp_grid, mlp_part, mlp_out_t, w_in, w_mid, w_out, f_mid, f_out, w_hidden, w_back):
    for conv, out, flip in ((conv_in, w_in, None), (conv_mid, w_mid, f_mid), (conv_out, w_out, f_out)):
        for dr in range(3):
            for dq in range(3):
                rows = slice(dq * CH, (dq + 1) * CH)
                lanes = slice(dr * CH, (dr + 1) * CH)
                out[rows, lanes] = conv[3 * dr + dq].astype(F32).T.astype(BF)
                if flip is not None:
                    flip[rows, lanes] = conv[8 - 3 * dr - dq]
    w_hidden[:, :CH] = mlp_grid[...].astype(F32).T.astype(BF)
    w_hidden[:, CH:] = mlp_part[...].astype(F32).T.astype(BF)
    w_back[...] = mlp_out_t[...].astype(F32).T.astype(BF)


def prepare(*weights):
    square = jax.ShapeDtypeStruct((3 * CH, 3 * CH), BF)
    shapes = [square] * 5 + [
        jax.ShapeDtypeStruct((HID, 2 * CH), BF),
        jax.ShapeDtypeStruct((HID, CH), BF),
    ]
    return pl.pallas_call(
        prepare_kernel,
        in_specs=[vmem()] * len(weights),
        out_specs=[vmem()] * len(shapes),
        out_shape=shapes,
        compiler_params=params(),
        cost_estimate=cost(0, 1 << 20),
        name="prepare",
    )(*weights)


def swap_blocks(parts):
    parts = list(parts)
    group = lane_index(parts[0].shape) // 16
    for s in (4, 2, 1):
        keep = (group & s) == 0
        for i in range(8):
            if i & s:
                continue
            a, b = parts[i], parts[i + s]
            parts[i] = jnp.where(keep, a, pltpu.roll(b, s * 16, 1))
            parts[i + s] = jnp.where(keep, pltpu.roll(a, LANES - s * 16, 1), b)
    return parts


def patches_to_rows(patch_of, own_ref):
    for part in range(4):
        first, half = part // 2, part % 2
        rows = swap_blocks([patch_of(first * 16 + half * 8 + k) for k in range(8)])
        for r in range(8):
            own_ref[first * 8 + r, :, half * LANES : (half + 1) * LANES] = rows[r].astype(BF)


def write_strips(width, own_ref, head_ref, tail_ref, left_ref, right_ref):
    for r in range(width):
        for half in range(2):
            lanes = slice(half * LANES, (half + 1) * LANES)
            head_ref[2 * r + half] = own_ref[r, :, lanes]
            tail_ref[2 * r + half] = own_ref[CR - width + r, :, lanes]
    group = lane_index((CH, LANES)) // 8
    left = jnp.zeros((CH, LANES), F32)
    right = jnp.zeros((CH, LANES), F32)
    for r in range(CR):
        piece = own_ref[r, :, :LANES].astype(F32)
        left = jnp.where(group == r, pltpu.roll(piece, 8 * r, 1) if r else piece, left)
        piece = own_ref[r, :, LANES:].astype(F32)
        turn = (8 * r + 8) % LANES
        right = jnp.where(group == r, pltpu.roll(piece, turn, 1) if turn else piece, right)
    left_ref[0] = left.astype(BF)
    right_ref[0] = right.astype(BF)


def strip_shapes(width):
    return [
        jax.ShapeDtypeStruct((CR, CH, CC), BF),
        jax.ShapeDtypeStruct((2 * width, CH, LANES), BF),
        jax.ShapeDtypeStruct((2 * width, CH, LANES), BF),
        jax.ShapeDtypeStruct((1, CH, LANES), BF),
        jax.ShapeDtypeStruct((1, CH, LANES), BF),
    ]


def exchange(head, tail, left, right):
    def ahead(value, axis):
        count = lax.axis_size(axis)
        return lax.ppermute(value, axis, [(i, i + 1) for i in range(count - 1)])

    def behind(value, axis):
        count = lax.axis_size(axis)
        return lax.ppermute(value, axis, [(i + 1, i) for i in range(count - 1)])

    from_left = ahead(right, "gx")
    from_right = behind(left, "gx")
    above = ahead(tail, "gy")
    below = behind(head, "gy")
    sides = jnp.concatenate([from_left, from_right], axis=0)
    return above, below, sides, ahead(sides, "gy"), behind(sides, "gy")


def side_lanes(left, right, r):
    lane = lane_index((CH, LANES))
    turn_right = (LANES - 8 * r) % LANES
    turn_left = (120 - 8 * r) % LANES
    right = pltpu.roll(right, turn_right, 1) if turn_right else right
    left = pltpu.roll(left, turn_left, 1) if turn_left else left
    return jnp.where(lane < 8, right, jnp.where(lane >= 120, left, 0.0)).astype(BF)


def fill_wide(width, wide, own_ref, above_ref, below_ref, sides_ref, above_sides, below_sides):
    left, right = sides_ref[0].astype(F32), sides_ref[1].astype(F32)
    for r in range(CR):
        wide[width + r, :, :CC] = own_ref[r]
        wide[width + r, :, CC:] = side_lanes(left, right, r)
    left, right = above_sides[0].astype(F32), above_sides[1].astype(F32)
    for r in range(width):
        wide[r, :, :LANES] = above_ref[2 * r]
        wide[r, :, LANES:CC] = above_ref[2 * r + 1]
        wide[r, :, CC:] = side_lanes(left, right, CR - width + r)
    left, right = below_sides[0].astype(F32), below_sides[1].astype(F32)
    for r in range(width):
        at = width + CR + r
        wide[at, :, :LANES] = below_ref[2 * r]
        wide[at, :, LANES:CC] = below_ref[2 * r + 1]
        wide[at, :, CC:] = side_lanes(left, right, r)


def conv_row(source, at, weight, shift):
    stacked = source[pl.ds(at, 3)].reshape(3 * CH, WIDE)
    terms = dot(weight, stacked)
    return (
        terms[CH : 2 * CH]
        + pltpu.roll(terms[:CH], shift, 1)
        + pltpu.roll(terms[2 * CH :], WIDE - shift, 1)
    )


def pair_sum(value):
    even = (lane_index(value.shape) & 1) == 0
    return value + jnp.where(even, pltpu.roll(value, WIDE - 1, 1), pltpu.roll(value, 1, 1))


def column_mask(gx, columns):
    lane = lane_index((1, WIDE))
    right = jnp.where(gx < columns - 1, 1.0, 0.0)
    left = jnp.where(gx > 0, 1.0, 0.0)
    return jnp.where(lane < CC, 1.0, jnp.where(lane < CC + 64, right, left))


def one_hot(code):
    cell = lax.broadcasted_iota(jnp.int32, (LANES, LANES), 0).astype(F32).astype(BF)
    code = jnp.broadcast_to(code, (16, LANES)).astype(BF)
    match = cell.reshape(8, 16, LANES) == code[None]
    return jnp.where(match, jnp.ones((), BF), jnp.zeros((), BF)).reshape(LANES, LANES)


def deposit_kernel(per, last, got_ref, own, head, tail, left, right, patch_s, total):
    step = pl.program_id(0)

    @pl.when(step == 0)
    def _():
        total[...] = jnp.zeros_like(total)

    ones = jnp.ones((META, LANES), BF)

    def one(i, carry):
        meta = got_ref[i, 2 * CH :, :].astype(F32)
        for r in range(2):
            feat = jnp.concatenate([got_ref[i, r * CH : (r + 1) * CH, :], ones], axis=0)
            at = meta[2 + r, 0].astype(jnp.int32)
            patch_s[2 * (step * per + i) + r] = at
            total[at] += nt_dot(feat, one_hot(meta[r : r + 1]))
        return carry

    lax.fori_loop(0, per, one, 0, unroll=32)

    @pl.when(step == last)
    def _():
        def patch_of(a):
            value = total[a]
            return value[:CH] / (1.0 + value[CH : CH + 1])

        patches_to_rows(patch_of, own)
        write_strips(HALO_IN, own, head, tail, left, right)


SELF_PATCH = 1


def deposit(got):
    devices = got.shape[0]
    steps = 4
    per = devices // steps
    shapes = strip_shapes(HALO_IN)
    return pl.pallas_call(
        functools.partial(deposit_kernel, per, steps - 1),
        grid=(steps,),
        in_specs=[pl.BlockSpec((per, SLOT_ROWS, LANES), lambda i: (i, 0, 0))],
        out_specs=[whole(s.shape) for s in shapes] + [smem()],
        out_shape=shapes + [jax.ShapeDtypeStruct((2 * devices,), jnp.int32)],
        scratch_shapes=[pltpu.VMEM((NPATCH, CH + META, LANES), F32)],
        compiler_params=params(),
        cost_estimate=cost(2 * 256 * 80 * 128 * 128, 6 << 20),
        name="deposit",
    )(got)


def forward_kernel(
    columns,
    rows,
    where_s,
    own,
    above,
    below,
    sides,
    above_sides,
    below_sides,
    w_in,
    w_mid,
    w_out,
    patches,
    wide,
    coarse,
    rebuilt,
    slope_in,
    slope_mid,
    fine,
    grid_out,
):
    gx, gy = where_s[0], where_s[1]
    across = column_mask(gx, columns)
    fill_wide(HALO_IN, wide, own, above, below, sides, above_sides, below_sides)

    def row_mask(row):
        at = gy * CR + row
        return jnp.where(jnp.logical_and(at >= 0, at < rows * CR), across, 0.0)

    def first(g, carry):
        total = None
        for j in range(2):
            pre = conv_row(wide, 2 * g + j, w_in[...], 1)
            value, slope = gelu_both(pre)
            value = (value * row_mask(2 * g + j - 4)).astype(BF)
            fine[2 * g + j] = value
            slope_in[2 * g + j] = slope[:, :CC]
            value = value.astype(F32)
            total = value if j == 0 else total + value
        coarse[g] = (0.25 * pair_sum(total)).astype(BF)
        return carry

    lax.fori_loop(0, 12, first, 0, unroll=2)

    def middle(g, carry):
        pre = conv_row(coarse, g, w_mid[...], 2)
        value, slope = gelu_both(pre)
        slope_mid[g] = slope
        before = coarse[g + 1].astype(F32)
        change = (before + value).astype(BF).astype(F32) - before
        for j in range(2):
            row = fine[2 * g + 2 + j].astype(F32) + change
            rebuilt[2 * g + j] = (row * row_mask(2 * g + j - 2)).astype(BF)
        return carry

    lax.fori_loop(0, 10, middle, 0, unroll=2)

    def last(r, carry):
        grid_out[r] = conv_row(rebuilt, r + 1, w_out[...], 1)[:, :CC]
        return carry

    lax.fori_loop(0, CR, last, 0, unroll=4)
    for part in range(4):
        first_row, half = part // 2, part % 2
        lanes = slice(half * LANES, (half + 1) * LANES)
        found = swap_blocks([grid_out[first_row * 8 + r, :, lanes] for r in range(8)])
        for k in range(8):
            patches[first_row * 16 + half * 8 + k] = found[k].astype(BF)


def unet_forward(where, halo, w_in, w_mid, w_out, columns, rows):
    shapes = [
        jax.ShapeDtypeStruct((NPATCH, CH, LANES), BF),
        jax.ShapeDtypeStruct((CR + 2 * HALO_IN, CH, WIDE), BF),
        jax.ShapeDtypeStruct((12, CH, WIDE), BF),
        jax.ShapeDtypeStruct((20, CH, WIDE), BF),
        jax.ShapeDtypeStruct((24, CH, CC), F32),
        jax.ShapeDtypeStruct((10, CH, WIDE), F32),
    ]
    ins = (where, *halo, w_in, w_mid, w_out)
    return pl.pallas_call(
        functools.partial(forward_kernel, columns, rows),
        in_specs=[smem()] + [vmem()] * (len(ins) - 1),
        out_specs=[vmem()] * len(shapes),
        out_shape=shapes,
        scratch_shapes=[pltpu.VMEM((24, CH, WIDE), BF), pltpu.VMEM((CR, CH, CC), F32)],
        compiler_params=params(),
        cost_estimate=cost(2 * 50 * 192 * 192 * 384, 10 << 20, 34 * CH * WIDE),
        name="unet_forward",
    )(*ins)


def gather_kernel(per, patch_s, meta_ref, patches, out_ref):
    step = pl.program_id(0)

    def one(i, carry):
        meta = meta_ref[i].astype(F32)
        for r in range(2):
            patch = patch_s[2 * (step * per + i) + r]
            values = dot(patches[patch], one_hot(meta[r : r + 1]))
            out_ref[i, r * CH : (r + 1) * CH, :] = values.astype(BF)
        return carry

    lax.fori_loop(0, per, one, 0, unroll=32)


def gather(patch_at, got, patches):
    devices = got.shape[0]
    steps = 4
    per = devices // steps
    return pl.pallas_call(
        functools.partial(gather_kernel, per),
        grid=(steps,),
        in_specs=[
            smem(),
            pl.BlockSpec((per, META, LANES), lambda i: (i, 2 * CH // META, 0)),
            whole(patches.shape),
        ],
        out_specs=pl.BlockSpec((per, 2 * CH, LANES), lambda i: (i, 0, 0)),
        out_shape=jax.ShapeDtypeStruct((devices, 2 * CH, LANES), BF),
        compiler_params=params(),
        cost_estimate=cost(2 * 256 * 64 * 128 * 128, 6 << 20),
        name="gather",
    )(patch_at, got, patches)


GROUP = 16
GROUP_LANES = 2 * GROUP * LANES
PIECES = 1


def particle_kernel(
    last,
    scale,
    patch_s,
    got_ref,
    value_ref,
    first_ref,
    second_ref,
    w_hidden,
    w_pred,
    w_back,
    w_grid,
    own,
    head,
    tail,
    left,
    right,
    grads,
    total,
    pair,
    errors,
):
    step = pl.program_id(0)

    @pl.when(step == 0)
    def _():
        total[...] = jnp.zeros_like(total)
        grads[...] = jnp.zeros_like(grads)

    count = GROUP // PIECES
    span = 2 * count * LANES
    grad_hidden = jnp.zeros((HID, HID), F32)
    grad_pred = jnp.zeros((CH, HID), F32)
    for piece in range(PIECES):
        whole_lanes = slice(piece * span, (piece + 1) * span)
        codes = []
        for k in range(count):
            at = piece * count + k
            meta = got_ref[at, 2 * CH :, :].astype(F32)
            for r in range(2):
                rows = slice(r * CH, (r + 1) * CH)
                start = piece * span + (2 * k + r) * LANES
                lanes = slice(start, start + LANES)
                pair[:CH, lanes] = value_ref[at, rows, :]
                pair[CH:, lanes] = got_ref[at, rows, :]
                codes.append(meta[r : r + 1])
        inputs = pair[:, whole_lanes]
        hidden, slope = gelu_both(dot(w_hidden[...], inputs))
        hidden = hidden.astype(BF)
        pred = dot(w_pred[...], hidden)
        for k in range(count):
            for r, target_ref in enumerate((first_ref, second_ref)):
                slot = 2 * k + r
                lanes = slice(slot * LANES, (slot + 1) * LANES)
                live = jnp.where(codes[slot] >= 0.0, scale, 0.0)
                target = target_ref[piece * count + k].astype(F32)
                start = piece * span + slot * LANES
                errors[:, start : start + LANES] = (live * (pred[:, lanes] - target)).astype(BF)
        wrong = errors[:, whole_lanes]
        back = (dot(w_back[...], wrong) * slope).astype(BF)
        grad_hidden += nt_dot(inputs, back)
        grad_pred += nt_dot(wrong, hidden)
        given = dot(w_grid[...], back).astype(BF)
        for k in range(count):
            for r in range(2):
                slot = 2 * k + r
                patch = patch_s[2 * (step * GROUP + piece * count + k) + r]
                part = given[:, slot * LANES : (slot + 1) * LANES]
                total[patch] += nt_dot(part, one_hot(codes[slot]))
    grads[:HID] += grad_hidden
    grads[HID:] += grad_pred

    @pl.when(step == last)
    def _():
        patches_to_rows(lambda a: total[a], own)
        write_strips(HALO_OUT, own, head, tail, left, right)


def particles(patch_at, got, values, first, second, w_hidden, w_pred, w_back, w_grid, scale):
    devices = got.shape[0]
    steps = devices // GROUP
    half = pl.BlockSpec((GROUP, CH, LANES), lambda i: (i, 0, 0))
    shapes = strip_shapes(HALO_OUT) + [jax.ShapeDtypeStruct((HID + CH, HID), F32)]
    return pl.pallas_call(
        functools.partial(particle_kernel, steps - 1, scale),
        grid=(steps,),
        in_specs=[
            smem(),
            pl.BlockSpec((GROUP, SLOT_ROWS, LANES), lambda i: (i, 0, 0)),
            pl.BlockSpec((GROUP, 2 * CH, LANES), lambda i: (i, 0, 0)),
            half,
            half,
            whole(w_hidden.shape),
            whole(w_pred.shape),
            whole(w_back.shape),
            whole(w_grid.shape),
        ],
        out_specs=[whole(s.shape) for s in shapes],
        out_shape=shapes,
        scratch_shapes=[
            pltpu.VMEM((NPATCH, CH, LANES), F32),
            pltpu.VMEM((2 * CH, GROUP_LANES), BF),
            pltpu.VMEM((CH, GROUP_LANES), BF),
        ],
        compiler_params=params(),
        cost_estimate=cost(2 * 32768 * 128 * 700, 16 << 20, 32768 * 128),
        name="particles",
    )(patch_at, got, values, first, second, w_hidden, w_pred, w_back, w_grid)


def shifted(value, shift):
    value = jnp.concatenate([value, jnp.zeros((CH, LANES), F32)], axis=1)
    return jnp.concatenate(
        [pltpu.roll(value, WIDE - shift, 1), value, pltpu.roll(value, shift, 1)], axis=0
    ).astype(BF)


def out_terms_kernel(own, rebuilt, sum_out):
    sum_out[...] = jnp.zeros_like(sum_out)

    def one(r, carry):
        sum_out[:, : 3 * CH] += nt_dot(
            rebuilt[pl.ds(r + 1, 3)].reshape(3 * CH, WIDE), shifted(own[r].astype(F32), 1)
        )
        return carry

    lax.fori_loop(0, CR, one, 0, unroll=4)


def out_terms(own, rebuilt):
    return pl.pallas_call(
        out_terms_kernel,
        in_specs=[vmem(), vmem()],
        out_specs=vmem(),
        out_shape=jax.ShapeDtypeStruct((3 * CH, 2 * LANES), F32),
        compiler_params=params(),
        cost_estimate=cost(2 * 16 * 192 * 192 * 384, 10 << 20),
        name="out_terms",
    )(own, rebuilt)


def backward_kernel(
    columns,
    rows,
    where_s,
    own,
    above,
    below,
    sides,
    above_sides,
    below_sides,
    wide_in,
    coarse,
    slope_in,
    slope_mid,
    flip_mid,
    flip_out,
    particle_grads,
    sum_out,
    staged,
    wide,
    rebuilt_grad,
    mid_grad,
    first_grad,
    sum_in,
    sum_mid,
):
    gx, gy = where_s[0], where_s[1]
    across = column_mask(gx, columns)
    fill_wide(HALO_OUT, wide, own, above, below, sides, above_sides, below_sides)

    def pooled(g, carry):
        total = None
        for j in range(2):
            value = conv_row(wide, 2 * g + j, flip_out[...], 1).astype(BF)
            rebuilt_grad[2 * g + j] = value
            value = value.astype(F32)
            total = value if j == 0 else total + value
        at = gy * CR + 2 * g - 2
        mask = jnp.where(jnp.logical_and(at >= 0, at < rows * CR), across, 0.0)
        mid_grad[g] = (pair_sum(total) * slope_mid[g] * mask).astype(BF)
        return carry

    lax.fori_loop(0, 10, pooled, 0, unroll=2)

    def fine(g, carry):
        spread = 0.25 * conv_row(mid_grad, g, flip_mid[...], 2)[:, :CC]
        for j in range(2):
            value = rebuilt_grad[2 * g + 2 + j, :, :CC].astype(F32) + spread
            first_grad[2 * g + j] = (value * slope_in[2 * g + 4 + j]).astype(BF)
        return carry

    lax.fori_loop(0, 8, fine, 0, unroll=4)

    sum_in[...] = jnp.zeros_like(sum_in)
    sum_mid[...] = jnp.zeros_like(sum_mid)

    def fine_terms(r, carry):
        sum_in[:, : 3 * CH] += nt_dot(
            wide_in[pl.ds(r + HALO_IN - 1, 3)].reshape(3 * CH, WIDE),
            shifted(first_grad[r].astype(F32), 1),
        )
        return carry

    lax.fori_loop(0, CR, fine_terms, 0, unroll=4)
    even = (lane_index((CH, CC)) & 1) == 0

    def coarse_terms(g, carry):
        value = jnp.where(even, mid_grad[g + 1, :, :CC].astype(F32), 0.0)
        sum_mid[:, : 3 * CH] += nt_dot(
            coarse[pl.ds(g + 1, 3)].reshape(3 * CH, WIDE), shifted(value, 2)
        )
        return carry

    lax.fori_loop(0, 8, coarse_terms, 0, unroll=4)

    rows_each = 3 * CH
    for which, total in enumerate((sum_in, sum_mid, sum_out)):
        for half in range(2):
            start = (2 * which + half) * rows_each
            staged[start : start + rows_each] = total[
                :, half * LANES : (half + 1) * LANES
            ].astype(BF)
    start = 6 * rows_each
    staged[start : start + HID + CH] = particle_grads[...].astype(BF)
    staged[start + HID + CH :] = jnp.zeros((REDUCE_ROWS - start - HID - CH, LANES), BF)


def unet_backward(where, halo, saved, flip_mid, flip_out, particle_grads, sum_out, columns, rows):
    ins = (where, *halo, *saved, flip_mid, flip_out, particle_grads, sum_out)
    return pl.pallas_call(
        functools.partial(backward_kernel, columns, rows),
        in_specs=[smem()] + [vmem()] * (len(ins) - 1),
        out_specs=vmem(),
        out_shape=jax.ShapeDtypeStruct((REDUCE_ROWS, LANES), BF),
        scratch_shapes=[
            pltpu.VMEM((CR + 2 * HALO_OUT, CH, WIDE), BF),
            pltpu.VMEM((20, CH, WIDE), BF),
            pltpu.VMEM((10, CH, WIDE), BF),
            pltpu.VMEM((CR, CH, CC), BF),
            pltpu.VMEM((3 * CH, 2 * LANES), F32),
            pltpu.VMEM((3 * CH, 2 * LANES), F32),
        ],
        compiler_params=params(),
        cost_estimate=cost(2 * 70 * 192 * 192 * 384, 10 << 20),
        name="unet_backward",
    )(*ins)


def split_kernel(sums, grad_in, grad_mid, grad_out, grad_grid, grad_part, grad_pred):
    for which, out in enumerate((grad_in, grad_mid, grad_out)):
        for dr in range(3):
            start = 2 * which * 3 * CH + dr * CH
            low = sums[start : start + CH, :].astype(F32)
            out[3 * dr] = low[:, :CH]
            out[3 * dr + 1] = low[:, CH:]
            out[3 * dr + 2] = sums[start + 3 * CH : start + 4 * CH, :CH].astype(F32)
    start = 18 * CH
    grad_grid[...] = sums[start : start + CH, :].astype(F32)
    grad_part[...] = sums[start + CH : start + 2 * CH, :].astype(F32)
    grad_pred[...] = sums[start + 2 * CH : start + 3 * CH, :].astype(F32)


def split(sums):
    conv = jax.ShapeDtypeStruct((9, CH, CH), F32)
    mlp = jax.ShapeDtypeStruct((CH, HID), F32)
    shapes = [conv, conv, conv, mlp, mlp, mlp]
    return pl.pallas_call(
        split_kernel,
        in_specs=[vmem()],
        out_specs=[vmem()] * 6,
        out_shape=shapes,
        compiler_params=params(),
        cost_estimate=cost(0, 3 << 20),
        name="split",
    )(sums)


def swap(value):
    return lax.all_to_all(value, ("gx", "gy"), split_axis=0, concat_axis=0, tiled=True)


def shards(
    part_feat,
    target,
    block_tile,
    block_patch,
    cell_idx,
    block_fill,
    conv_in,
    conv_mid,
    conv_out,
    mlp_grid,
    mlp_part,
    mlp_out,
):
    nblocks = block_tile.shape[0]
    columns, rows = lax.axis_size("gx"), lax.axis_size("gy")
    devices = columns * rows
    tile = block_tile[:, 0]
    where = jnp.stack([lax.axis_index("gx"), lax.axis_index("gy")]).astype(jnp.int32)
    scale = 1.0 / math.sqrt(nblocks * LANES * devices)
    w_pred = mlp_out.T

    sent = dispatch(tile, block_patch, block_fill, cell_idx, part_feat, devices)
    sent_first, sent_second = dispatch_target(tile, target, devices)
    got = swap(sent)
    prepared = prepare(conv_in, conv_mid, conv_out, mlp_grid, mlp_part, w_pred)
    got, sent_first, sent_second, where, *prepared = lax.optimization_barrier(
        (got, sent_first, sent_second, where, *prepared)
    )
    w_in, w_mid, w_out, f_mid, f_out, w_hidden, w_back = prepared
    got_first = swap(sent_first)

    own, *strips, patch_at = deposit(got)
    halo = (own, *exchange(*strips))
    sent_second, *halo = lax.optimization_barrier((sent_second, *halo))
    got_second = swap(sent_second)
    patches, wide_in, coarse, rebuilt, slope_in, slope_mid = unet_forward(
        where, halo, w_in, w_mid, w_out, columns, rows
    )
    values = gather(patch_at, got, patches)
    got_values = swap(values)
    own, *strips, particle_grads = particles(
        patch_at, got, values, got_first, got_second, w_hidden, w_pred, w_back, mlp_grid, scale
    )
    halo = (own, *exchange(*strips))
    sum_out = out_terms(own, rebuilt)
    saved = (wide_in, coarse, slope_in, slope_mid)
    staged = unet_backward(
        where, halo, saved, f_mid, f_out, particle_grads, sum_out, columns, rows
    )
    staged, got_values = lax.optimization_barrier((staged, got_values))
    terms = swap(staged.reshape(devices, REDUCE_ROWS // devices, LANES))
    mine = jnp.sum(terms.astype(F32), axis=0).astype(BF)
    spread = swap(jnp.broadcast_to(mine[None], (devices, *mine.shape)))
    pred = home_predictions(tile, got_values, part_feat, w_hidden, w_pred, devices)
    *grads, grad_pred = split(spread.reshape(REDUCE_ROWS, LANES))
    return (pred, *grads, grad_pred.T)


def solution(mesh):
    return jax.shard_map(
        shards,
        mesh=mesh,
        in_specs=(
            P(None, ("gx", "gy")),
            P(None, ("gx", "gy")),
            P(("gx", "gy"), None),
            P(("gx", "gy")),
            P(("gx", "gy"), None),
            P(("gx", "gy")),
            P(),
            P(),
            P(),
            P(),
            P(),
            P(),
        ),
        out_specs=(P(None, ("gx", "gy")), P(), P(), P(), P(), P(), P()),
        check_vma=False,
    )
```

time: 721 us -> 272 us (0.38); the launches traced: 710 us -> 271 us
  waiting for transfers between devices: 377 us -> 81.5 us
  matrix products: 133 us -> 0 us
  Pallas kernels: 0 us -> 92.9 us
  local copies, waits for them, and re-layouts: 67.4 us -> 3.73 us
  other arithmetic: 33.8 us -> 0.79 us
  blocking collectives: 0 us -> 21.5 us
  between operations: 15.7 us -> 0.91 us
  starting transfers between devices: 83.7 us -> 69.8 us
    psum x2 -> x0, waiting for transfers between devices: 221 us -> none  [shards(): lax.psum((grad_in, grad_mid, grad_conv, grad_grid, grad_part, grad_out),...]
    pallas_call x0 -> x11, Pallas kernels: none -> 92.9 us  [the longest x1 31 us: particles(): pl.pallas_call(functools.partial(particle_kernel, steps - 1, scale), grid...]
    dot_general x18 -> x0, matrix products: 89 us -> none  [the longest x2 32.7 us: deposit_cells(): jnp.einsum('ksj,sjc->ksc', values, cell_hot, preferred_element_type=jnp.f...]
    all_to_all x4 -> x5, waiting for transfers between devices: 124 us -> 70.9 us  [swap(): lax.all_to_all(value, ('gx', 'gy'), split_axis=0, concat_axis=0, tiled=True)]
    transpose x3 -> x0, matrix products: 31.6 us -> none  [weight_term(): jnp.transpose(result, (2, 3, 0, 1))]
    all_to_all x0 -> x1, blocking collectives: none -> 21.5 us  [swap(): lax.all_to_all(value, ('gx', 'gy'), split_axis=0, concat_axis=0, tiled=True)]
    ppermute x20 -> x12, waiting for transfers between devices: 31.4 us -> 10.6 us  [the longest x6 6.22 us: behind(): return lax.ppermute(value, axis, [(i + 1, i) for i in range(count - 1)])]
    reduce_sum x5 -> x1, other arithmetic: 17.2 us -> 0.14 us  [shards(): mine = jnp.sum(terms.astype(F32), axis=0).astype(BF)]
  transfers between devices with their start and end apart: 26 -> 17, of which waited for: 17 -> 8; matrix products, arithmetic and copies ran while one was open for 13% -> 0% of each run, Pallas kernels for 0% -> 32%
where the time goes in v1:
time: 272 us; the launch traced here: 271 us
  Pallas kernels  92.9 us (34%)
  waiting for transfers between devices  81.5 us (30%)
  starting transfers between devices  69.8 us (26%)
  blocking collectives  21.5 us (8%)
  local copies, waits for them, and re-layouts  3.73 us (1%)
    all_to_all x5, waiting for transfers between devices, swap(): lax.all_to_all(value, ('gx', 'gy'), split_axis=0, concat_axis=0, tiled=True)  70.9 us
    all_to_all x5, starting transfers between devices, swap(): lax.all_to_all(value, ('gx', 'gy'), split_axis=0, concat_axis=0, tiled=True)  36.9 us
    pallas_call x1, Pallas kernels, particles(): pl.pallas_call(functools.partial(particle_kernel, steps - 1, scale), grid...  31 us
    all_to_all x1, blocking collectives, swap(): lax.all_to_all(value, ('gx', 'gy'), split_axis=0, concat_axis=0, tiled=True)  21.5 us
    ppermute x6, starting transfers between devices, ahead(): return lax.ppermute(value, axis, [(i, i + 1) for i in range(count - 1)])  21.1 us
    pallas_call x1, Pallas kernels, unet_forward(): pl.pallas_call(functools.partial(forward_kernel, columns, rows), in_specs...  12 us
    ppermute x6, starting transfers between devices, behind(): return lax.ppermute(value, axis, [(i + 1, i) for i in range(count - 1)])  11.9 us
    pallas_call x1, Pallas kernels, unet_backward(): pl.pallas_call(functools.partial(backward_kernel, columns, rows), in_spec...  10.6 us
  transfers between devices with their start and end apart: 17, of which 8 were waited for; matrix products, arithmetic and copies ran while one was open for 0% of the time, Pallas kernels for 32%

profile of v1, /device:TPU:1, one launch (start us, length us, event | category | flops | bytes accessed | tf_op | source)
XLA Modules:
  0.0 271.2 jit_solution(2197012404889921712)
XLA Ops:
  0.6 5.1 %dispatch.1 = bf16[128,144,128]{2,1,0:T(8,128)(2,1)} custom-call(s32[64]{0:T(128)} %bitcast.12, s32[64]{0:T(128)} %patch_s.1, s32[64]{0:T(128)} %fill_s.1, s32[64,128]{1,0:T(8,128)} %cell_ref.1, bf16[64,8192]{1,0:T(8,128)(2,1)} %feat_ref.5), custom_call_target="tpu_custom_call" | custom-call | bytes 6291456 | tf_op jit(solution)/shard_map/dispatch/pallas_call | solution.py:134
  5.7 11.9 %all-to-all-start = ((bf16[128,144,128]{2,1,0:T(8,128)(2,1)}), bf16[128,144,128]{2,1,0:T(8,128)(2,1)}, u32[]{:S(2)}, u32[]{:S(2)}) async-start(bf16[128,144,128]{2,1,0:T(8,128)(2,1)} %dispatch.1), calls=%async_computation | async-start | bytes 9437184 | tf_op jit(solution)/shard_map/all_to_all | solution.py:841
  17.7 4.8 %dispatch_target.1 = (bf16[128,64,128]{2,1,0:T(8,128)(2,1)}, bf16[128,64,128]{2,1,0:T(8,128)(2,1)}) custom-call(s32[64]{0:T(128)} %bitcast.13, bf16[64,8192]{1,0:T(8,128)(2,1)} %feat_ref.4), custom_call_target="tpu_custom_call" | custom-call | bytes 6291456 | tf_op jit(solution)/shard_map/dispatch_target/pallas_call | solution.py:170
  25.2 50.9 %all-to-all-done.got_ref.meta_ref = bf16[128,144,128]{2,1,0:T(8,128)(2,1)} async-done(((bf16[128,144,128]{2,1,0:T(8,128)(2,1)}), bf16[128,144,128]{2,1,0:T(8,128)(2,1)}, u32[]{:S(2)}, u32[]{:S(2)}) %all-to-all-start) | async-done | bytes 4718624 | tf_op jit(solution)/shard_map/all_to_all | solution.py:841
  76.1 4.3 %all-to-all-start.1 = ((bf16[128,64,128]{2,1,0:T(8,128)(2,1)}), bf16[128,64,128]{2,1,0:T(8,128)(2,1)S(1)}, u32[]{:S(2)}, u32[]{:S(2)}) async-start(bf16[128,64,128]{2,1,0:T(8,128)(2,1)} %get-tuple-element.88), calls=%async_computation.1 | async-start | bytes 4194304 | tf_op jit(solution)/shard_map/all_to_all | solution.py:841
  80.4 9.7 %deposit.1 = (bf16[16,64,256]{2,1,0:T(8,128)(2,1)}, bf16[10,64,128]{2,1,0:T(8,128)(2,1)}, bf16[10,64,128]{2,1,0:T(8,128)(2,1)}, bf16[1,64,128]{2,1,0:T(8,128)(2,...) custom-call(bf16[128,144,128]{2,1,0:T(8,128)(2,1)} %all-to-all-done.got_ref.meta_ref), custom_call_target="tpu_custom_call" | custom-call | flops 671088640 | bytes 6291456 | tf_op jit(solution)/shard_map/deposit/pallas_call | solution.py:417
  90.1 3.3 %collective-permute-start.2 = (bf16[1,64,128]{2,1,0:T(8,128)(2,1)}, bf16[1,64,128]{2,1,0:T(8,128)(2,1)S(1)}, u32[]{:S(2)}, u32[]{:S(2)}) collective-permute-start(bf16[1,64,128]{2,1,0:T(8,128)(2,1)} %get-tuple-element.76), channel_id=1, source_target_pairs={{0,8},{8,16},{16,24},{24,32},{32,40},{40,48},{48,56},{56,64},{64,7... | collective-permute-start | bytes 49160 | tf_op jit(solution)/shard_map/ppermute | solution.py:309
  94.7 3.7 %collective-permute-start = (bf16[10,64,128]{2,1,0:T(8,128)(2,1)}, bf16[10,64,128]{2,1,0:T(8,128)(2,1)S(1)}, u32[]{:S(2)}, u32[]{:S(2)}) collective-permute-start(bf16[10,64,128]{2,1,0:T(8,128)(2,1)} %get-tuple-element.74), channel_id=1, source_target_pairs={{0,1},{1,2},{2,3},{3,4},{4,5},{5,6},{6,7},{8,9},{9,10},{10,11},{11... | collective-permute-start | bytes 491528 | tf_op jit(solution)/shard_map/ppermute | solution.py:309
  113.1 10.7 %all-to-all-start.2 = ((bf16[128,64,128]{2,1,0:T(8,128)(2,1)}), bf16[128,64,128]{2,1,0:T(8,128)(2,1)}, u32[]{:S(2)}, u32[]{:S(2)}) async-start(bf16[128,64,128]{2,1,0:T(8,128)(2,1)} %get-tuple-element.89), calls=%async_computation.2 | async-start | bytes 4194304 | tf_op jit(solution)/shard_map/all_to_all | solution.py:841
  123.8 12.0 %unet_forward.1 = (bf16[32,64,128]{2,1,0:T(8,128)(2,1)}, bf16[26,64,384]{2,1,0:T(8,128)(2,1)}, bf16[12,64,384]{2,1,0:T(8,128)(2,1)}, bf16[20,64,384]{2,1,0:T(8,1...) custom-call(s32[2]{0:T(128)} %pad_add_fusion.where_s, bf16[16,64,256]{2,1,0:T(8,128)(2,1)} %get-tuple-element.78.own, ...), custom_call_target="tpu_custom_call" | custom-call | flops 1415577600 | bytes 10485760 | tf_op jit(solution)/shard_map/unet_forward/pallas_call | solution.py:511
  135.8 5.6 %gather.1.value_ref = bf16[128,128,128]{2,1,0:T(8,128)(2,1)} custom-call(s32[256]{0:T(256)} %get-tuple-element.71.patch_s, bf16[128,144,128]{2,1,0:T(8,128)(2,1)} %all-to-all-done.got_ref.meta_ref, bf16[32,64,128]{2,1,0:T(8,128)(2,1)} %get-tuple-element.87.patches), custom_call_target="tpu_custom_call" | custom-call | flops 536870912 | bytes 6291456 | tf_op jit(solution)/shard_map/gather/pallas_call | solution.py:541
  141.3 12.6 %all-to-all-done.2.second_ref = bf16[128,64,128]{2,1,0:T(8,128)(2,1)} async-done(((bf16[128,64,128]{2,1,0:T(8,128)(2,1)}), bf16[128,64,128]{2,1,0:T(8,128)(2,1)}, u32[]{:S(2)}, u32[]{:S(2)}) %all-to-all-start.2) | async-done | bytes 2097184 | tf_op jit(solution)/shard_map/all_to_all | solution.py:841
  153.9 5.5 %all-to-all-start.3 = ((bf16[128,128,128]{2,1,0:T(8,128)(2,1)}), bf16[128,128,128]{2,1,0:T(8,128)(2,1)}, u32[]{:S(2)}, u32[]{:S(2)}) async-start(bf16[128,128,128]{2,1,0:T(8,128)(2,1)} %gather.1.value_ref), calls=%async_computation.3 | async-start | bytes 8388608 | tf_op jit(solution)/shard_map/all_to_all | solution.py:841
  159.4 31.0 %particles.1 = (bf16[16,64,256]{2,1,0:T(8,128)(2,1)}, bf16[6,64,128]{2,1,0:T(8,128)(2,1)}, bf16[6,64,128]{2,1,0:T(8,128)(2,1)}, bf16[1,64,128]{2,1,0:T(8,128)(2,...) custom-call(s32[256]{0:T(256)} %get-tuple-element.71.patch_s, bf16[128,144,128]{2,1,0:T(8,128)(2,1)} %all-to-all-done.got_ref.meta_ref, ...), custom_call_target="tpu_custom_call" | custom-call | flops 5872025600 | bytes 16777216 | tf_op jit(solution)/shard_map/particles/pallas_call | solution.py:645
  190.4 3.3 %collective-permute-start.8 = (bf16[1,64,128]{2,1,0:T(8,128)(2,1)}, bf16[1,64,128]{2,1,0:T(8,128)(2,1)S(1)}, u32[]{:S(2)}, u32[]{:S(2)}) collective-permute-start(bf16[1,64,128]{2,1,0:T(8,128)(2,1)} %get-tuple-element.95), channel_id=1, source_target_pairs={{0,8},{8,16},{16,24},{24,32},{32,40},{40,48},{48,56},{56,64},{64,7... | collective-permute-start | bytes 49160 | tf_op jit(solution)/shard_map/ppermute | solution.py:309
  195.0 3.7 %collective-permute-start.6 = (bf16[6,64,128]{2,1,0:T(8,128)(2,1)}, bf16[6,64,128]{2,1,0:T(8,128)(2,1)S(1)}, u32[]{:S(2)}, u32[]{:S(2)}) collective-permute-start(bf16[6,64,128]{2,1,0:T(8,128)(2,1)} %get-tuple-element.93), channel_id=1, source_target_pairs={{0,1},{1,2},{2,3},{3,4},{4,5},{5,6},{6,7},{8,9},{9,10},{10,11},{11... | collective-permute-start | bytes 294920 | tf_op jit(solution)/shard_map/ppermute | solution.py:309
  202.6 3.3 %collective-permute-done.9 = bf16[1,64,128]{2,1,0:T(8,128)(2,1)S(1)} collective-permute-done((bf16[1,64,128]{2,1,0:T(8,128)(2,1)}, bf16[1,64,128]{2,1,0:T(8,128)(2,1)S(1)}, u32[]{:S(2)}, u32[]{:S(2)}) %collective-permute-start.9) | collective-permute-done | bytes 16416 | tf_op jit(solution)/shard_map/ppermute | solution.py:313
  208.5 4.0 %collective-permute-start.10 = (bf16[2,64,128]{2,1,0:T(8,128)(2,1)S(1)}, bf16[2,64,128]{2,1,0:T(8,128)(2,1)S(1)}, u32[]{:S(2)}, u32[]{:S(2)}) collective-permute-start(bf16[2,64,128]{2,1,0:T(8,128)(2,1)S(1)} %constant_dynamic-update-slice_fusion.2.sides), channel_id=1, source_target_pairs={{0,1},{1,2},{2,3},{3,4},{4,5},{5,6},{6,7},{8,9},{9,10},{10,11},{11... | collective-permute-start | bytes 98312 | tf_op jit(solution)/shard_map/ppermute | solution.py:309
  212.5 4.0 %out_terms.1.sum_out = f32[192,256]{1,0:T(8,128)} custom-call(bf16[16,64,256]{2,1,0:T(8,128)(2,1)} %get-tuple-element.92.own, bf16[20,64,384]{2,1,0:T(8,128)(2,1)} %get-tuple-element.104.rebuilt), custom_call_target="tpu_custom_call" | custom-call | flops 452984832 | bytes 10485760 | tf_op jit(solution)/shard_map/out_terms/pallas_call | solution.py:692
  217.2 10.6 %unet_backward.1 = bf16[2048,128]{1,0:T(8,128)(2,1)} custom-call(s32[2]{0:T(128)} %pad_add_fusion.where_s, bf16[16,64,256]{2,1,0:T(8,128)(2,1)} %get-tuple-element.92.own, bf16[6,64,128]{2,1,0:T(8,128)(2,1)} %copy-done.6, bf16[6,64,128]{2,1,0:T(8,128)(2,1)} %copy-done.7, bf16[2,64,128]{2,1,0:T(8,128)(2,1)} %copy-done.3, bf16[2,64,128]{2,1,0:T(8,128)(2,1)} %copy-done.11, ...), custom_call_target="tpu_custom_call" | custom-call | flops 1981808640 | bytes 10485760 | tf_op jit(solution)/shard_map/unet_backward/pallas_call | solution.py:792
  227.8 21.5 %all_to_all.30 = bf16[128,16,128]{2,1,0:T(8,128)(2,1)S(1)} all-to-all(bf16[128,16,128]{2,1,0:T(8,128)(2,1)} %bitcast.8), channel_id=1, replica_groups=mesh['gx'=16,'gy'=8] {'gx','gy'}, dimensions={0} | all-to-all | bytes 1048576 | tf_op jit(solution)/shard_map/all_to_all | solution.py:841
  250.3 4.6 %all-to-all-start.5 = ((bf16[128,16,128]{2,1,0:T(8,128)(2,1)}), bf16[128,16,128]{2,1,0:T(8,128)(2,1)S(1)}, u32[]{:S(2)}, u32[]{:S(2)}) async-start(bf16[128,16,128]{2,1,0:T(8,128)(2,1)} %broadcast_in_dim.2), calls=%async_computation.5 | async-start | bytes 1048576 | tf_op jit(solution)/shard_map/all_to_all | solution.py:841
  254.8 6.1 %home_predictions.1 = bf16[64,8192]{1,0:T(8,128)(2,1)} custom-call(s32[64]{0:T(128)} %bitcast.14, bf16[128,128,128]{2,1,0:T(8,128)(2,1)} %all-to-all-done.3.got_ref, bf16[64,8192]{1,0:T(8,128)(2,1)} %feat_ref.5, bf16[128,128]{1,0:T(8,128)(2,1)} %get-tuple-element.90.w_hidden, bf16[64,128]{1,0:T(8,128)(2,1)} %bitcast.11), custom_call_target="tpu_custom_call" | custom-call | flops 402653184 | bytes 8388608 | tf_op jit(solution)/shard_map/home_predictions/pallas_call | solution.py:209
  261.0 7.4 %all-to-all-done.5 = bf16[128,16,128]{2,1,0:T(8,128)(2,1)S(1)} async-done(((bf16[128,16,128]{2,1,0:T(8,128)(2,1)}), bf16[128,16,128]{2,1,0:T(8,128)(2,1)S(1)}, u32[]{:S(2)}, u32[]{:S(2)}) %all-to-all-start.5) | async-done | bytes 524320 | tf_op jit(solution)/shard_map/all_to_all | solution.py:841
  (53 shorter events, 31.0 us)
Async XLA Ops:
  5.7 70.4 %all-to-all-start = ((bf16[128,144,128]{2,1,0:T(8,128)(2,1)}), bf16[128,144,128]{2,1,0:T(8,128)(2,1)}, u32[]{:S(2)}, u32[]{:S(2)}) async-start(bf16[128,144,128]{2,1,0:T(8,128)(2,1)} %dispatch.1), calls=%async_computation | async-start | bytes 9437184 | tf_op jit(solution)/shard_map/all_to_all | solution.py:841
  76.1 35.5 %all-to-all-start.1 = ((bf16[128,64,128]{2,1,0:T(8,128)(2,1)}), bf16[128,64,128]{2,1,0:T(8,128)(2,1)S(1)}, u32[]{:S(2)}, u32[]{:S(2)}) async-start(bf16[128,64,128]{2,1,0:T(8,128)(2,1)} %get-tuple-element.88), calls=%async_computation.1 | async-start | bytes 4194304 | tf_op jit(solution)/shard_map/all_to_all | solution.py:841
  90.1 11.7 %collective-permute-start.2 = (bf16[1,64,128]{2,1,0:T(8,128)(2,1)}, bf16[1,64,128]{2,1,0:T(8,128)(2,1)S(1)}, u32[]{:S(2)}, u32[]{:S(2)}) collective-permute-start(bf16[1,64,128]{2,1,0:T(8,128)(2,1)} %get-tuple-element.76), channel_id=1, source_target_pairs={{0,8},{8,16},{16,24},{24,32},{32,40},{40,48},{48,56},{56,64},{64,7... | collective-permute-start | bytes 49160 | tf_op jit(solution)/shard_map/ppermute | solution.py:309
  93.4 11.3 %collective-permute-start.3 = (bf16[1,64,128]{2,1,0:T(8,128)(2,1)}, bf16[1,64,128]{2,1,0:T(8,128)(2,1)S(1)}, u32[]{:S(2)}, u32[]{:S(2)}) collective-permute-start(bf16[1,64,128]{2,1,0:T(8,128)(2,1)} %get-tuple-element.77), channel_id=1, source_target_pairs={{8,0},{16,8},{24,16},{32,24},{40,32},{48,40},{56,48},{64,56},{72,6... | collective-permute-start | bytes 49160 | tf_op jit(solution)/shard_map/ppermute | solution.py:313
  94.7 16.9 %collective-permute-start = (bf16[10,64,128]{2,1,0:T(8,128)(2,1)}, bf16[10,64,128]{2,1,0:T(8,128)(2,1)S(1)}, u32[]{:S(2)}, u32[]{:S(2)}) collective-permute-start(bf16[10,64,128]{2,1,0:T(8,128)(2,1)} %get-tuple-element.74), channel_id=1, source_target_pairs={{0,1},{1,2},{2,3},{3,4},{4,5},{5,6},{6,7},{8,9},{9,10},{10,11},{11... | collective-permute-start | bytes 491528 | tf_op jit(solution)/shard_map/ppermute | solution.py:309
  98.4 13.2 %collective-permute-start.1 = (bf16[10,64,128]{2,1,0:T(8,128)(2,1)}, bf16[10,64,128]{2,1,0:T(8,128)(2,1)S(1)}, u32[]{:S(2)}, u32[]{:S(2)}) collective-permute-start(bf16[10,64,128]{2,1,0:T(8,128)(2,1)} %get-tuple-element.75), channel_id=1, source_target_pairs={{1,0},{2,1},{3,2},{4,3},{5,4},{6,5},{7,6},{9,8},{10,9},{11,10},{12... | collective-permute-start | bytes 491528 | tf_op jit(solution)/shard_map/ppermute | solution.py:313
  104.8 6.9 %copy-start.2 = (bf16[2,64,128]{2,1,0:T(8,128)(2,1)}, bf16[2,64,128]{2,1,0:T(8,128)(2,1)S(1)}, u32[]{:S(2)}) copy-start(bf16[2,64,128]{2,1,0:T(8,128)(2,1)S(1)} %constant_dynamic-update-slice_fusion.sides) | copy-start | bytes 98308
  104.8 5.8 %collective-permute-start.5 = (bf16[2,64,128]{2,1,0:T(8,128)(2,1)S(1)}, bf16[2,64,128]{2,1,0:T(8,128)(2,1)S(1)}, u32[]{:S(2)}, u32[]{:S(2)}) collective-permute-start(bf16[2,64,128]{2,1,0:T(8,128)(2,1)S(1)} %constant_dynamic-update-slice_fusion.sides), channel_id=1, source_target_pairs={{1,0},{2,1},{3,2},{4,3},{5,4},{6,5},{7,6},{9,8},{10,9},{11,10},{12... | collective-permute-start | bytes 98312 | tf_op jit(solution)/shard_map/ppermute | solution.py:313
  107.5 4.1 %collective-permute-start.4 = (bf16[2,64,128]{2,1,0:T(8,128)(2,1)S(1)}, bf16[2,64,128]{2,1,0:T(8,128)(2,1)S(1)}, u32[]{:S(2)}, u32[]{:S(2)}) collective-permute-start(bf16[2,64,128]{2,1,0:T(8,128)(2,1)S(1)} %constant_dynamic-update-slice_fusion.sides), channel_id=1, source_target_pairs={{0,1},{1,2},{2,3},{3,4},{4,5},{5,6},{6,7},{8,9},{9,10},{10,11},{11... | collective-permute-start | bytes 98312 | tf_op jit(solution)/shard_map/ppermute | solution.py:309
  110.6 1.1 copy-start.8
  111.6 0.7 copy-start.4
  111.6 0.7 copy-start.5
  111.6 1.4 copy-start
  113.1 40.9 %all-to-all-start.2 = ((bf16[128,64,128]{2,1,0:T(8,128)(2,1)}), bf16[128,64,128]{2,1,0:T(8,128)(2,1)}, u32[]{:S(2)}, u32[]{:S(2)}) async-start(bf16[128,64,128]{2,1,0:T(8,128)(2,1)} %get-tuple-element.89), calls=%async_computation.2 | async-start | bytes 4194304 | tf_op jit(solution)/shard_map/all_to_all | solution.py:841
  153.9 73.9 %all-to-all-start.3 = ((bf16[128,128,128]{2,1,0:T(8,128)(2,1)}), bf16[128,128,128]{2,1,0:T(8,128)(2,1)}, u32[]{:S(2)}, u32[]{:S(2)}) async-start(bf16[128,128,128]{2,1,0:T(8,128)(2,1)} %gather.1.value_ref), calls=%async_computation.3 | async-start | bytes 8388608 | tf_op jit(solution)/shard_map/all_to_all | solution.py:841
  190.4 12.2 %collective-permute-start.8 = (bf16[1,64,128]{2,1,0:T(8,128)(2,1)}, bf16[1,64,128]{2,1,0:T(8,128)(2,1)S(1)}, u32[]{:S(2)}, u32[]{:S(2)}) collective-permute-start(bf16[1,64,128]{2,1,0:T(8,128)(2,1)} %get-tuple-element.95), channel_id=1, source_target_pairs={{0,8},{8,16},{16,24},{24,32},{32,40},{40,48},{48,56},{56,64},{64,7... | collective-permute-start | bytes 49160 | tf_op jit(solution)/shard_map/ppermute | solution.py:309
  193.7 12.2 %collective-permute-start.9 = (bf16[1,64,128]{2,1,0:T(8,128)(2,1)}, bf16[1,64,128]{2,1,0:T(8,128)(2,1)S(1)}, u32[]{:S(2)}, u32[]{:S(2)}) collective-permute-start(bf16[1,64,128]{2,1,0:T(8,128)(2,1)} %get-tuple-element.96), channel_id=1, source_target_pairs={{8,0},{16,8},{24,16},{32,24},{40,32},{48,40},{56,48},{64,56},{72,6... | collective-permute-start | bytes 49160 | tf_op jit(solution)/shard_map/ppermute | solution.py:313
  195.0 21.6 %collective-permute-start.6 = (bf16[6,64,128]{2,1,0:T(8,128)(2,1)}, bf16[6,64,128]{2,1,0:T(8,128)(2,1)S(1)}, u32[]{:S(2)}, u32[]{:S(2)}) collective-permute-start(bf16[6,64,128]{2,1,0:T(8,128)(2,1)} %get-tuple-element.93), channel_id=1, source_target_pairs={{0,1},{1,2},{2,3},{3,4},{4,5},{5,6},{6,7},{8,9},{9,10},{10,11},{11... | collective-permute-start | bytes 294920 | tf_op jit(solution)/shard_map/ppermute | solution.py:309
  198.7 17.9 %collective-permute-start.7 = (bf16[6,64,128]{2,1,0:T(8,128)(2,1)}, bf16[6,64,128]{2,1,0:T(8,128)(2,1)S(1)}, u32[]{:S(2)}, u32[]{:S(2)}) collective-permute-start(bf16[6,64,128]{2,1,0:T(8,128)(2,1)} %get-tuple-element.94), channel_id=1, source_target_pairs={{1,0},{2,1},{3,2},{4,3},{5,4},{6,5},{7,6},{9,8},{10,9},{11,10},{12... | collective-permute-start | bytes 294920 | tf_op jit(solution)/shard_map/ppermute | solution.py:313
  205.8 10.8 %copy-start.3 = (bf16[2,64,128]{2,1,0:T(8,128)(2,1)}, bf16[2,64,128]{2,1,0:T(8,128)(2,1)S(1)}, u32[]{:S(2)}) copy-start(bf16[2,64,128]{2,1,0:T(8,128)(2,1)S(1)} %constant_dynamic-update-slice_fusion.2.sides) | copy-start | bytes 98308
  205.8 10.7 %collective-permute-start.11 = (bf16[2,64,128]{2,1,0:T(8,128)(2,1)S(1)}, bf16[2,64,128]{2,1,0:T(8,128)(2,1)S(1)}, u32[]{:S(2)}, u32[]{:S(2)}) collective-permute-start(bf16[2,64,128]{2,1,0:T(8,128)(2,1)S(1)} %constant_dynamic-update-slice_fusion.2.sides), channel_id=1, source_target_pairs={{1,0},{2,1},{3,2},{4,3},{5,4},{6,5},{7,6},{9,8},{10,9},{11,10},{12... | collective-permute-start | bytes 98312 | tf_op jit(solution)/shard_map/ppermute | solution.py:313
  208.5 8.0 %collective-permute-start.10 = (bf16[2,64,128]{2,1,0:T(8,128)(2,1)S(1)}, bf16[2,64,128]{2,1,0:T(8,128)(2,1)S(1)}, u32[]{:S(2)}, u32[]{:S(2)}) collective-permute-start(bf16[2,64,128]{2,1,0:T(8,128)(2,1)S(1)} %constant_dynamic-update-slice_fusion.2.sides), channel_id=1, source_target_pairs={{0,1},{1,2},{2,3},{3,4},{4,5},{5,6},{6,7},{8,9},{9,10},{10,11},{11... | collective-permute-start | bytes 98312 | tf_op jit(solution)/shard_map/ppermute | solution.py:309
  250.3 18.1 %all-to-all-start.5 = ((bf16[128,16,128]{2,1,0:T(8,128)(2,1)}), bf16[128,16,128]{2,1,0:T(8,128)(2,1)S(1)}, u32[]{:S(2)}, u32[]{:S(2)}) async-start(bf16[128,16,128]{2,1,0:T(8,128)(2,1)} %broadcast_in_dim.2), calls=%async_computation.5 | async-start | bytes 1048576 | tf_op jit(solution)/shard_map/all_to_all | solution.py:841
  268.4 0.8 copy-start.1
  (5 other events, 3.1 us)

commit v2 on v1

--- a/solution.py
+++ b/solution.py
@@ -15,7 +15,7 @@
 LANES = 128
 WIDE = 384
 NPATCH = 32
-META = 16
+META = 8
 SLOT_ROWS = 2 * CH + META
 HALO_IN = 5
 HALO_OUT = 3
@@ -66,6 +66,18 @@
     return result, half + (result - result * half) * bend
 
 
+def gelu_slope(half, result, square):
+    bend = 2.0 * root_two_pi + (6.0 * cubic_coef * root_two_pi) * square
+    return half + (result - result * half) * bend
+
+
+def gelu_parts(value):
+    square = value * value
+    inner = jnp.tanh(value * (root_two_pi + (root_two_pi * cubic_coef) * square))
+    half = 0.5 + 0.5 * inner
+    return value * half, half, square
+
+
 def gelu_value(value):
     inner = jnp.tanh(value * (root_two_pi + (root_two_pi * cubic_coef) * (value * value)))
     return value * (0.5 + 0.5 * inner)
@@ -75,7 +87,14 @@
     return lax.broadcasted_iota(jnp.int32, shape, len(shape) - 1)
 
 
-def place_blocks(tile_s, slot_s, count_s, blocks, devices):
+def peer_of(tile, grid):
+    columns, rows = grid
+    return lax.rem(tile, rows) * columns + lax.div(tile, rows)
+
+
+def place_blocks(tile_s, slot_s, count_s, blocks, grid):
+    devices = grid[0] * grid[1]
+
     def clear(i, carry):
         count_s[i] = 0
         slot_s[2 * i] = -1
@@ -83,7 +102,7 @@
         return carry
 
     def place(b, carry):
-        owner = tile_s[b]
+        owner = peer_of(tile_s[b], grid)
         rank = count_s[owner]
         slot_s[2 * owner + rank] = b
         count_s[owner] = rank + 1
@@ -97,12 +116,12 @@
     return pl.ds(pl.multiple_of(b * LANES, LANES), LANES)
 
 
-def dispatch_kernel(blocks, devices, per, tile_s, patch_s, fill_s, cell_ref, feat_ref, out_ref, slot_s, count_s):
+def dispatch_kernel(blocks, grid, per, tile_s, patch_s, fill_s, cell_ref, feat_ref, out_ref, slot_s, count_s):
     step = pl.program_id(0)
 
     @pl.when(step == 0)
     def _():
-        place_blocks(tile_s, slot_s, count_s, blocks, devices)
+        place_blocks(tile_s, slot_s, count_s, blocks, grid)
 
     def one(i, carry):
         owner = step * per + i
@@ -127,12 +146,13 @@
     return [pltpu.SMEM((2 * devices,), jnp.int32), pltpu.SMEM((devices,), jnp.int32)]
 
 
-def dispatch(tile, patch, fill, cells, features, devices):
+def dispatch(tile, patch, fill, cells, features, grid):
+    devices = grid[0] * grid[1]
     blocks = tile.shape[0]
-    steps = 4
+    steps = 2
     per = devices // steps
     return pl.pallas_call(
-        functools.partial(dispatch_kernel, blocks, devices, per),
+        functools.partial(dispatch_kernel, blocks, grid, per),
         grid=(steps,),
         in_specs=[smem(), smem(), smem(), whole(cells.shape), whole(features.shape)],
         out_specs=pl.BlockSpec((per, SLOT_ROWS, LANES), lambda i: (i, 0, 0)),
@@ -144,35 +164,34 @@
     )(tile, patch, fill, cells, features)
 
 
-def dispatch_target_kernel(blocks, devices, per, tile_s, feat_ref, first_ref, second_ref, slot_s, count_s):
+def dispatch_target_kernel(blocks, grid, per, tile_s, feat_ref, out_ref, slot_s, count_s):
     step = pl.program_id(0)
 
     @pl.when(step == 0)
     def _():
-        place_blocks(tile_s, slot_s, count_s, blocks, devices)
+        place_blocks(tile_s, slot_s, count_s, blocks, grid)
 
     def one(i, carry):
         owner = step * per + i
-        for r, out_ref in enumerate((first_ref, second_ref)):
+        for r in range(2):
             at = jnp.maximum(slot_s[2 * owner + r], 0)
-            out_ref[i] = feat_ref[:, block_lanes(at)]
+            out_ref[i, r * CH : (r + 1) * CH, :] = feat_ref[:, block_lanes(at)]
         return carry
 
     lax.fori_loop(0, per, one, 0, unroll=16)
 
 
-def dispatch_target(tile, features, devices):
+def dispatch_target(tile, features, grid):
+    devices = grid[0] * grid[1]
     blocks = tile.shape[0]
     steps = 4
     per = devices // steps
-    shape = jax.ShapeDtypeStruct((devices, CH, LANES), BF)
-    spec = pl.BlockSpec((per, CH, LANES), lambda i: (i, 0, 0))
-    return pl.pallas_call(
-        functools.partial(dispatch_target_kernel, blocks, devices, per),
+    return pl.pallas_call(
+        functools.partial(dispatch_target_kernel, blocks, grid, per),
         grid=(steps,),
         in_specs=[smem(), whole(features.shape)],
-        out_specs=[spec, spec],
-        out_shape=[shape, shape],
+        out_specs=pl.BlockSpec((per, 2 * CH, LANES), lambda i: (i, 0, 0)),
+        out_shape=jax.ShapeDtypeStruct((devices, 2 * CH, LANES), BF),
         scratch_shapes=route_scratch(devices),
         compiler_params=params(),
         cost_estimate=cost(0, 6 << 20),
@@ -180,22 +199,24 @@
     )(tile, features)
 
 
-def home_kernel(blocks, devices, tile_s, got_ref, feat_ref, w_hidden, w_pred, out_ref, pair, count_s):
+def home_kernel(blocks, grid, tile_s, fill_s, cell_ref, got_ref, feat_ref, w_hidden, w_pred, out_ref, pair, count_s):
     def clear(i, carry):
         count_s[i] = 0
         return carry
 
-    lax.fori_loop(0, devices, clear, 0, unroll=16)
+    lax.fori_loop(0, grid[0] * grid[1], clear, 0, unroll=16)
 
     def one(b, carry):
-        owner = tile_s[b]
+        owner = peer_of(tile_s[b], grid)
         rank = count_s[owner]
         count_s[owner] = rank + 1
         rows = pl.ds(pl.multiple_of(rank * CH, CH), CH)
-        pair[:CH, block_lanes(b)] = got_ref[owner, rows, :]
-        return carry
-
-    lax.fori_loop(0, blocks, one, 0, unroll=8)
+        code = jnp.where(lane_index((1, LANES)) < fill_s[b], cell_ref[pl.ds(b, 1), :], -1)
+        values = dot(got_ref[owner, rows, :], one_hot(code.astype(F32)))
+        pair[:CH, block_lanes(b)] = values.astype(BF)
+        return carry
+
+    lax.fori_loop(0, blocks, one, 0, unroll=16)
     pair[CH:, :] = feat_ref[...]
     span = 2048
     for start in range(0, blocks * LANES, span):
@@ -204,11 +225,12 @@
         out_ref[:, lanes] = dot(w_pred[...], value).astype(BF)
 
 
-def home_predictions(tile, got, features, w_hidden, w_pred, devices):
+def home_predictions(tile, fill, cells, got, features, w_hidden, w_pred, grid):
+    devices = grid[0] * grid[1]
     blocks = tile.shape[0]
     return pl.pallas_call(
-        functools.partial(home_kernel, blocks, devices),
-        in_specs=[smem()] + [vmem()] * 4,
+        functools.partial(home_kernel, blocks, grid),
+        in_specs=[smem(), smem()] + [vmem()] * 5,
         out_specs=vmem(),
         out_shape=jax.ShapeDtypeStruct((CH, blocks * LANES), BF),
         scratch_shapes=[
@@ -218,7 +240,7 @@
         compiler_params=params(),
         cost_estimate=cost(2 * 8192 * 128 * 192, 8 << 20, 8192 * 128),
         name="home_predictions",
-    )(tile, got, features, w_hidden, w_pred)
+    )(tile, fill, cells, got, features, w_hidden, w_pred)
 
 
 def prepare_kernel(conv_in, conv_mid, conv_out, mlp_grid, mlp_part, mlp_out_t, w_in, w_mid, w_out, f_mid, f_out, w_hidden, w_back):
@@ -303,21 +325,23 @@
     ]
 
 
-def exchange(head, tail, left, right):
-    def ahead(value, axis):
-        count = lax.axis_size(axis)
-        return lax.ppermute(value, axis, [(i, i + 1) for i in range(count - 1)])
-
-    def behind(value, axis):
-        count = lax.axis_size(axis)
-        return lax.ppermute(value, axis, [(i + 1, i) for i in range(count - 1)])
-
-    from_left = ahead(right, "gx")
-    from_right = behind(left, "gx")
-    above = ahead(tail, "gy")
-    below = behind(head, "gy")
+def ahead(value, axis):
+    count = lax.axis_size(axis)
+    return lax.ppermute(value, axis, [(i, i + 1) for i in range(count - 1)])
+
+
+def behind(value, axis):
+    count = lax.axis_size(axis)
+    return lax.ppermute(value, axis, [(i + 1, i) for i in range(count - 1)])
+
+
+def exchange(head, tail, left, right, beside=None):
+    from_left, from_right = ahead(right, "gx"), behind(left, "gx")
+    above, below = ahead(tail, "gy"), behind(head, "gy")
+    if beside is not None:
+        from_left, from_right, beside = lax.optimization_barrier((from_left, from_right, beside))
     sides = jnp.concatenate([from_left, from_right], axis=0)
-    return above, below, sides, ahead(sides, "gy"), behind(sides, "gy")
+    return (above, below, sides, ahead(sides, "gy"), behind(sides, "gy")), beside
 
 
 def side_lanes(left, right, r):
@@ -329,8 +353,8 @@
     return jnp.where(lane < 8, right, jnp.where(lane >= 120, left, 0.0)).astype(BF)
 
 
-def fill_wide(width, wide, own_ref, above_ref, below_ref, sides_ref, above_sides, below_sides):
-    left, right = sides_ref[0].astype(F32), sides_ref[1].astype(F32)
+def fill_wide(width, wide, own_ref, above_ref, below_ref, sides, above_sides, below_sides):
+    left, right = sides[0].astype(F32), sides[1].astype(F32)
     for r in range(CR):
         wide[width + r, :, :CC] = own_ref[r]
         wide[width + r, :, CC:] = side_lanes(left, right, r)
@@ -383,7 +407,7 @@
     def _():
         total[...] = jnp.zeros_like(total)
 
-    ones = jnp.ones((META, LANES), BF)
+    ones = jnp.ones((16, LANES), BF)
 
     def one(i, carry):
         meta = got_ref[i, 2 * CH :, :].astype(F32)
@@ -420,7 +444,7 @@
         in_specs=[pl.BlockSpec((per, SLOT_ROWS, LANES), lambda i: (i, 0, 0))],
         out_specs=[whole(s.shape) for s in shapes] + [smem()],
         out_shape=shapes + [jax.ShapeDtypeStruct((2 * devices,), jnp.int32)],
-        scratch_shapes=[pltpu.VMEM((NPATCH, CH + META, LANES), F32)],
+        scratch_shapes=[pltpu.VMEM((NPATCH, CH + 16, LANES), F32)],
         compiler_params=params(),
         cost_estimate=cost(2 * 256 * 80 * 128 * 128, 6 << 20),
         name="deposit",
@@ -457,22 +481,25 @@
         at = gy * CR + row
         return jnp.where(jnp.logical_and(at >= 0, at < rows * CR), across, 0.0)
 
-    def first(g, carry):
+    for g in range(12):
         total = None
         for j in range(2):
-            pre = conv_row(wide, 2 * g + j, w_in[...], 1)
-            value, slope = gelu_both(pre)
-            value = (value * row_mask(2 * g + j - 4)).astype(BF)
-            fine[2 * g + j] = value
-            slope_in[2 * g + j] = slope[:, :CC]
+            row = 2 * g + j
+            pre = conv_row(wide, row, w_in[...], 1)
+            value, half, square = gelu_parts(pre)
+            if 4 <= row < 4 + CR:
+                slope_in[row - 4] = gelu_slope(half[:, :CC], value[:, :CC], square[:, :CC])
+                value = jnp.concatenate(
+                    [value[:, :CC], value[:, CC:] * across[:, CC:]], axis=1
+                ).astype(BF)
+            else:
+                value = (value * row_mask(row - 4)).astype(BF)
+            fine[row] = value
             value = value.astype(F32)
             total = value if j == 0 else total + value
         coarse[g] = (0.25 * pair_sum(total)).astype(BF)
-        return carry
-
-    lax.fori_loop(0, 12, first, 0, unroll=2)
-
-    def middle(g, carry):
+
+    for g in range(10):
         pre = conv_row(coarse, g, w_mid[...], 2)
         value, slope = gelu_both(pre)
         slope_mid[g] = slope
@@ -480,16 +507,14 @@
         change = (before + value).astype(BF).astype(F32) - before
         for j in range(2):
             row = fine[2 * g + 2 + j].astype(F32) + change
-            rebuilt[2 * g + j] = (row * row_mask(2 * g + j - 2)).astype(BF)
-        return carry
-
-    lax.fori_loop(0, 10, middle, 0, unroll=2)
-
-    def last(r, carry):
+            if 1 <= g < 9:
+                rebuilt[2 * g + j, :, :CC] = row[:, :CC].astype(BF)
+                rebuilt[2 * g + j, :, CC:] = (row[:, CC:] * across[:, CC:]).astype(BF)
+            else:
+                rebuilt[2 * g + j] = (row * row_mask(2 * g + j - 2)).astype(BF)
+
+    for r in range(CR):
         grid_out[r] = conv_row(rebuilt, r + 1, w_out[...], 1)[:, :CC]
-        return carry
-
-    lax.fori_loop(0, CR, last, 0, unroll=4)
     for part in range(4):
         first_row, half = part // 2, part % 2
         lanes = slice(half * LANES, (half + 1) * LANES)
@@ -504,7 +529,7 @@
         jax.ShapeDtypeStruct((CR + 2 * HALO_IN, CH, WIDE), BF),
         jax.ShapeDtypeStruct((12, CH, WIDE), BF),
         jax.ShapeDtypeStruct((20, CH, WIDE), BF),
-        jax.ShapeDtypeStruct((24, CH, CC), F32),
+        jax.ShapeDtypeStruct((CR, CH, CC), F32),
         jax.ShapeDtypeStruct((10, CH, WIDE), F32),
     ]
     ins = (where, *halo, w_in, w_mid, w_out)
@@ -520,38 +545,31 @@
     )(*ins)
 
 
-def gather_kernel(per, patch_s, meta_ref, patches, out_ref):
+def share_kernel(per, patch_s, patches, out_ref):
     step = pl.program_id(0)
 
     def one(i, carry):
-        meta = meta_ref[i].astype(F32)
         for r in range(2):
             patch = patch_s[2 * (step * per + i) + r]
-            values = dot(patches[patch], one_hot(meta[r : r + 1]))
-            out_ref[i, r * CH : (r + 1) * CH, :] = values.astype(BF)
-        return carry
-
-    lax.fori_loop(0, per, one, 0, unroll=32)
-
-
-def gather(patch_at, got, patches):
-    devices = got.shape[0]
-    steps = 4
+            out_ref[i, r * CH : (r + 1) * CH, :] = patches[patch]
+        return carry
+
+    lax.fori_loop(0, per, one, 0, unroll=16)
+
+
+def share(patch_at, patches, devices):
+    steps = 2
     per = devices // steps
     return pl.pallas_call(
-        functools.partial(gather_kernel, per),
+        functools.partial(share_kernel, per),
         grid=(steps,),
-        in_specs=[
-            smem(),
-            pl.BlockSpec((per, META, LANES), lambda i: (i, 2 * CH // META, 0)),
-            whole(patches.shape),
-        ],
+        in_specs=[smem(), whole(patches.shape)],
         out_specs=pl.BlockSpec((per, 2 * CH, LANES), lambda i: (i, 0, 0)),
         out_shape=jax.ShapeDtypeStruct((devices, 2 * CH, LANES), BF),
         compiler_params=params(),
-        cost_estimate=cost(2 * 256 * 64 * 128 * 128, 6 << 20),
-        name="gather",
-    )(patch_at, got, patches)
+        cost_estimate=cost(0, 6 << 20),
+        name="share",
+    )(patch_at, patches)
 
 
 GROUP = 16
@@ -564,9 +582,8 @@
     scale,
     patch_s,
     got_ref,
-    value_ref,
-    first_ref,
-    second_ref,
+    patches,
+    target_ref,
     w_hidden,
     w_pred,
     w_back,
@@ -602,19 +619,21 @@
                 rows = slice(r * CH, (r + 1) * CH)
                 start = piece * span + (2 * k + r) * LANES
                 lanes = slice(start, start + LANES)
-                pair[:CH, lanes] = value_ref[at, rows, :]
+                code = meta[r : r + 1]
+                patch = patch_s[2 * (step * GROUP + at) + r]
+                pair[:CH, lanes] = dot(patches[patch], one_hot(code)).astype(BF)
                 pair[CH:, lanes] = got_ref[at, rows, :]
-                codes.append(meta[r : r + 1])
+                codes.append(code)
         inputs = pair[:, whole_lanes]
         hidden, slope = gelu_both(dot(w_hidden[...], inputs))
         hidden = hidden.astype(BF)
         pred = dot(w_pred[...], hidden)
         for k in range(count):
-            for r, target_ref in enumerate((first_ref, second_ref)):
+            for r in range(2):
                 slot = 2 * k + r
                 lanes = slice(slot * LANES, (slot + 1) * LANES)
                 live = jnp.where(codes[slot] >= 0.0, scale, 0.0)
-                target = target_ref[piece * count + k].astype(F32)
+                target = target_ref[piece * count + k, r * CH : (r + 1) * CH, :].astype(F32)
                 start = piece * span + slot * LANES
                 errors[:, start : start + LANES] = (live * (pred[:, lanes] - target)).astype(BF)
         wrong = errors[:, whole_lanes]
@@ -637,10 +656,9 @@
         write_strips(HALO_OUT, own, head, tail, left, right)
 
 
-def particles(patch_at, got, values, first, second, w_hidden, w_pred, w_back, w_grid, scale):
+def particles(patch_at, got, patches, target, w_hidden, w_pred, w_back, w_grid, scale):
     devices = got.shape[0]
     steps = devices // GROUP
-    half = pl.BlockSpec((GROUP, CH, LANES), lambda i: (i, 0, 0))
     shapes = strip_shapes(HALO_OUT) + [jax.ShapeDtypeStruct((HID + CH, HID), F32)]
     return pl.pallas_call(
         functools.partial(particle_kernel, steps - 1, scale),
@@ -648,9 +666,8 @@
         in_specs=[
             smem(),
             pl.BlockSpec((GROUP, SLOT_ROWS, LANES), lambda i: (i, 0, 0)),
+            whole(patches.shape),
             pl.BlockSpec((GROUP, 2 * CH, LANES), lambda i: (i, 0, 0)),
-            half,
-            half,
             whole(w_hidden.shape),
             whole(w_pred.shape),
             whole(w_back.shape),
@@ -666,7 +683,7 @@
         compiler_params=params(),
         cost_estimate=cost(2 * 32768 * 128 * 700, 16 << 20, 32768 * 128),
         name="particles",
-    )(patch_at, got, values, first, second, w_hidden, w_pred, w_back, w_grid)
+    )(patch_at, got, patches, target, w_hidden, w_pred, w_back, w_grid)
 
 
 def shifted(value, shift):
@@ -742,16 +759,16 @@
         mid_grad[g] = (pair_sum(total) * slope_mid[g] * mask).astype(BF)
         return carry
 
-    lax.fori_loop(0, 10, pooled, 0, unroll=2)
+    lax.fori_loop(0, 10, pooled, 0, unroll=10)
 
     def fine(g, carry):
         spread = 0.25 * conv_row(mid_grad, g, flip_mid[...], 2)[:, :CC]
         for j in range(2):
             value = rebuilt_grad[2 * g + 2 + j, :, :CC].astype(F32) + spread
-            first_grad[2 * g + j] = (value * slope_in[2 * g + 4 + j]).astype(BF)
-        return carry
-
-    lax.fori_loop(0, 8, fine, 0, unroll=4)
+            first_grad[2 * g + j] = (value * slope_in[2 * g + j]).astype(BF)
+        return carry
+
+    lax.fori_loop(0, 8, fine, 0, unroll=8)
 
     sum_in[...] = jnp.zeros_like(sum_in)
     sum_mid[...] = jnp.zeros_like(sum_mid)
@@ -763,7 +780,7 @@
         )
         return carry
 
-    lax.fori_loop(0, CR, fine_terms, 0, unroll=4)
+    lax.fori_loop(0, CR, fine_terms, 0, unroll=16)
     even = (lane_index((CH, CC)) & 1) == 0
 
     def coarse_terms(g, carry):
@@ -773,7 +790,7 @@
         )
         return carry
 
-    lax.fori_loop(0, 8, coarse_terms, 0, unroll=4)
+    lax.fori_loop(0, 8, coarse_terms, 0, unroll=8)
 
     rows_each = 3 * CH
     for which, total in enumerate((sum_in, sum_mid, sum_out)):
@@ -837,8 +854,8 @@
     )(sums)
 
 
-def swap(value):
-    return lax.all_to_all(value, ("gx", "gy"), split_axis=0, concat_axis=0, tiled=True)
+def swap(value, axes=("gx", "gy")):
+    return lax.all_to_all(value, axes, split_axis=0, concat_axis=0, tiled=True)
 
 
 def shards(
@@ -857,36 +874,35 @@
 ):
     nblocks = block_tile.shape[0]
     columns, rows = lax.axis_size("gx"), lax.axis_size("gy")
-    devices = columns * rows
+    devices, grid = columns * rows, (columns, rows)
     tile = block_tile[:, 0]
     where = jnp.stack([lax.axis_index("gx"), lax.axis_index("gy")]).astype(jnp.int32)
     scale = 1.0 / math.sqrt(nblocks * LANES * devices)
     w_pred = mlp_out.T
-
-    sent = dispatch(tile, block_patch, block_fill, cell_idx, part_feat, devices)
-    sent_first, sent_second = dispatch_target(tile, target, devices)
-    got = swap(sent)
+    by_row = ("gy", "gx")
+
+    sent = dispatch(tile, block_patch, block_fill, cell_idx, part_feat, grid)
+    sent_target = dispatch_target(tile, target, grid)
+    got = swap(sent, by_row)
     prepared = prepare(conv_in, conv_mid, conv_out, mlp_grid, mlp_part, w_pred)
-    got, sent_first, sent_second, where, *prepared = lax.optimization_barrier(
-        (got, sent_first, sent_second, where, *prepared)
+    got, sent_target, where, *prepared = lax.optimization_barrier(
+        (got, sent_target, where, *prepared)
     )
     w_in, w_mid, w_out, f_mid, f_out, w_hidden, w_back = prepared
-    got_first = swap(sent_first)
+    got_target = swap(sent_target, by_row)
 
     own, *strips, patch_at = deposit(got)
-    halo = (own, *exchange(*strips))
-    sent_second, *halo = lax.optimization_barrier((sent_second, *halo))
-    got_second = swap(sent_second)
+    strips, _ = exchange(*strips)
+    halo = (own, *strips)
     patches, wide_in, coarse, rebuilt, slope_in, slope_mid = unet_forward(
         where, halo, w_in, w_mid, w_out, columns, rows
     )
-    values = gather(patch_at, got, patches)
-    got_values = swap(values)
+    got_values = swap(share(patch_at, patches, devices), by_row)
     own, *strips, particle_grads = particles(
-        patch_at, got, values, got_first, got_second, w_hidden, w_pred, w_back, mlp_grid, scale
+        patch_at, got, patches, got_target, w_hidden, w_pred, w_back, mlp_grid, scale
     )
-    halo = (own, *exchange(*strips))
-    sum_out = out_terms(own, rebuilt)
+    strips, sum_out = exchange(*strips, out_terms(own, rebuilt))
+    halo = (own, *strips)
     saved = (wide_in, coarse, slope_in, slope_mid)
     staged = unet_backward(
         where, halo, saved, f_mid, f_out, particle_grads, sum_out, columns, rows
@@ -895,7 +911,9 @@
     terms = swap(staged.reshape(devices, REDUCE_ROWS // devices, LANES))
     mine = jnp.sum(terms.astype(F32), axis=0).astype(BF)
     spread = swap(jnp.broadcast_to(mine[None], (devices, *mine.shape)))
-    pred = home_predictions(tile, got_values, part_feat, w_hidden, w_pred, devices)
+    pred = home_predictions(
+        tile, block_fill, cell_idx, got_values, part_feat, w_hidden, w_pred, grid
+    )
     *grads, grad_pred = split(spread.reshape(REDUCE_ROWS, LANES))
     return (pred, *grads, grad_pred.T)
 

time: 272 us -> 264 us (0.971)
  Pallas kernels: 92.9 us -> 87.5 us
  starting transfers between devices: 69.8 us -> 64.4 us
  blocking collectives: 21.5 us -> 25.1 us
    ppermute x6, waiting for transfers between devices: 4.41 us -> 25.8 us  [ahead(): return lax.ppermute(value, axis, [(i, i + 1) for i in range(count - 1)])]
    all_to_all x5 -> x4, waiting for transfers between devices: 70.9 us -> 53 us  [swap(): return lax.all_to_all(value, axes, split_axis=0, concat_axis=0, tiled=True)]
    all_to_all x5 -> x4, starting transfers between devices: 36.9 us -> 32.8 us  [swap(): return lax.all_to_all(value, axes, split_axis=0, concat_axis=0, tiled=True)]
    all_to_all x1, blocking collectives: 21.5 us -> 25.1 us  [swap(): return lax.all_to_all(value, axes, split_axis=0, concat_axis=0, tiled=True)]
    ppermute x6, waiting for transfers between devices: 6.22 us -> 2.76 us  [behind(): return lax.ppermute(value, axis, [(i + 1, i) for i in range(count - 1)])]
  transfers between devices with their start and end apart: 17 -> 16, of which waited for: 8 -> 6; matrix products, arithmetic and copies ran while one was open for 0% -> 0% of each run, Pallas kernels for 32% -> 31%
where the time goes in v2:
time: 264 us; the launch traced here: 263 us
  Pallas kernels  87.5 us (33%)
  waiting for transfers between devices  81.6 us (31%)
  starting transfers between devices  64.4 us (24%)
  blocking collectives  25.1 us (10%)
  local copies, waits for them, and re-layouts  3.02 us (1%)
    all_to_all x4, waiting for transfers between devices, swap(): return lax.all_to_all(value, axes, split_axis=0, concat_axis=0, tiled=True)  53 us
    all_to_all x4, starting transfers between devices, swap(): return lax.all_to_all(value, axes, split_axis=0, concat_axis=0, tiled=True)  32.8 us
    pallas_call x1, Pallas kernels, particles(): pl.pallas_call(functools.partial(particle_kernel, steps - 1, scale), grid...  32.6 us
    ppermute x6, waiting for transfers between devices, ahead(): return lax.ppermute(value, axis, [(i, i + 1) for i in range(count - 1)])  25.8 us
    all_to_all x1, blocking collectives, swap(): return lax.all_to_all(value, axes, split_axis=0, concat_axis=0, tiled=True)  25.1 us
    ppermute x6, starting transfers between devices, ahead(): return lax.ppermute(value, axis, [(i, i + 1) for i in range(count - 1)])  20.2 us
    ppermute x6, starting transfers between devices, behind(): return lax.ppermute(value, axis, [(i + 1, i) for i in range(count - 1)])  11.3 us
    pallas_call x1, Pallas kernels, deposit(): pl.pallas_call(functools.partial(deposit_kernel, per, steps - 1), grid=(s...  9.63 us
  transfers between devices with their start and end apart: 16, of which 6 were waited for; matrix products, arithmetic and copies ran while one was open for 0% of the time, Pallas kernels for 31%

profile of v2, /device:TPU:1, one launch (start us, length us, event | category | flops | bytes accessed | tf_op | source)
XLA Modules:
  0.0 263.4 jit_solution(1134027638453615623)
XLA Ops:
  0.6 4.7 %dispatch.1 = bf16[128,136,128]{2,1,0:T(8,128)(2,1)} custom-call(s32[64]{0:T(128)} %bitcast.12, s32[64]{0:T(128)} %patch_s.1, s32[64]{0:T(128)} %fill_s.3, s32[64,128]{1,0:T(8,128)} %cell_ref.3, bf16[64,8192]{1,0:T(8,128)(2,1)} %feat_ref.5), custom_call_target="tpu_custom_call" | custom-call | bytes 6291456 | tf_op jit(solution)/shard_map/dispatch/pallas_call | solution.py:154
  5.3 11.9 %all-to-all-start = ((bf16[128,136,128]{2,1,0:T(8,128)(2,1)}), bf16[128,136,128]{2,1,0:T(8,128)(2,1)}, u32[]{:S(2)}, u32[]{:S(2)}) async-start(bf16[128,136,128]{2,1,0:T(8,128)(2,1)} %dispatch.1), calls=%async_computation | async-start | bytes 8912896 | tf_op jit(solution)/shard_map/all_to_all | solution.py:858
  17.2 4.9 %dispatch_target.1 = bf16[128,128,128]{2,1,0:T(8,128)(2,1)} custom-call(s32[64]{0:T(128)} %bitcast.13, bf16[64,8192]{1,0:T(8,128)(2,1)} %feat_ref.4), custom_call_target="tpu_custom_call" | custom-call | bytes 6291456 | tf_op jit(solution)/shard_map/dispatch_target/pallas_call | solution.py:189
  25.0 46.3 %all-to-all-done.got_ref = bf16[128,136,128]{2,1,0:T(8,128)(2,1)} async-done(((bf16[128,136,128]{2,1,0:T(8,128)(2,1)}), bf16[128,136,128]{2,1,0:T(8,128)(2,1)}, u32[]{:S(2)}, u32[]{:S(2)}) %all-to-all-start) | async-done | bytes 4456480 | tf_op jit(solution)/shard_map/all_to_all | solution.py:858
  71.3 5.7 %all-to-all-start.1 = ((bf16[128,128,128]{2,1,0:T(8,128)(2,1)}), bf16[128,128,128]{2,1,0:T(8,128)(2,1)}, u32[]{:S(2)}, u32[]{:S(2)}) async-start(bf16[128,128,128]{2,1,0:T(8,128)(2,1)} %dispatch_target.1), calls=%async_computation.1 | async-start | bytes 8388608 | tf_op jit(solution)/shard_map/all_to_all | solution.py:858
  77.0 9.6 %deposit.1 = (bf16[16,64,256]{2,1,0:T(8,128)(2,1)}, bf16[10,64,128]{2,1,0:T(8,128)(2,1)}, bf16[10,64,128]{2,1,0:T(8,128)(2,1)}, bf16[1,64,128]{2,1,0:T(8,128)(2,...) custom-call(bf16[128,136,128]{2,1,0:T(8,128)(2,1)} %all-to-all-done.got_ref), custom_call_target="tpu_custom_call" | custom-call | flops 671088640 | bytes 6291456 | tf_op jit(solution)/shard_map/deposit/pallas_call | solution.py:441
  86.7 3.3 %collective-permute-start.2 = (bf16[1,64,128]{2,1,0:T(8,128)(2,1)}, bf16[1,64,128]{2,1,0:T(8,128)(2,1)S(1)}, u32[]{:S(2)}, u32[]{:S(2)}) collective-permute-start(bf16[1,64,128]{2,1,0:T(8,128)(2,1)} %get-tuple-element.66), channel_id=1, source_target_pairs={{0,8},{8,16},{16,24},{24,32},{32,40},{40,48},{48,56},{56,64},{64,7... | collective-permute-start | bytes 49160 | tf_op jit(solution)/shard_map/ppermute | solution.py:330
  91.3 3.6 %collective-permute-start = (bf16[10,64,128]{2,1,0:T(8,128)(2,1)}, bf16[10,64,128]{2,1,0:T(8,128)(2,1)S(1)}, u32[]{:S(2)}, u32[]{:S(2)}) collective-permute-start(bf16[10,64,128]{2,1,0:T(8,128)(2,1)} %get-tuple-element.64), channel_id=1, source_target_pairs={{0,1},{1,2},{2,3},{3,4},{4,5},{5,6},{6,7},{8,9},{9,10},{10,11},{11... | collective-permute-start | bytes 491528 | tf_op jit(solution)/shard_map/ppermute | solution.py:330
  96.8 23.9 %collective-permute-done.2 = bf16[1,64,128]{2,1,0:T(8,128)(2,1)S(1)} collective-permute-done((bf16[1,64,128]{2,1,0:T(8,128)(2,1)}, bf16[1,64,128]{2,1,0:T(8,128)(2,1)S(1)}, u32[]{:S(2)}, u32[]{:S(2)}) %collective-permute-start.2) | collective-permute-done | bytes 16416 | tf_op jit(solution)/shard_map/ppermute | solution.py:330
  120.7 2.8 %collective-permute-done.3 = bf16[1,64,128]{2,1,0:T(8,128)(2,1)S(1)} collective-permute-done((bf16[1,64,128]{2,1,0:T(8,128)(2,1)}, bf16[1,64,128]{2,1,0:T(8,128)(2,1)S(1)}, u32[]{:S(2)}, u32[]{:S(2)}) %collective-permute-start.3) | collective-permute-done | bytes 16416 | tf_op jit(solution)/shard_map/ppermute | solution.py:335
  126.1 3.0 %collective-permute-start.4 = (bf16[2,64,128]{2,1,0:T(8,128)(2,1)S(1)}, bf16[2,64,128]{2,1,0:T(8,128)(2,1)S(1)}, u32[]{:S(2)}, u32[]{:S(2)}) collective-permute-start(bf16[2,64,128]{2,1,0:T(8,128)(2,1)S(1)} %constant_dynamic-update-slice_fusion.sides), channel_id=1, source_target_pairs={{0,1},{1,2},{2,3},{3,4},{4,5},{5,6},{6,7},{8,9},{9,10},{10,11},{11... | collective-permute-start | bytes 98312 | tf_op jit(solution)/shard_map/ppermute | solution.py:330
  130.9 9.4 %unet_forward.1 = (bf16[32,64,128]{2,1,0:T(8,128)(2,1)}, bf16[26,64,384]{2,1,0:T(8,128)(2,1)}, bf16[12,64,384]{2,1,0:T(8,128)(2,1)}, bf16[20,64,384]{2,1,0:T(8,1...) custom-call(s32[2]{0:T(128)} %pad_add_fusion.where_s, bf16[16,64,256]{2,1,0:T(8,128)(2,1)} %get-tuple-element.63.own, ...), custom_call_target="tpu_custom_call" | custom-call | flops 1415577600 | bytes 10485760 | tf_op jit(solution)/shard_map/unet_forward/pallas_call | solution.py:536
  140.3 3.2 %share.1 = bf16[128,128,128]{2,1,0:T(8,128)(2,1)} custom-call(s32[256]{0:T(256)} %get-tuple-element.62.patch_s, bf16[32,64,128]{2,1,0:T(8,128)(2,1)} %get-tuple-element.71.patches), custom_call_target="tpu_custom_call" | custom-call | bytes 6291456 | tf_op jit(solution)/shard_map/share/pallas_call | solution.py:563
  143.5 10.6 %all-to-all-start.2 = ((bf16[128,128,128]{2,1,0:T(8,128)(2,1)}), bf16[128,128,128]{2,1,0:T(8,128)(2,1)}, u32[]{:S(2)}, u32[]{:S(2)}) async-start(bf16[128,128,128]{2,1,0:T(8,128)(2,1)} %share.1), calls=%async_computation.2 | async-start | bytes 8388608 | tf_op jit(solution)/shard_map/all_to_all | solution.py:858
  154.1 32.6 %particles.1 = (bf16[16,64,256]{2,1,0:T(8,128)(2,1)}, bf16[6,64,128]{2,1,0:T(8,128)(2,1)}, bf16[6,64,128]{2,1,0:T(8,128)(2,1)}, bf16[1,64,128]{2,1,0:T(8,128)(2,...) custom-call(s32[256]{0:T(256)} %get-tuple-element.62.patch_s, bf16[128,136,128]{2,1,0:T(8,128)(2,1)} %all-to-all-done.got_ref, ...), custom_call_target="tpu_custom_call" | custom-call | flops 5872025600 | bytes 16777216 | tf_op jit(solution)/shard_map/particles/pallas_call | solution.py:663
  186.8 3.3 %collective-permute-start.8 = (bf16[1,64,128]{2,1,0:T(8,128)(2,1)}, bf16[1,64,128]{2,1,0:T(8,128)(2,1)S(1)}, u32[]{:S(2)}, u32[]{:S(2)}) collective-permute-start(bf16[1,64,128]{2,1,0:T(8,128)(2,1)} %get-tuple-element.78), channel_id=1, source_target_pairs={{0,8},{8,16},{16,24},{24,32},{32,40},{40,48},{48,56},{56,64},{64,7... | collective-permute-start | bytes 49160 | tf_op jit(solution)/shard_map/ppermute | solution.py:330
  191.4 3.7 %collective-permute-start.6 = (bf16[6,64,128]{2,1,0:T(8,128)(2,1)}, bf16[6,64,128]{2,1,0:T(8,128)(2,1)S(1)}, u32[]{:S(2)}, u32[]{:S(2)}) collective-permute-start(bf16[6,64,128]{2,1,0:T(8,128)(2,1)} %get-tuple-element.76), channel_id=1, source_target_pairs={{0,1},{1,2},{2,3},{3,4},{4,5},{5,6},{6,7},{8,9},{9,10},{10,11},{11... | collective-permute-start | bytes 294920 | tf_op jit(solution)/shard_map/ppermute | solution.py:330
  197.0 4.0 %out_terms.1.sum_out = f32[192,256]{1,0:T(8,128)} custom-call(bf16[16,64,256]{2,1,0:T(8,128)(2,1)} %get-tuple-element.75.own, bf16[20,64,384]{2,1,0:T(8,128)(2,1)} %get-tuple-element.80.rebuilt), custom_call_target="tpu_custom_call" | custom-call | flops 452984832 | bytes 10485760 | tf_op jit(solution)/shard_map/out_terms/pallas_call | solution.py:709
  203.2 3.4 %collective-permute-start.10 = (bf16[2,64,128]{2,1,0:T(8,128)(2,1)S(1)}, bf16[2,64,128]{2,1,0:T(8,128)(2,1)S(1)}, u32[]{:S(2)}, u32[]{:S(2)}) collective-permute-start(bf16[2,64,128]{2,1,0:T(8,128)(2,1)S(1)} %constant_dynamic-update-slice_fusion.2.sides), channel_id=1, source_target_pairs={{0,1},{1,2},{2,3},{3,4},{4,5},{5,6},{6,7},{8,9},{9,10},{10,11},{11... | collective-permute-start | bytes 98312 | tf_op jit(solution)/shard_map/ppermute | solution.py:330
  208.3 8.0 %unet_backward.1 = bf16[2048,128]{1,0:T(8,128)(2,1)} custom-call(s32[2]{0:T(128)} %pad_add_fusion.where_s, bf16[16,64,256]{2,1,0:T(8,128)(2,1)} %get-tuple-element.75.own, bf16[6,64,128]{2,1,0:T(8,128)(2,1)} %copy-done.5, bf16[6,64,128]{2,1,0:T(8,128)(2,1)} %copy-done.6, bf16[2,64,128]{2,1,0:T(8,128)(2,1)} %copy-done.2, bf16[2,64,128]{2,1,0:T(8,128)(2,1)} %copy-done.9, ...), custom_call_target="tpu_custom_call" | custom-call | flops 1981808640 | bytes 10485760 | tf_op jit(solution)/shard_map/unet_backward/pallas_call | solution.py:809
  216.3 25.1 %all_to_all.25 = bf16[128,16,128]{2,1,0:T(8,128)(2,1)S(1)} all-to-all(bf16[128,16,128]{2,1,0:T(8,128)(2,1)} %bitcast.8), channel_id=1, replica_groups=mesh['gx'=16,'gy'=8] {'gx','gy'}, dimensions={0} | all-to-all | bytes 1048576 | tf_op jit(solution)/shard_map/all_to_all | solution.py:858
  242.4 4.6 %all-to-all-start.4 = ((bf16[128,16,128]{2,1,0:T(8,128)(2,1)}), bf16[128,16,128]{2,1,0:T(8,128)(2,1)S(1)}, u32[]{:S(2)}, u32[]{:S(2)}) async-start(bf16[128,16,128]{2,1,0:T(8,128)(2,1)} %broadcast_in_dim.2), calls=%async_computation.4 | async-start | bytes 1048576 | tf_op jit(solution)/shard_map/all_to_all | solution.py:858
  247.0 6.8 %home_predictions.1 = bf16[64,8192]{1,0:T(8,128)(2,1)} custom-call(s32[64]{0:T(128)} %bitcast.14, s32[64]{0:T(128)} %fill_s.3, s32[64,128]{1,0:T(8,128)} %cell_ref.3, bf16[128,128,128]{2,1,0:T(8,128)(2,1)} %all-to-all-done.2.got_ref, bf16[64,8192]{1,0:T(8,128)(2,1)} %feat_ref.5, bf16[128,128]{1,0:T(8,128)(2,1)} %get-tuple-element.73.w_hidden, ...), custom_call_target="tpu_custom_call" | custom-call | flops 402653184 | bytes 8388608 | tf_op jit(solution)/shard_map/home_predictions/pallas_call | solution.py:231
  253.8 6.7 %all-to-all-done.4 = bf16[128,16,128]{2,1,0:T(8,128)(2,1)S(1)} async-done(((bf16[128,16,128]{2,1,0:T(8,128)(2,1)}), bf16[128,16,128]{2,1,0:T(8,128)(2,1)S(1)}, u32[]{:S(2)}, u32[]{:S(2)}) %all-to-all-start.4) | async-done | bytes 524320 | tf_op jit(solution)/shard_map/all_to_all | solution.py:858
  (49 shorter events, 21.3 us)
Async XLA Ops:
  5.3 66.0 %all-to-all-start = ((bf16[128,136,128]{2,1,0:T(8,128)(2,1)}), bf16[128,136,128]{2,1,0:T(8,128)(2,1)}, u32[]{:S(2)}, u32[]{:S(2)}) async-start(bf16[128,136,128]{2,1,0:T(8,128)(2,1)} %dispatch.1), calls=%async_computation | async-start | bytes 8912896 | tf_op jit(solution)/shard_map/all_to_all | solution.py:858
  71.3 72.2 %all-to-all-start.1 = ((bf16[128,128,128]{2,1,0:T(8,128)(2,1)}), bf16[128,128,128]{2,1,0:T(8,128)(2,1)}, u32[]{:S(2)}, u32[]{:S(2)}) async-start(bf16[128,128,128]{2,1,0:T(8,128)(2,1)} %dispatch_target.1), calls=%async_computation.1 | async-start | bytes 8388608 | tf_op jit(solution)/shard_map/all_to_all | solution.py:858
  86.7 34.0 %collective-permute-start.2 = (bf16[1,64,128]{2,1,0:T(8,128)(2,1)}, bf16[1,64,128]{2,1,0:T(8,128)(2,1)S(1)}, u32[]{:S(2)}, u32[]{:S(2)}) collective-permute-start(bf16[1,64,128]{2,1,0:T(8,128)(2,1)} %get-tuple-element.66), channel_id=1, source_target_pairs={{0,8},{8,16},{16,24},{24,32},{32,40},{40,48},{48,56},{56,64},{64,7... | collective-permute-start | bytes 49160 | tf_op jit(solution)/shard_map/ppermute | solution.py:330
  90.0 33.5 %collective-permute-start.3 = (bf16[1,64,128]{2,1,0:T(8,128)(2,1)}, bf16[1,64,128]{2,1,0:T(8,128)(2,1)S(1)}, u32[]{:S(2)}, u32[]{:S(2)}) collective-permute-start(bf16[1,64,128]{2,1,0:T(8,128)(2,1)} %get-tuple-element.67), channel_id=1, source_target_pairs={{8,0},{16,8},{24,16},{32,24},{40,32},{48,40},{56,48},{64,56},{72,6... | collective-permute-start | bytes 49160 | tf_op jit(solution)/shard_map/ppermute | solution.py:335
  91.3 38.9 %collective-permute-start = (bf16[10,64,128]{2,1,0:T(8,128)(2,1)}, bf16[10,64,128]{2,1,0:T(8,128)(2,1)S(1)}, u32[]{:S(2)}, u32[]{:S(2)}) collective-permute-start(bf16[10,64,128]{2,1,0:T(8,128)(2,1)} %get-tuple-element.64), channel_id=1, source_target_pairs={{0,1},{1,2},{2,3},{3,4},{4,5},{5,6},{6,7},{8,9},{9,10},{10,11},{11... | collective-permute-start | bytes 491528 | tf_op jit(solution)/shard_map/ppermute | solution.py:330
  94.9 35.3 %collective-permute-start.1 = (bf16[10,64,128]{2,1,0:T(8,128)(2,1)}, bf16[10,64,128]{2,1,0:T(8,128)(2,1)S(1)}, u32[]{:S(2)}, u32[]{:S(2)}) collective-permute-start(bf16[10,64,128]{2,1,0:T(8,128)(2,1)} %get-tuple-element.65), channel_id=1, source_target_pairs={{1,0},{2,1},{3,2},{4,3},{5,4},{6,5},{7,6},{9,8},{10,9},{11,10},{12... | collective-permute-start | bytes 491528 | tf_op jit(solution)/shard_map/ppermute | solution.py:335
  123.5 6.7 %copy-start.1 = (bf16[2,64,128]{2,1,0:T(8,128)(2,1)}, bf16[2,64,128]{2,1,0:T(8,128)(2,1)S(1)}, u32[]{:S(2)}) copy-start(bf16[2,64,128]{2,1,0:T(8,128)(2,1)S(1)} %constant_dynamic-update-slice_fusion.sides) | copy-start | bytes 98308
  123.5 5.7 %collective-permute-start.5 = (bf16[2,64,128]{2,1,0:T(8,128)(2,1)S(1)}, bf16[2,64,128]{2,1,0:T(8,128)(2,1)S(1)}, u32[]{:S(2)}, u32[]{:S(2)}) collective-permute-start(bf16[2,64,128]{2,1,0:T(8,128)(2,1)S(1)} %constant_dynamic-update-slice_fusion.sides), channel_id=1, source_target_pairs={{1,0},{2,1},{3,2},{4,3},{5,4},{6,5},{7,6},{9,8},{10,9},{11,10},{12... | collective-permute-start | bytes 98312 | tf_op jit(solution)/shard_map/ppermute | solution.py:335
  126.1 4.0 %collective-permute-start.4 = (bf16[2,64,128]{2,1,0:T(8,128)(2,1)S(1)}, bf16[2,64,128]{2,1,0:T(8,128)(2,1)S(1)}, u32[]{:S(2)}, u32[]{:S(2)}) collective-permute-start(bf16[2,64,128]{2,1,0:T(8,128)(2,1)S(1)} %constant_dynamic-update-slice_fusion.sides), channel_id=1, source_target_pairs={{0,1},{1,2},{2,3},{3,4},{4,5},{5,6},{6,7},{8,9},{9,10},{10,11},{11... | collective-permute-start | bytes 98312 | tf_op jit(solution)/shard_map/ppermute | solution.py:330
  129.2 1.0 copy-start.8
  130.2 0.7 copy-start.3
  130.2 0.7 copy-start.4
  143.5 72.8 %all-to-all-start.2 = ((bf16[128,128,128]{2,1,0:T(8,128)(2,1)}), bf16[128,128,128]{2,1,0:T(8,128)(2,1)}, u32[]{:S(2)}, u32[]{:S(2)}) async-start(bf16[128,128,128]{2,1,0:T(8,128)(2,1)} %share.1), calls=%async_computation.2 | async-start | bytes 8388608 | tf_op jit(solution)/shard_map/all_to_all | solution.py:858
  186.8 14.2 %collective-permute-start.8 = (bf16[1,64,128]{2,1,0:T(8,128)(2,1)}, bf16[1,64,128]{2,1,0:T(8,128)(2,1)S(1)}, u32[]{:S(2)}, u32[]{:S(2)}) collective-permute-start(bf16[1,64,128]{2,1,0:T(8,128)(2,1)} %get-tuple-element.78), channel_id=1, source_target_pairs={{0,8},{8,16},{16,24},{24,32},{32,40},{40,48},{48,56},{56,64},{64,7... | collective-permute-start | bytes 49160 | tf_op jit(solution)/shard_map/ppermute | solution.py:330
  190.1 10.9 %collective-permute-start.9 = (bf16[1,64,128]{2,1,0:T(8,128)(2,1)}, bf16[1,64,128]{2,1,0:T(8,128)(2,1)S(1)}, u32[]{:S(2)}, u32[]{:S(2)}) collective-permute-start(bf16[1,64,128]{2,1,0:T(8,128)(2,1)} %get-tuple-element.79), channel_id=1, source_target_pairs={{8,0},{16,8},{24,16},{32,24},{40,32},{48,40},{56,48},{64,56},{72,6... | collective-permute-start | bytes 49160 | tf_op jit(solution)/shard_map/ppermute | solution.py:335
  191.4 16.3 %collective-permute-start.6 = (bf16[6,64,128]{2,1,0:T(8,128)(2,1)}, bf16[6,64,128]{2,1,0:T(8,128)(2,1)S(1)}, u32[]{:S(2)}, u32[]{:S(2)}) collective-permute-start(bf16[6,64,128]{2,1,0:T(8,128)(2,1)} %get-tuple-element.76), channel_id=1, source_target_pairs={{0,1},{1,2},{2,3},{3,4},{4,5},{5,6},{6,7},{8,9},{9,10},{10,11},{11... | collective-permute-start | bytes 294920 | tf_op jit(solution)/shard_map/ppermute | solution.py:330
  195.0 12.6 %collective-permute-start.7 = (bf16[6,64,128]{2,1,0:T(8,128)(2,1)}, bf16[6,64,128]{2,1,0:T(8,128)(2,1)S(1)}, u32[]{:S(2)}, u32[]{:S(2)}) collective-permute-start(bf16[6,64,128]{2,1,0:T(8,128)(2,1)} %get-tuple-element.77), channel_id=1, source_target_pairs={{1,0},{2,1},{3,2},{4,3},{5,4},{6,5},{7,6},{9,8},{10,9},{11,10},{12... | collective-permute-start | bytes 294920 | tf_op jit(solution)/shard_map/ppermute | solution.py:335
  201.0 6.6 %copy-start.2 = (bf16[2,64,128]{2,1,0:T(8,128)(2,1)}, bf16[2,64,128]{2,1,0:T(8,128)(2,1)S(1)}, u32[]{:S(2)}) copy-start(bf16[2,64,128]{2,1,0:T(8,128)(2,1)S(1)} %constant_dynamic-update-slice_fusion.2.sides) | copy-start | bytes 98308
  201.0 5.6 %collective-permute-start.11 = (bf16[2,64,128]{2,1,0:T(8,128)(2,1)S(1)}, bf16[2,64,128]{2,1,0:T(8,128)(2,1)S(1)}, u32[]{:S(2)}, u32[]{:S(2)}) collective-permute-start(bf16[2,64,128]{2,1,0:T(8,128)(2,1)S(1)} %constant_dynamic-update-slice_fusion.2.sides), channel_id=1, source_target_pairs={{1,0},{2,1},{3,2},{4,3},{5,4},{6,5},{7,6},{9,8},{10,9},{11,10},{12... | collective-permute-start | bytes 98312 | tf_op jit(solution)/shard_map/ppermute | solution.py:335
  203.2 4.4 %collective-permute-start.10 = (bf16[2,64,128]{2,1,0:T(8,128)(2,1)S(1)}, bf16[2,64,128]{2,1,0:T(8,128)(2,1)S(1)}, u32[]{:S(2)}, u32[]{:S(2)}) collective-permute-start(bf16[2,64,128]{2,1,0:T(8,128)(2,1)S(1)} %constant_dynamic-update-slice_fusion.2.sides), channel_id=1, source_target_pairs={{0,1},{1,2},{2,3},{3,4},{4,5},{5,6},{6,7},{8,9},{9,10},{10,11},{11... | collective-permute-start | bytes 98312 | tf_op jit(solution)/shard_map/ppermute | solution.py:330
  206.6 1.0 copy-start.7
  207.6 0.7 copy-start.6
  242.4 18.1 %all-to-all-start.4 = ((bf16[128,16,128]{2,1,0:T(8,128)(2,1)}), bf16[128,16,128]{2,1,0:T(8,128)(2,1)S(1)}, u32[]{:S(2)}, u32[]{:S(2)}) async-start(bf16[128,16,128]{2,1,0:T(8,128)(2,1)} %broadcast_in_dim.2), calls=%async_computation.4 | async-start | bytes 1048576 | tf_op jit(solution)/shard_map/all_to_all | solution.py:858
  260.5 0.8 copy-start
  (3 other events, 1.9 us)

commit v3 on v2

--- a/solution.py
+++ b/solution.py
@@ -693,26 +693,22 @@
     ).astype(BF)
 
 
-def out_terms_kernel(own, rebuilt, sum_out):
+def out_terms_kernel(start, own, rebuilt, sum_out):
     sum_out[...] = jnp.zeros_like(sum_out)
-
-    def one(r, carry):
+    for r in range(start, start + CR // 2):
         sum_out[:, : 3 * CH] += nt_dot(
-            rebuilt[pl.ds(r + 1, 3)].reshape(3 * CH, WIDE), shifted(own[r].astype(F32), 1)
+            rebuilt[r + 1 : r + 4].reshape(3 * CH, WIDE), shifted(own[r].astype(F32), 1)
         )
-        return carry
-
-    lax.fori_loop(0, CR, one, 0, unroll=4)
-
-
-def out_terms(own, rebuilt):
-    return pl.pallas_call(
-        out_terms_kernel,
+
+
+def out_terms(own, rebuilt, start):
+    return pl.pallas_call(
+        functools.partial(out_terms_kernel, start),
         in_specs=[vmem(), vmem()],
         out_specs=vmem(),
         out_shape=jax.ShapeDtypeStruct((3 * CH, 2 * LANES), F32),
         compiler_params=params(),
-        cost_estimate=cost(2 * 16 * 192 * 192 * 384, 10 << 20),
+        cost_estimate=cost(2 * 8 * 192 * 192 * 384, 5 << 20),
         name="out_terms",
     )(own, rebuilt)
 
@@ -734,7 +730,8 @@
     flip_mid,
     flip_out,
     particle_grads,
-    sum_out,
+    upper_out,
+    lower_out,
     staged,
     wide,
     rebuilt_grad,
@@ -793,19 +790,18 @@
     lax.fori_loop(0, 8, coarse_terms, 0, unroll=8)
 
     rows_each = 3 * CH
-    for which, total in enumerate((sum_in, sum_mid, sum_out)):
+    for which, total in enumerate(((sum_in,), (sum_mid,), (upper_out, lower_out))):
         for half in range(2):
             start = (2 * which + half) * rows_each
-            staged[start : start + rows_each] = total[
-                :, half * LANES : (half + 1) * LANES
-            ].astype(BF)
+            lanes = slice(half * LANES, (half + 1) * LANES)
+            staged[start : start + rows_each] = sum(part[:, lanes] for part in total).astype(BF)
     start = 6 * rows_each
     staged[start : start + HID + CH] = particle_grads[...].astype(BF)
     staged[start + HID + CH :] = jnp.zeros((REDUCE_ROWS - start - HID - CH, LANES), BF)
 
 
-def unet_backward(where, halo, saved, flip_mid, flip_out, particle_grads, sum_out, columns, rows):
-    ins = (where, *halo, *saved, flip_mid, flip_out, particle_grads, sum_out)
+def unet_backward(where, halo, saved, flip_mid, flip_out, particle_grads, sums_out, columns, rows):
+    ins = (where, *halo, *saved, flip_mid, flip_out, particle_grads, *sums_out)
     return pl.pallas_call(
         functools.partial(backward_kernel, columns, rows),
         in_specs=[smem()] + [vmem()] * (len(ins) - 1),
@@ -901,11 +897,12 @@
     own, *strips, particle_grads = particles(
         patch_at, got, patches, got_target, w_hidden, w_pred, w_back, mlp_grid, scale
     )
-    strips, sum_out = exchange(*strips, out_terms(own, rebuilt))
+    strips, upper_out = exchange(*strips, out_terms(own, rebuilt, 0))
+    sums_out = (upper_out, out_terms(own, rebuilt, CR // 2))
     halo = (own, *strips)
     saved = (wide_in, coarse, slope_in, slope_mid)
     staged = unet_backward(
-        where, halo, saved, f_mid, f_out, particle_grads, sum_out, columns, rows
+        where, halo, saved, f_mid, f_out, particle_grads, sums_out, columns, rows
     )
     staged, got_values = lax.optimization_barrier((staged, got_values))
     terms = swap(staged.reshape(devices, REDUCE_ROWS // devices, LANES))

time: 264 us -> 264 us (level)
    pallas_call x1 -> x2, Pallas kernels: 4.01 us -> 5.55 us  [out_terms(): pl.pallas_call(functools.partial(out_terms_kernel, start), in_specs=[vmem...]
where the time goes in v3:
time: 264 us; the launch traced here: 263 us
  Pallas kernels  89.5 us (34%)
  waiting for transfers between devices  81.4 us (31%)
  starting transfers between devices  64.4 us (24%)
  blocking collectives  22.9 us (9%)
  local copies, waits for them, and re-layouts  3.01 us (1%)
    all_to_all x4, waiting for transfers between devices, swap(): return lax.all_to_all(value, axes, split_axis=0, concat_axis=0, tiled=True)  53 us
    all_to_all x4, starting transfers between devices, swap(): return lax.all_to_all(value, axes, split_axis=0, concat_axis=0, tiled=True)  32.9 us
    pallas_call x1, Pallas kernels, particles(): pl.pallas_call(functools.partial(particle_kernel, steps - 1, scale), grid...  32.7 us
    ppermute x6, waiting for transfers between devices, ahead(): return lax.ppermute(value, axis, [(i, i + 1) for i in range(count - 1)])  24.9 us
    all_to_all x1, blocking collectives, swap(): return lax.all_to_all(value, axes, split_axis=0, concat_axis=0, tiled=True)  22.9 us
    ppermute x6, starting transfers between devices, ahead(): return lax.ppermute(value, axis, [(i, i + 1) for i in range(count - 1)])  19.8 us
    ppermute x6, starting transfers between devices, behind(): return lax.ppermute(value, axis, [(i + 1, i) for i in range(count - 1)])  11.8 us
    pallas_call x1, Pallas kernels, deposit(): pl.pallas_call(functools.partial(deposit_kernel, per, steps - 1), grid=(s...  9.64 us
  transfers between devices with their start and end apart: 16, of which 6 were waited for; matrix products, arithmetic and copies ran while one was open for 0% of the time, Pallas kernels for 31%

profile of v3, /device:TPU:1, one launch (start us, length us, event | category | flops | bytes accessed | tf_op | source)
XLA Modules:
  0.0 262.9 jit_solution(11886371150439138009)
XLA Ops:
  0.6 4.8 %dispatch.1 = bf16[128,136,128]{2,1,0:T(8,128)(2,1)} custom-call(s32[64]{0:T(128)} %bitcast.12, s32[64]{0:T(128)} %patch_s.1, s32[64]{0:T(128)} %fill_s.3, s32[64,128]{1,0:T(8,128)} %cell_ref.3, bf16[64,8192]{1,0:T(8,128)(2,1)} %feat_ref.5), custom_call_target="tpu_custom_call" | custom-call | bytes 6291456 | tf_op jit(solution)/shard_map/dispatch/pallas_call | solution.py:154
  5.5 11.9 %all-to-all-start = ((bf16[128,136,128]{2,1,0:T(8,128)(2,1)}), bf16[128,136,128]{2,1,0:T(8,128)(2,1)}, u32[]{:S(2)}, u32[]{:S(2)}) async-start(bf16[128,136,128]{2,1,0:T(8,128)(2,1)} %dispatch.1), calls=%async_computation | async-start | bytes 8912896 | tf_op jit(solution)/shard_map/all_to_all | solution.py:854
  17.4 4.9 %dispatch_target.1 = bf16[128,128,128]{2,1,0:T(8,128)(2,1)} custom-call(s32[64]{0:T(128)} %bitcast.13, bf16[64,8192]{1,0:T(8,128)(2,1)} %feat_ref.4), custom_call_target="tpu_custom_call" | custom-call | bytes 6291456 | tf_op jit(solution)/shard_map/dispatch_target/pallas_call | solution.py:189
  25.1 46.3 %all-to-all-done.got_ref = bf16[128,136,128]{2,1,0:T(8,128)(2,1)} async-done(((bf16[128,136,128]{2,1,0:T(8,128)(2,1)}), bf16[128,136,128]{2,1,0:T(8,128)(2,1)}, u32[]{:S(2)}, u32[]{:S(2)}) %all-to-all-start) | async-done | bytes 4456480 | tf_op jit(solution)/shard_map/all_to_all | solution.py:854
  71.4 5.7 %all-to-all-start.1 = ((bf16[128,128,128]{2,1,0:T(8,128)(2,1)}), bf16[128,128,128]{2,1,0:T(8,128)(2,1)}, u32[]{:S(2)}, u32[]{:S(2)}) async-start(bf16[128,128,128]{2,1,0:T(8,128)(2,1)} %dispatch_target.1), calls=%async_computation.1 | async-start | bytes 8388608 | tf_op jit(solution)/shard_map/all_to_all | solution.py:854
  77.2 9.6 %deposit.1 = (bf16[16,64,256]{2,1,0:T(8,128)(2,1)}, bf16[10,64,128]{2,1,0:T(8,128)(2,1)}, bf16[10,64,128]{2,1,0:T(8,128)(2,1)}, bf16[1,64,128]{2,1,0:T(8,128)(2,...) custom-call(bf16[128,136,128]{2,1,0:T(8,128)(2,1)} %all-to-all-done.got_ref), custom_call_target="tpu_custom_call" | custom-call | flops 671088640 | bytes 6291456 | tf_op jit(solution)/shard_map/deposit/pallas_call | solution.py:441
  86.8 3.3 %collective-permute-start.2 = (bf16[1,64,128]{2,1,0:T(8,128)(2,1)}, bf16[1,64,128]{2,1,0:T(8,128)(2,1)S(1)}, u32[]{:S(2)}, u32[]{:S(2)}) collective-permute-start(bf16[1,64,128]{2,1,0:T(8,128)(2,1)} %get-tuple-element.66), channel_id=1, source_target_pairs={{0,8},{8,16},{16,24},{24,32},{32,40},{40,48},{48,56},{56,64},{64,7... | collective-permute-start | bytes 49160 | tf_op jit(solution)/shard_map/ppermute | solution.py:330
  91.4 3.6 %collective-permute-start = (bf16[10,64,128]{2,1,0:T(8,128)(2,1)}, bf16[10,64,128]{2,1,0:T(8,128)(2,1)S(1)}, u32[]{:S(2)}, u32[]{:S(2)}) collective-permute-start(bf16[10,64,128]{2,1,0:T(8,128)(2,1)} %get-tuple-element.64), channel_id=1, source_target_pairs={{0,1},{1,2},{2,3},{3,4},{4,5},{5,6},{6,7},{8,9},{9,10},{10,11},{11... | collective-permute-start | bytes 491528 | tf_op jit(solution)/shard_map/ppermute | solution.py:330
  97.0 23.9 %collective-permute-done.2 = bf16[1,64,128]{2,1,0:T(8,128)(2,1)S(1)} collective-permute-done((bf16[1,64,128]{2,1,0:T(8,128)(2,1)}, bf16[1,64,128]{2,1,0:T(8,128)(2,1)S(1)}, u32[]{:S(2)}, u32[]{:S(2)}) %collective-permute-start.2) | collective-permute-done | bytes 16416 | tf_op jit(solution)/shard_map/ppermute | solution.py:330
  126.3 3.0 %collective-permute-start.4 = (bf16[2,64,128]{2,1,0:T(8,128)(2,1)S(1)}, bf16[2,64,128]{2,1,0:T(8,128)(2,1)S(1)}, u32[]{:S(2)}, u32[]{:S(2)}) collective-permute-start(bf16[2,64,128]{2,1,0:T(8,128)(2,1)S(1)} %constant_dynamic-update-slice_fusion.sides), channel_id=1, source_target_pairs={{0,1},{1,2},{2,3},{3,4},{4,5},{5,6},{6,7},{8,9},{9,10},{10,11},{11... | collective-permute-start | bytes 98312 | tf_op jit(solution)/shard_map/ppermute | solution.py:330
  131.0 9.4 %unet_forward.1 = (bf16[32,64,128]{2,1,0:T(8,128)(2,1)}, bf16[26,64,384]{2,1,0:T(8,128)(2,1)}, bf16[12,64,384]{2,1,0:T(8,128)(2,1)}, bf16[20,64,384]{2,1,0:T(8,1...) custom-call(s32[2]{0:T(128)} %pad_add_fusion.where_s, bf16[16,64,256]{2,1,0:T(8,128)(2,1)} %get-tuple-element.63.own, ...), custom_call_target="tpu_custom_call" | custom-call | flops 1415577600 | bytes 10485760 | tf_op jit(solution)/shard_map/unet_forward/pallas_call | solution.py:536
  140.4 3.3 %share.1 = bf16[128,128,128]{2,1,0:T(8,128)(2,1)} custom-call(s32[256]{0:T(256)} %get-tuple-element.62.patch_s, bf16[32,64,128]{2,1,0:T(8,128)(2,1)} %get-tuple-element.71.patches), custom_call_target="tpu_custom_call" | custom-call | bytes 6291456 | tf_op jit(solution)/shard_map/share/pallas_call | solution.py:563
  143.8 10.6 %all-to-all-start.2 = ((bf16[128,128,128]{2,1,0:T(8,128)(2,1)}), bf16[128,128,128]{2,1,0:T(8,128)(2,1)}, u32[]{:S(2)}, u32[]{:S(2)}) async-start(bf16[128,128,128]{2,1,0:T(8,128)(2,1)} %share.1), calls=%async_computation.2 | async-start | bytes 8388608 | tf_op jit(solution)/shard_map/all_to_all | solution.py:854
  154.4 32.7 %particles.1 = (bf16[16,64,256]{2,1,0:T(8,128)(2,1)}, bf16[6,64,128]{2,1,0:T(8,128)(2,1)}, bf16[6,64,128]{2,1,0:T(8,128)(2,1)}, bf16[1,64,128]{2,1,0:T(8,128)(2,...) custom-call(s32[256]{0:T(256)} %get-tuple-element.62.patch_s, bf16[128,136,128]{2,1,0:T(8,128)(2,1)} %all-to-all-done.got_ref, ...), custom_call_target="tpu_custom_call" | custom-call | flops 5872025600 | bytes 16777216 | tf_op jit(solution)/shard_map/particles/pallas_call | solution.py:663
  187.1 3.3 %collective-permute-start.8 = (bf16[1,64,128]{2,1,0:T(8,128)(2,1)}, bf16[1,64,128]{2,1,0:T(8,128)(2,1)S(1)}, u32[]{:S(2)}, u32[]{:S(2)}) collective-permute-start(bf16[1,64,128]{2,1,0:T(8,128)(2,1)} %get-tuple-element.78), channel_id=1, source_target_pairs={{0,8},{8,16},{16,24},{24,32},{32,40},{40,48},{48,56},{56,64},{64,7... | collective-permute-start | bytes 49160 | tf_op jit(solution)/shard_map/ppermute | solution.py:330
  191.7 3.6 %collective-permute-start.6 = (bf16[6,64,128]{2,1,0:T(8,128)(2,1)}, bf16[6,64,128]{2,1,0:T(8,128)(2,1)S(1)}, u32[]{:S(2)}, u32[]{:S(2)}) collective-permute-start(bf16[6,64,128]{2,1,0:T(8,128)(2,1)} %get-tuple-element.76), channel_id=1, source_target_pairs={{0,1},{1,2},{2,3},{3,4},{4,5},{5,6},{6,7},{8,9},{9,10},{10,11},{11... | collective-permute-start | bytes 294920 | tf_op jit(solution)/shard_map/ppermute | solution.py:330
  197.3 2.8 %out_terms.2.upper_out = f32[192,256]{1,0:T(8,128)} custom-call(bf16[16,64,256]{2,1,0:T(8,128)(2,1)} %get-tuple-element.75.own, bf16[20,64,384]{2,1,0:T(8,128)(2,1)} %get-tuple-element.80.rebuilt), custom_call_target="tpu_custom_call" | custom-call | flops 226492416 | bytes 5242880 | tf_op jit(solution)/shard_map/out_terms/pallas_call | solution.py:705
  203.5 3.0 %collective-permute-start.10 = (bf16[2,64,128]{2,1,0:T(8,128)(2,1)S(1)}, bf16[2,64,128]{2,1,0:T(8,128)(2,1)S(1)}, u32[]{:S(2)}, u32[]{:S(2)}) collective-permute-start(bf16[2,64,128]{2,1,0:T(8,128)(2,1)S(1)} %constant_dynamic-update-slice_fusion.2.sides), channel_id=1, source_target_pairs={{0,1},{1,2},{2,3},{3,4},{4,5},{5,6},{6,7},{8,9},{9,10},{10,11},{11... | collective-permute-start | bytes 98312 | tf_op jit(solution)/shard_map/ppermute | solution.py:330
  206.5 2.8 %out_terms.3.lower_out = f32[192,256]{1,0:T(8,128)} custom-call(bf16[16,64,256]{2,1,0:T(8,128)(2,1)} %get-tuple-element.75.own, bf16[20,64,384]{2,1,0:T(8,128)(2,1)} %get-tuple-element.80.rebuilt), custom_call_target="tpu_custom_call" | custom-call | flops 226492416 | bytes 5242880 | tf_op jit(solution)/shard_map/out_terms/pallas_call | solution.py:705
  210.0 8.1 %unet_backward.1 = bf16[2048,128]{1,0:T(8,128)(2,1)} custom-call(s32[2]{0:T(128)} %pad_add_fusion.where_s, bf16[16,64,256]{2,1,0:T(8,128)(2,1)} %get-tuple-element.75.own, bf16[6,64,128]{2,1,0:T(8,128)(2,1)} %copy-done.5, bf16[6,64,128]{2,1,0:T(8,128)(2,1)} %copy-done.6, bf16[2,64,128]{2,1,0:T(8,128)(2,1)} %copy-done.2, bf16[2,64,128]{2,1,0:T(8,128)(2,1)} %copy-done.8, ...), custom_call_target="tpu_custom_call" | custom-call | flops 1981808640 | bytes 10485760 | tf_op jit(solution)/shard_map/unet_backward/pallas_call | solution.py:805
  218.1 22.9 %all_to_all.25 = bf16[128,16,128]{2,1,0:T(8,128)(2,1)S(1)} all-to-all(bf16[128,16,128]{2,1,0:T(8,128)(2,1)} %bitcast.8), channel_id=1, replica_groups=mesh['gx'=16,'gy'=8] {'gx','gy'}, dimensions={0} | all-to-all | bytes 1048576 | tf_op jit(solution)/shard_map/all_to_all | solution.py:854
  242.0 4.6 %all-to-all-start.4 = ((bf16[128,16,128]{2,1,0:T(8,128)(2,1)}), bf16[128,16,128]{2,1,0:T(8,128)(2,1)S(1)}, u32[]{:S(2)}, u32[]{:S(2)}) async-start(bf16[128,16,128]{2,1,0:T(8,128)(2,1)} %broadcast_in_dim.2), calls=%async_computation.4 | async-start | bytes 1048576 | tf_op jit(solution)/shard_map/all_to_all | solution.py:854
  246.6 6.8 %home_predictions.1 = bf16[64,8192]{1,0:T(8,128)(2,1)} custom-call(s32[64]{0:T(128)} %bitcast.14, s32[64]{0:T(128)} %fill_s.3, s32[64,128]{1,0:T(8,128)} %cell_ref.3, bf16[128,128,128]{2,1,0:T(8,128)(2,1)} %all-to-all-done.2.got_ref, bf16[64,8192]{1,0:T(8,128)(2,1)} %feat_ref.5, bf16[128,128]{1,0:T(8,128)(2,1)} %get-tuple-element.73.w_hidden, ...), custom_call_target="tpu_custom_call" | custom-call | flops 402653184 | bytes 8388608 | tf_op jit(solution)/shard_map/home_predictions/pallas_call | solution.py:231
  253.4 6.7 %all-to-all-done.4 = bf16[128,16,128]{2,1,0:T(8,128)(2,1)S(1)} async-done(((bf16[128,16,128]{2,1,0:T(8,128)(2,1)}), bf16[128,16,128]{2,1,0:T(8,128)(2,1)S(1)}, u32[]{:S(2)}, u32[]{:S(2)}) %all-to-all-start.4) | async-done | bytes 524320 | tf_op jit(solution)/shard_map/all_to_all | solution.py:854
  (50 shorter events, 24.3 us)
Async XLA Ops:
  5.5 66.0 %all-to-all-start = ((bf16[128,136,128]{2,1,0:T(8,128)(2,1)}), bf16[128,136,128]{2,1,0:T(8,128)(2,1)}, u32[]{:S(2)}, u32[]{:S(2)}) async-start(bf16[128,136,128]{2,1,0:T(8,128)(2,1)} %dispatch.1), calls=%async_computation | async-start | bytes 8912896 | tf_op jit(solution)/shard_map/all_to_all | solution.py:854
  71.4 72.3 %all-to-all-start.1 = ((bf16[128,128,128]{2,1,0:T(8,128)(2,1)}), bf16[128,128,128]{2,1,0:T(8,128)(2,1)}, u32[]{:S(2)}, u32[]{:S(2)}) async-start(bf16[128,128,128]{2,1,0:T(8,128)(2,1)} %dispatch_target.1), calls=%async_computation.1 | async-start | bytes 8388608 | tf_op jit(solution)/shard_map/all_to_all | solution.py:854
  86.8 34.0 %collective-permute-start.2 = (bf16[1,64,128]{2,1,0:T(8,128)(2,1)}, bf16[1,64,128]{2,1,0:T(8,128)(2,1)S(1)}, u32[]{:S(2)}, u32[]{:S(2)}) collective-permute-start(bf16[1,64,128]{2,1,0:T(8,128)(2,1)} %get-tuple-element.66), channel_id=1, source_target_pairs={{0,8},{8,16},{16,24},{24,32},{32,40},{40,48},{48,56},{56,64},{64,7... | collective-permute-start | bytes 49160 | tf_op jit(solution)/shard_map/ppermute | solution.py:330
  90.1 33.5 %collective-permute-start.3 = (bf16[1,64,128]{2,1,0:T(8,128)(2,1)}, bf16[1,64,128]{2,1,0:T(8,128)(2,1)S(1)}, u32[]{:S(2)}, u32[]{:S(2)}) collective-permute-start(bf16[1,64,128]{2,1,0:T(8,128)(2,1)} %get-tuple-element.67), channel_id=1, source_target_pairs={{8,0},{16,8},{24,16},{32,24},{40,32},{48,40},{56,48},{64,56},{72,6... | collective-permute-start | bytes 49160 | tf_op jit(solution)/shard_map/ppermute | solution.py:335
  91.4 38.9 %collective-permute-start = (bf16[10,64,128]{2,1,0:T(8,128)(2,1)}, bf16[10,64,128]{2,1,0:T(8,128)(2,1)S(1)}, u32[]{:S(2)}, u32[]{:S(2)}) collective-permute-start(bf16[10,64,128]{2,1,0:T(8,128)(2,1)} %get-tuple-element.64), channel_id=1, source_target_pairs={{0,1},{1,2},{2,3},{3,4},{4,5},{5,6},{6,7},{8,9},{9,10},{10,11},{11... | collective-permute-start | bytes 491528 | tf_op jit(solution)/shard_map/ppermute | solution.py:330
  95.1 35.2 %collective-permute-start.1 = (bf16[10,64,128]{2,1,0:T(8,128)(2,1)}, bf16[10,64,128]{2,1,0:T(8,128)(2,1)S(1)}, u32[]{:S(2)}, u32[]{:S(2)}) collective-permute-start(bf16[10,64,128]{2,1,0:T(8,128)(2,1)} %get-tuple-element.65), channel_id=1, source_target_pairs={{1,0},{2,1},{3,2},{4,3},{5,4},{6,5},{7,6},{9,8},{10,9},{11,10},{12... | collective-permute-start | bytes 491528 | tf_op jit(solution)/shard_map/ppermute | solution.py:335
  123.6 6.7 %copy-start.1 = (bf16[2,64,128]{2,1,0:T(8,128)(2,1)}, bf16[2,64,128]{2,1,0:T(8,128)(2,1)S(1)}, u32[]{:S(2)}) copy-start(bf16[2,64,128]{2,1,0:T(8,128)(2,1)S(1)} %constant_dynamic-update-slice_fusion.sides) | copy-start | bytes 98308
  123.6 5.7 %collective-permute-start.5 = (bf16[2,64,128]{2,1,0:T(8,128)(2,1)S(1)}, bf16[2,64,128]{2,1,0:T(8,128)(2,1)S(1)}, u32[]{:S(2)}, u32[]{:S(2)}) collective-permute-start(bf16[2,64,128]{2,1,0:T(8,128)(2,1)S(1)} %constant_dynamic-update-slice_fusion.sides), channel_id=1, source_target_pairs={{1,0},{2,1},{3,2},{4,3},{5,4},{6,5},{7,6},{9,8},{10,9},{11,10},{12... | collective-permute-start | bytes 98312 | tf_op jit(solution)/shard_map/ppermute | solution.py:335
  126.3 4.0 %collective-permute-start.4 = (bf16[2,64,128]{2,1,0:T(8,128)(2,1)S(1)}, bf16[2,64,128]{2,1,0:T(8,128)(2,1)S(1)}, u32[]{:S(2)}, u32[]{:S(2)}) collective-permute-start(bf16[2,64,128]{2,1,0:T(8,128)(2,1)S(1)} %constant_dynamic-update-slice_fusion.sides), channel_id=1, source_target_pairs={{0,1},{1,2},{2,3},{3,4},{4,5},{5,6},{6,7},{8,9},{9,10},{10,11},{11... | collective-permute-start | bytes 98312 | tf_op jit(solution)/shard_map/ppermute | solution.py:330
  129.3 1.0 copy-start.9
  130.3 0.7 copy-start.3
  130.3 0.7 copy-start.4
  143.8 74.3 %all-to-all-start.2 = ((bf16[128,128,128]{2,1,0:T(8,128)(2,1)}), bf16[128,128,128]{2,1,0:T(8,128)(2,1)}, u32[]{:S(2)}, u32[]{:S(2)}) async-start(bf16[128,128,128]{2,1,0:T(8,128)(2,1)} %share.1), calls=%async_computation.2 | async-start | bytes 8388608 | tf_op jit(solution)/shard_map/all_to_all | solution.py:854
  187.1 12.9 %collective-permute-start.8 = (bf16[1,64,128]{2,1,0:T(8,128)(2,1)}, bf16[1,64,128]{2,1,0:T(8,128)(2,1)S(1)}, u32[]{:S(2)}, u32[]{:S(2)}) collective-permute-start(bf16[1,64,128]{2,1,0:T(8,128)(2,1)} %get-tuple-element.78), channel_id=1, source_target_pairs={{0,8},{8,16},{16,24},{24,32},{32,40},{40,48},{48,56},{56,64},{64,7... | collective-permute-start | bytes 49160 | tf_op jit(solution)/shard_map/ppermute | solution.py:330
  190.4 10.4 %collective-permute-start.9 = (bf16[1,64,128]{2,1,0:T(8,128)(2,1)}, bf16[1,64,128]{2,1,0:T(8,128)(2,1)S(1)}, u32[]{:S(2)}, u32[]{:S(2)}) collective-permute-start(bf16[1,64,128]{2,1,0:T(8,128)(2,1)} %get-tuple-element.79), channel_id=1, source_target_pairs={{8,0},{16,8},{24,16},{32,24},{40,32},{48,40},{56,48},{64,56},{72,6... | collective-permute-start | bytes 49160 | tf_op jit(solution)/shard_map/ppermute | solution.py:335
  191.7 17.6 %collective-permute-start.6 = (bf16[6,64,128]{2,1,0:T(8,128)(2,1)}, bf16[6,64,128]{2,1,0:T(8,128)(2,1)S(1)}, u32[]{:S(2)}, u32[]{:S(2)}) collective-permute-start(bf16[6,64,128]{2,1,0:T(8,128)(2,1)} %get-tuple-element.76), channel_id=1, source_target_pairs={{0,1},{1,2},{2,3},{3,4},{4,5},{5,6},{6,7},{8,9},{9,10},{10,11},{11... | collective-permute-start | bytes 294920 | tf_op jit(solution)/shard_map/ppermute | solution.py:330
  195.3 14.0 %collective-permute-start.7 = (bf16[6,64,128]{2,1,0:T(8,128)(2,1)}, bf16[6,64,128]{2,1,0:T(8,128)(2,1)S(1)}, u32[]{:S(2)}, u32[]{:S(2)}) collective-permute-start(bf16[6,64,128]{2,1,0:T(8,128)(2,1)} %get-tuple-element.77), channel_id=1, source_target_pairs={{1,0},{2,1},{3,2},{4,3},{5,4},{6,5},{7,6},{9,8},{10,9},{11,10},{12... | collective-permute-start | bytes 294920 | tf_op jit(solution)/shard_map/ppermute | solution.py:335
  200.8 8.5 %copy-start.2 = (bf16[2,64,128]{2,1,0:T(8,128)(2,1)}, bf16[2,64,128]{2,1,0:T(8,128)(2,1)S(1)}, u32[]{:S(2)}) copy-start(bf16[2,64,128]{2,1,0:T(8,128)(2,1)S(1)} %constant_dynamic-update-slice_fusion.2.sides) | copy-start | bytes 98308
  200.8 8.5 %collective-permute-start.11 = (bf16[2,64,128]{2,1,0:T(8,128)(2,1)S(1)}, bf16[2,64,128]{2,1,0:T(8,128)(2,1)S(1)}, u32[]{:S(2)}, u32[]{:S(2)}) collective-permute-start(bf16[2,64,128]{2,1,0:T(8,128)(2,1)S(1)} %constant_dynamic-update-slice_fusion.2.sides), channel_id=1, source_target_pairs={{1,0},{2,1},{3,2},{4,3},{5,4},{6,5},{7,6},{9,8},{10,9},{11,10},{12... | collective-permute-start | bytes 98312 | tf_op jit(solution)/shard_map/ppermute | solution.py:335
  203.5 5.8 %collective-permute-start.10 = (bf16[2,64,128]{2,1,0:T(8,128)(2,1)S(1)}, bf16[2,64,128]{2,1,0:T(8,128)(2,1)S(1)}, u32[]{:S(2)}, u32[]{:S(2)}) collective-permute-start(bf16[2,64,128]{2,1,0:T(8,128)(2,1)S(1)} %constant_dynamic-update-slice_fusion.2.sides), channel_id=1, source_target_pairs={{0,1},{1,2},{2,3},{3,4},{4,5},{5,6},{6,7},{8,9},{9,10},{10,11},{11... | collective-permute-start | bytes 98312 | tf_op jit(solution)/shard_map/ppermute | solution.py:330
  209.3 0.6 copy-start.5
  209.3 0.7 copy-start.6
  242.0 18.1 %all-to-all-start.4 = ((bf16[128,16,128]{2,1,0:T(8,128)(2,1)}), bf16[128,16,128]{2,1,0:T(8,128)(2,1)S(1)}, u32[]{:S(2)}, u32[]{:S(2)}) async-start(bf16[128,16,128]{2,1,0:T(8,128)(2,1)} %broadcast_in_dim.2), calls=%async_computation.4 | async-start | bytes 1048576 | tf_op jit(solution)/shard_map/all_to_all | solution.py:854
  260.1 0.8 copy-start
  (3 other events, 1.8 us)

commit v4 on v3

--- a/solution.py
+++ b/solution.py
@@ -756,7 +756,8 @@
         mid_grad[g] = (pair_sum(total) * slope_mid[g] * mask).astype(BF)
         return carry
 
-    lax.fori_loop(0, 10, pooled, 0, unroll=10)
+    for at in range(10):
+        pooled(at, 0)
 
     def fine(g, carry):
         spread = 0.25 * conv_row(mid_grad, g, flip_mid[...], 2)[:, :CC]
@@ -765,7 +766,8 @@
             first_grad[2 * g + j] = (value * slope_in[2 * g + j]).astype(BF)
         return carry
 
-    lax.fori_loop(0, 8, fine, 0, unroll=8)
+    for at in range(8):
+        fine(at, 0)
 
     sum_in[...] = jnp.zeros_like(sum_in)
     sum_mid[...] = jnp.zeros_like(sum_mid)
@@ -777,7 +779,8 @@
         )
         return carry
 
-    lax.fori_loop(0, CR, fine_terms, 0, unroll=16)
+    for at in range(CR):
+        fine_terms(at, 0)
     even = (lane_index((CH, CC)) & 1) == 0
 
     def coarse_terms(g, carry):
@@ -787,7 +790,8 @@
         )
         return carry
 
-    lax.fori_loop(0, 8, coarse_terms, 0, unroll=8)
+    for at in range(8):
+        coarse_terms(at, 0)
 
     rows_each = 3 * CH
     for which, total in enumerate(((sum_in,), (sum_mid,), (upper_out, lower_out))):

time: 264 us -> 264 us (level)
  no operation moved by 1% of the time
where the time goes in v4:
time: 264 us; the launch traced here: 263 us
  Pallas kernels  89.5 us (34%)
  waiting for transfers between devices  81.4 us (31%)
  starting transfers between devices  64.4 us (24%)
  blocking collectives  22.9 us (9%)
  local copies, waits for them, and re-layouts  3.01 us (1%)
    all_to_all x4, waiting for transfers between devices, swap(): return lax.all_to_all(value, axes, split_axis=0, concat_axis=0, tiled=True)  53 us
    all_to_all x4, starting transfers between devices, swap(): return lax.all_to_all(value, axes, split_axis=0, concat_axis=0, tiled=True)  32.9 us
    pallas_call x1, Pallas kernels, particles(): pl.pallas_call(functools.partial(particle_kernel, steps - 1, scale), grid...  32.7 us
    ppermute x6, waiting for transfers between devices, ahead(): return lax.ppermute(value, axis, [(i, i + 1) for i in range(count - 1)])  24.9 us
    all_to_all x1, blocking collectives, swap(): return lax.all_to_all(value, axes, split_axis=0, concat_axis=0, tiled=True)  22.9 us
    ppermute x6, starting transfers between devices, ahead(): return lax.ppermute(value, axis, [(i, i + 1) for i in range(count - 1)])  19.8 us
    ppermute x6, starting transfers between devices, behind(): return lax.ppermute(value, axis, [(i + 1, i) for i in range(count - 1)])  11.8 us
    pallas_call x1, Pallas kernels, deposit(): pl.pallas_call(functools.partial(deposit_kernel, per, steps - 1), grid=(s...  9.64 us
  transfers between devices with their start and end apart: 16, of which 6 were waited for; matrix products, arithmetic and copies ran while one was open for 0% of the time, Pallas kernels for 31%

profile of v4, /device:TPU:1, one launch (start us, length us, event | category | flops | bytes accessed | tf_op | source)
XLA Modules:
  0.0 262.9 jit_solution(11886371150439138009)
XLA Ops:
  0.6 4.8 %dispatch.1 = bf16[128,136,128]{2,1,0:T(8,128)(2,1)} custom-call(s32[64]{0:T(128)} %bitcast.12, s32[64]{0:T(128)} %patch_s.1, s32[64]{0:T(128)} %fill_s.3, s32[64,128]{1,0:T(8,128)} %cell_ref.3, bf16[64,8192]{1,0:T(8,128)(2,1)} %feat_ref.5), custom_call_target="tpu_custom_call" | custom-call | bytes 6291456 | tf_op jit(solution)/shard_map/dispatch/pallas_call | solution.py:154
  5.5 11.9 %all-to-all-start = ((bf16[128,136,128]{2,1,0:T(8,128)(2,1)}), bf16[128,136,128]{2,1,0:T(8,128)(2,1)}, u32[]{:S(2)}, u32[]{:S(2)}) async-start(bf16[128,136,128]{2,1,0:T(8,128)(2,1)} %dispatch.1), calls=%async_computation | async-start | bytes 8912896 | tf_op jit(solution)/shard_map/all_to_all | solution.py:858
  17.4 4.9 %dispatch_target.1 = bf16[128,128,128]{2,1,0:T(8,128)(2,1)} custom-call(s32[64]{0:T(128)} %bitcast.13, bf16[64,8192]{1,0:T(8,128)(2,1)} %feat_ref.4), custom_call_target="tpu_custom_call" | custom-call | bytes 6291456 | tf_op jit(solution)/shard_map/dispatch_target/pallas_call | solution.py:189
  25.2 46.3 %all-to-all-done.got_ref = bf16[128,136,128]{2,1,0:T(8,128)(2,1)} async-done(((bf16[128,136,128]{2,1,0:T(8,128)(2,1)}), bf16[128,136,128]{2,1,0:T(8,128)(2,1)}, u32[]{:S(2)}, u32[]{:S(2)}) %all-to-all-start) | async-done | bytes 4456480 | tf_op jit(solution)/shard_map/all_to_all | solution.py:858
  71.4 5.7 %all-to-all-start.1 = ((bf16[128,128,128]{2,1,0:T(8,128)(2,1)}), bf16[128,128,128]{2,1,0:T(8,128)(2,1)}, u32[]{:S(2)}, u32[]{:S(2)}) async-start(bf16[128,128,128]{2,1,0:T(8,128)(2,1)} %dispatch_target.1), calls=%async_computation.1 | async-start | bytes 8388608 | tf_op jit(solution)/shard_map/all_to_all | solution.py:858
  77.2 9.6 %deposit.1 = (bf16[16,64,256]{2,1,0:T(8,128)(2,1)}, bf16[10,64,128]{2,1,0:T(8,128)(2,1)}, bf16[10,64,128]{2,1,0:T(8,128)(2,1)}, bf16[1,64,128]{2,1,0:T(8,128)(2,...) custom-call(bf16[128,136,128]{2,1,0:T(8,128)(2,1)} %all-to-all-done.got_ref), custom_call_target="tpu_custom_call" | custom-call | flops 671088640 | bytes 6291456 | tf_op jit(solution)/shard_map/deposit/pallas_call | solution.py:441
  86.8 3.3 %collective-permute-start.2 = (bf16[1,64,128]{2,1,0:T(8,128)(2,1)}, bf16[1,64,128]{2,1,0:T(8,128)(2,1)S(1)}, u32[]{:S(2)}, u32[]{:S(2)}) collective-permute-start(bf16[1,64,128]{2,1,0:T(8,128)(2,1)} %get-tuple-element.66), channel_id=1, source_target_pairs={{0,8},{8,16},{16,24},{24,32},{32,40},{40,48},{48,56},{56,64},{64,7... | collective-permute-start | bytes 49160 | tf_op jit(solution)/shard_map/ppermute | solution.py:330
  91.4 3.6 %collective-permute-start = (bf16[10,64,128]{2,1,0:T(8,128)(2,1)}, bf16[10,64,128]{2,1,0:T(8,128)(2,1)S(1)}, u32[]{:S(2)}, u32[]{:S(2)}) collective-permute-start(bf16[10,64,128]{2,1,0:T(8,128)(2,1)} %get-tuple-element.64), channel_id=1, source_target_pairs={{0,1},{1,2},{2,3},{3,4},{4,5},{5,6},{6,7},{8,9},{9,10},{10,11},{11... | collective-permute-start | bytes 491528 | tf_op jit(solution)/shard_map/ppermute | solution.py:330
  97.0 23.9 %collective-permute-done.2 = bf16[1,64,128]{2,1,0:T(8,128)(2,1)S(1)} collective-permute-done((bf16[1,64,128]{2,1,0:T(8,128)(2,1)}, bf16[1,64,128]{2,1,0:T(8,128)(2,1)S(1)}, u32[]{:S(2)}, u32[]{:S(2)}) %collective-permute-start.2) | collective-permute-done | bytes 16416 | tf_op jit(solution)/shard_map/ppermute | solution.py:330
  126.3 3.0 %collective-permute-start.4 = (bf16[2,64,128]{2,1,0:T(8,128)(2,1)S(1)}, bf16[2,64,128]{2,1,0:T(8,128)(2,1)S(1)}, u32[]{:S(2)}, u32[]{:S(2)}) collective-permute-start(bf16[2,64,128]{2,1,0:T(8,128)(2,1)S(1)} %constant_dynamic-update-slice_fusion.sides), channel_id=1, source_target_pairs={{0,1},{1,2},{2,3},{3,4},{4,5},{5,6},{6,7},{8,9},{9,10},{10,11},{11... | collective-permute-start | bytes 98312 | tf_op jit(solution)/shard_map/ppermute | solution.py:330
  131.0 9.4 %unet_forward.1 = (bf16[32,64,128]{2,1,0:T(8,128)(2,1)}, bf16[26,64,384]{2,1,0:T(8,128)(2,1)}, bf16[12,64,384]{2,1,0:T(8,128)(2,1)}, bf16[20,64,384]{2,1,0:T(8,1...) custom-call(s32[2]{0:T(128)} %pad_add_fusion.where_s, bf16[16,64,256]{2,1,0:T(8,128)(2,1)} %get-tuple-element.63.own, ...), custom_call_target="tpu_custom_call" | custom-call | flops 1415577600 | bytes 10485760 | tf_op jit(solution)/shard_map/unet_forward/pallas_call | solution.py:536
  140.4 3.3 %share.1 = bf16[128,128,128]{2,1,0:T(8,128)(2,1)} custom-call(s32[256]{0:T(256)} %get-tuple-element.62.patch_s, bf16[32,64,128]{2,1,0:T(8,128)(2,1)} %get-tuple-element.71.patches), custom_call_target="tpu_custom_call" | custom-call | bytes 6291456 | tf_op jit(solution)/shard_map/share/pallas_call | solution.py:563
  143.8 10.6 %all-to-all-start.2 = ((bf16[128,128,128]{2,1,0:T(8,128)(2,1)}), bf16[128,128,128]{2,1,0:T(8,128)(2,1)}, u32[]{:S(2)}, u32[]{:S(2)}) async-start(bf16[128,128,128]{2,1,0:T(8,128)(2,1)} %share.1), calls=%async_computation.2 | async-start | bytes 8388608 | tf_op jit(solution)/shard_map/all_to_all | solution.py:858
  154.4 32.7 %particles.1 = (bf16[16,64,256]{2,1,0:T(8,128)(2,1)}, bf16[6,64,128]{2,1,0:T(8,128)(2,1)}, bf16[6,64,128]{2,1,0:T(8,128)(2,1)}, bf16[1,64,128]{2,1,0:T(8,128)(2,...) custom-call(s32[256]{0:T(256)} %get-tuple-element.62.patch_s, bf16[128,136,128]{2,1,0:T(8,128)(2,1)} %all-to-all-done.got_ref, ...), custom_call_target="tpu_custom_call" | custom-call | flops 5872025600 | bytes 16777216 | tf_op jit(solution)/shard_map/particles/pallas_call | solution.py:663
  187.1 3.3 %collective-permute-start.8 = (bf16[1,64,128]{2,1,0:T(8,128)(2,1)}, bf16[1,64,128]{2,1,0:T(8,128)(2,1)S(1)}, u32[]{:S(2)}, u32[]{:S(2)}) collective-permute-start(bf16[1,64,128]{2,1,0:T(8,128)(2,1)} %get-tuple-element.78), channel_id=1, source_target_pairs={{0,8},{8,16},{16,24},{24,32},{32,40},{40,48},{48,56},{56,64},{64,7... | collective-permute-start | bytes 49160 | tf_op jit(solution)/shard_map/ppermute | solution.py:330
  191.7 3.6 %collective-permute-start.6 = (bf16[6,64,128]{2,1,0:T(8,128)(2,1)}, bf16[6,64,128]{2,1,0:T(8,128)(2,1)S(1)}, u32[]{:S(2)}, u32[]{:S(2)}) collective-permute-start(bf16[6,64,128]{2,1,0:T(8,128)(2,1)} %get-tuple-element.76), channel_id=1, source_target_pairs={{0,1},{1,2},{2,3},{3,4},{4,5},{5,6},{6,7},{8,9},{9,10},{10,11},{11... | collective-permute-start | bytes 294920 | tf_op jit(solution)/shard_map/ppermute | solution.py:330
  197.3 2.8 %out_terms.2.upper_out = f32[192,256]{1,0:T(8,128)} custom-call(bf16[16,64,256]{2,1,0:T(8,128)(2,1)} %get-tuple-element.75.own, bf16[20,64,384]{2,1,0:T(8,128)(2,1)} %get-tuple-element.80.rebuilt), custom_call_target="tpu_custom_call" | custom-call | flops 226492416 | bytes 5242880 | tf_op jit(solution)/shard_map/out_terms/pallas_call | solution.py:705
  203.5 3.0 %collective-permute-start.10 = (bf16[2,64,128]{2,1,0:T(8,128)(2,1)S(1)}, bf16[2,64,128]{2,1,0:T(8,128)(2,1)S(1)}, u32[]{:S(2)}, u32[]{:S(2)}) collective-permute-start(bf16[2,64,128]{2,1,0:T(8,128)(2,1)S(1)} %constant_dynamic-update-slice_fusion.2.sides), channel_id=1, source_target_pairs={{0,1},{1,2},{2,3},{3,4},{4,5},{5,6},{6,7},{8,9},{9,10},{10,11},{11... | collective-permute-start | bytes 98312 | tf_op jit(solution)/shard_map/ppermute | solution.py:330
  206.5 2.8 %out_terms.3.lower_out = f32[192,256]{1,0:T(8,128)} custom-call(bf16[16,64,256]{2,1,0:T(8,128)(2,1)} %get-tuple-element.75.own, bf16[20,64,384]{2,1,0:T(8,128)(2,1)} %get-tuple-element.80.rebuilt), custom_call_target="tpu_custom_call" | custom-call | flops 226492416 | bytes 5242880 | tf_op jit(solution)/shard_map/out_terms/pallas_call | solution.py:705
  210.0 8.1 %unet_backward.1 = bf16[2048,128]{1,0:T(8,128)(2,1)} custom-call(s32[2]{0:T(128)} %pad_add_fusion.where_s, bf16[16,64,256]{2,1,0:T(8,128)(2,1)} %get-tuple-element.75.own, bf16[6,64,128]{2,1,0:T(8,128)(2,1)} %copy-done.5, bf16[6,64,128]{2,1,0:T(8,128)(2,1)} %copy-done.6, bf16[2,64,128]{2,1,0:T(8,128)(2,1)} %copy-done.2, bf16[2,64,128]{2,1,0:T(8,128)(2,1)} %copy-done.8, ...), custom_call_target="tpu_custom_call" | custom-call | flops 1981808640 | bytes 10485760 | tf_op jit(solution)/shard_map/unet_backward/pallas_call | solution.py:809
  218.1 22.9 %all_to_all.25 = bf16[128,16,128]{2,1,0:T(8,128)(2,1)S(1)} all-to-all(bf16[128,16,128]{2,1,0:T(8,128)(2,1)} %bitcast.8), channel_id=1, replica_groups=mesh['gx'=16,'gy'=8] {'gx','gy'}, dimensions={0} | all-to-all | bytes 1048576 | tf_op jit(solution)/shard_map/all_to_all | solution.py:858
  242.0 4.6 %all-to-all-start.4 = ((bf16[128,16,128]{2,1,0:T(8,128)(2,1)}), bf16[128,16,128]{2,1,0:T(8,128)(2,1)S(1)}, u32[]{:S(2)}, u32[]{:S(2)}) async-start(bf16[128,16,128]{2,1,0:T(8,128)(2,1)} %broadcast_in_dim.2), calls=%async_computation.4 | async-start | bytes 1048576 | tf_op jit(solution)/shard_map/all_to_all | solution.py:858
  246.6 6.8 %home_predictions.1 = bf16[64,8192]{1,0:T(8,128)(2,1)} custom-call(s32[64]{0:T(128)} %bitcast.14, s32[64]{0:T(128)} %fill_s.3, s32[64,128]{1,0:T(8,128)} %cell_ref.3, bf16[128,128,128]{2,1,0:T(8,128)(2,1)} %all-to-all-done.2.got_ref, bf16[64,8192]{1,0:T(8,128)(2,1)} %feat_ref.5, bf16[128,128]{1,0:T(8,128)(2,1)} %get-tuple-element.73.w_hidden, ...), custom_call_target="tpu_custom_call" | custom-call | flops 402653184 | bytes 8388608 | tf_op jit(solution)/shard_map/home_predictions/pallas_call | solution.py:231
  253.4 6.7 %all-to-all-done.4 = bf16[128,16,128]{2,1,0:T(8,128)(2,1)S(1)} async-done(((bf16[128,16,128]{2,1,0:T(8,128)(2,1)}), bf16[128,16,128]{2,1,0:T(8,128)(2,1)S(1)}, u32[]{:S(2)}, u32[]{:S(2)}) %all-to-all-start.4) | async-done | bytes 524320 | tf_op jit(solution)/shard_map/all_to_all | solution.py:858
  (50 shorter events, 24.3 us)
Async XLA Ops:
  5.5 66.0 %all-to-all-start = ((bf16[128,136,128]{2,1,0:T(8,128)(2,1)}), bf16[128,136,128]{2,1,0:T(8,128)(2,1)}, u32[]{:S(2)}, u32[]{:S(2)}) async-start(bf16[128,136,128]{2,1,0:T(8,128)(2,1)} %dispatch.1), calls=%async_computation | async-start | bytes 8912896 | tf_op jit(solution)/shard_map/all_to_all | solution.py:858
  71.4 72.3 %all-to-all-start.1 = ((bf16[128,128,128]{2,1,0:T(8,128)(2,1)}), bf16[128,128,128]{2,1,0:T(8,128)(2,1)}, u32[]{:S(2)}, u32[]{:S(2)}) async-start(bf16[128,128,128]{2,1,0:T(8,128)(2,1)} %dispatch_target.1), calls=%async_computation.1 | async-start | bytes 8388608 | tf_op jit(solution)/shard_map/all_to_all | solution.py:858
  86.8 34.0 %collective-permute-start.2 = (bf16[1,64,128]{2,1,0:T(8,128)(2,1)}, bf16[1,64,128]{2,1,0:T(8,128)(2,1)S(1)}, u32[]{:S(2)}, u32[]{:S(2)}) collective-permute-start(bf16[1,64,128]{2,1,0:T(8,128)(2,1)} %get-tuple-element.66), channel_id=1, source_target_pairs={{0,8},{8,16},{16,24},{24,32},{32,40},{40,48},{48,56},{56,64},{64,7... | collective-permute-start | bytes 49160 | tf_op jit(solution)/shard_map/ppermute | solution.py:330
  90.1 33.5 %collective-permute-start.3 = (bf16[1,64,128]{2,1,0:T(8,128)(2,1)}, bf16[1,64,128]{2,1,0:T(8,128)(2,1)S(1)}, u32[]{:S(2)}, u32[]{:S(2)}) collective-permute-start(bf16[1,64,128]{2,1,0:T(8,128)(2,1)} %get-tuple-element.67), channel_id=1, source_target_pairs={{8,0},{16,8},{24,16},{32,24},{40,32},{48,40},{56,48},{64,56},{72,6... | collective-permute-start | bytes 49160 | tf_op jit(solution)/shard_map/ppermute | solution.py:335
  91.4 38.9 %collective-permute-start = (bf16[10,64,128]{2,1,0:T(8,128)(2,1)}, bf16[10,64,128]{2,1,0:T(8,128)(2,1)S(1)}, u32[]{:S(2)}, u32[]{:S(2)}) collective-permute-start(bf16[10,64,128]{2,1,0:T(8,128)(2,1)} %get-tuple-element.64), channel_id=1, source_target_pairs={{0,1},{1,2},{2,3},{3,4},{4,5},{5,6},{6,7},{8,9},{9,10},{10,11},{11... | collective-permute-start | bytes 491528 | tf_op jit(solution)/shard_map/ppermute | solution.py:330
  95.1 35.2 %collective-permute-start.1 = (bf16[10,64,128]{2,1,0:T(8,128)(2,1)}, bf16[10,64,128]{2,1,0:T(8,128)(2,1)S(1)}, u32[]{:S(2)}, u32[]{:S(2)}) collective-permute-start(bf16[10,64,128]{2,1,0:T(8,128)(2,1)} %get-tuple-element.65), channel_id=1, source_target_pairs={{1,0},{2,1},{3,2},{4,3},{5,4},{6,5},{7,6},{9,8},{10,9},{11,10},{12... | collective-permute-start | bytes 491528 | tf_op jit(solution)/shard_map/ppermute | solution.py:335
  123.6 6.7 %copy-start.1 = (bf16[2,64,128]{2,1,0:T(8,128)(2,1)}, bf16[2,64,128]{2,1,0:T(8,128)(2,1)S(1)}, u32[]{:S(2)}) copy-start(bf16[2,64,128]{2,1,0:T(8,128)(2,1)S(1)} %constant_dynamic-update-slice_fusion.sides) | copy-start | bytes 98308
  123.6 5.7 %collective-permute-start.5 = (bf16[2,64,128]{2,1,0:T(8,128)(2,1)S(1)}, bf16[2,64,128]{2,1,0:T(8,128)(2,1)S(1)}, u32[]{:S(2)}, u32[]{:S(2)}) collective-permute-start(bf16[2,64,128]{2,1,0:T(8,128)(2,1)S(1)} %constant_dynamic-update-slice_fusion.sides), channel_id=1, source_target_pairs={{1,0},{2,1},{3,2},{4,3},{5,4},{6,5},{7,6},{9,8},{10,9},{11,10},{12... | collective-permute-start | bytes 98312 | tf_op jit(solution)/shard_map/ppermute | solution.py:335
  126.3 4.0 %collective-permute-start.4 = (bf16[2,64,128]{2,1,0:T(8,128)(2,1)S(1)}, bf16[2,64,128]{2,1,0:T(8,128)(2,1)S(1)}, u32[]{:S(2)}, u32[]{:S(2)}) collective-permute-start(bf16[2,64,128]{2,1,0:T(8,128)(2,1)S(1)} %constant_dynamic-update-slice_fusion.sides), channel_id=1, source_target_pairs={{0,1},{1,2},{2,3},{3,4},{4,5},{5,6},{6,7},{8,9},{9,10},{10,11},{11... | collective-permute-start | bytes 98312 | tf_op jit(solution)/shard_map/ppermute | solution.py:330
  129.3 1.0 copy-start.9
  130.3 0.7 copy-start.3
  130.3 0.7 copy-start.4
  143.8 74.3 %all-to-all-start.2 = ((bf16[128,128,128]{2,1,0:T(8,128)(2,1)}), bf16[128,128,128]{2,1,0:T(8,128)(2,1)}, u32[]{:S(2)}, u32[]{:S(2)}) async-start(bf16[128,128,128]{2,1,0:T(8,128)(2,1)} %share.1), calls=%async_computation.2 | async-start | bytes 8388608 | tf_op jit(solution)/shard_map/all_to_all | solution.py:858
  187.1 12.9 %collective-permute-start.8 = (bf16[1,64,128]{2,1,0:T(8,128)(2,1)}, bf16[1,64,128]{2,1,0:T(8,128)(2,1)S(1)}, u32[]{:S(2)}, u32[]{:S(2)}) collective-permute-start(bf16[1,64,128]{2,1,0:T(8,128)(2,1)} %get-tuple-element.78), channel_id=1, source_target_pairs={{0,8},{8,16},{16,24},{24,32},{32,40},{40,48},{48,56},{56,64},{64,7... | collective-permute-start | bytes 49160 | tf_op jit(solution)/shard_map/ppermute | solution.py:330
  190.4 10.4 %collective-permute-start.9 = (bf16[1,64,128]{2,1,0:T(8,128)(2,1)}, bf16[1,64,128]{2,1,0:T(8,128)(2,1)S(1)}, u32[]{:S(2)}, u32[]{:S(2)}) collective-permute-start(bf16[1,64,128]{2,1,0:T(8,128)(2,1)} %get-tuple-element.79), channel_id=1, source_target_pairs={{8,0},{16,8},{24,16},{32,24},{40,32},{48,40},{56,48},{64,56},{72,6... | collective-permute-start | bytes 49160 | tf_op jit(solution)/shard_map/ppermute | solution.py:335
  191.7 17.6 %collective-permute-start.6 = (bf16[6,64,128]{2,1,0:T(8,128)(2,1)}, bf16[6,64,128]{2,1,0:T(8,128)(2,1)S(1)}, u32[]{:S(2)}, u32[]{:S(2)}) collective-permute-start(bf16[6,64,128]{2,1,0:T(8,128)(2,1)} %get-tuple-element.76), channel_id=1, source_target_pairs={{0,1},{1,2},{2,3},{3,4},{4,5},{5,6},{6,7},{8,9},{9,10},{10,11},{11... | collective-permute-start | bytes 294920 | tf_op jit(solution)/shard_map/ppermute | solution.py:330
  195.3 14.0 %collective-permute-start.7 = (bf16[6,64,128]{2,1,0:T(8,128)(2,1)}, bf16[6,64,128]{2,1,0:T(8,128)(2,1)S(1)}, u32[]{:S(2)}, u32[]{:S(2)}) collective-permute-start(bf16[6,64,128]{2,1,0:T(8,128)(2,1)} %get-tuple-element.77), channel_id=1, source_target_pairs={{1,0},{2,1},{3,2},{4,3},{5,4},{6,5},{7,6},{9,8},{10,9},{11,10},{12... | collective-permute-start | bytes 294920 | tf_op jit(solution)/shard_map/ppermute | solution.py:335
  200.8 8.5 %copy-start.2 = (bf16[2,64,128]{2,1,0:T(8,128)(2,1)}, bf16[2,64,128]{2,1,0:T(8,128)(2,1)S(1)}, u32[]{:S(2)}) copy-start(bf16[2,64,128]{2,1,0:T(8,128)(2,1)S(1)} %constant_dynamic-update-slice_fusion.2.sides) | copy-start | bytes 98308
  200.8 8.5 %collective-permute-start.11 = (bf16[2,64,128]{2,1,0:T(8,128)(2,1)S(1)}, bf16[2,64,128]{2,1,0:T(8,128)(2,1)S(1)}, u32[]{:S(2)}, u32[]{:S(2)}) collective-permute-start(bf16[2,64,128]{2,1,0:T(8,128)(2,1)S(1)} %constant_dynamic-update-slice_fusion.2.sides), channel_id=1, source_target_pairs={{1,0},{2,1},{3,2},{4,3},{5,4},{6,5},{7,6},{9,8},{10,9},{11,10},{12... | collective-permute-start | bytes 98312 | tf_op jit(solution)/shard_map/ppermute | solution.py:335
  203.5 5.8 %collective-permute-start.10 = (bf16[2,64,128]{2,1,0:T(8,128)(2,1)S(1)}, bf16[2,64,128]{2,1,0:T(8,128)(2,1)S(1)}, u32[]{:S(2)}, u32[]{:S(2)}) collective-permute-start(bf16[2,64,128]{2,1,0:T(8,128)(2,1)S(1)} %constant_dynamic-update-slice_fusion.2.sides), channel_id=1, source_target_pairs={{0,1},{1,2},{2,3},{3,4},{4,5},{5,6},{6,7},{8,9},{9,10},{10,11},{11... | collective-permute-start | bytes 98312 | tf_op jit(solution)/shard_map/ppermute | solution.py:330
  209.3 0.6 copy-start.5
  209.4 0.7 copy-start.6
  242.0 18.1 %all-to-all-start.4 = ((bf16[128,16,128]{2,1,0:T(8,128)(2,1)}), bf16[128,16,128]{2,1,0:T(8,128)(2,1)S(1)}, u32[]{:S(2)}, u32[]{:S(2)}) async-start(bf16[128,16,128]{2,1,0:T(8,128)(2,1)} %broadcast_in_dim.2), calls=%async_computation.4 | async-start | bytes 1048576 | tf_op jit(solution)/shard_map/all_to_all | solution.py:858
  260.1 0.8 copy-start
  (3 other events, 1.8 us)
